TPU v7x, 512 devices: a whole 4x4x16 slice. The times are simulated.
512 devices in a mesh: dom: 128 (over z_lo, x, y, core), rep: 4 (over z_hi).
Axes of the slice: x: 4, y: 4, z: 16 (z_hi: 4, z_lo: 4; z = z_hi * 4 + z_lo), core: 2. Of those that a mesh axis runs over, the one named last changes fastest.
Arguments:
- feat: bfloat16 [4, 8192, 128], P('rep', 'dom'), may hold values from -6 to 6
- species: int32 [4, 8192], P('rep', 'dom'), may hold values from 0 to 4
- species_gain: float32 [5, 128], replicated, may hold values from 0.5 to 2
- send_lists: int32 [4, 6, 3072], P('rep', None, 'dom'), may hold values from 0 to 63
- edge_src: int32 [4, 524288], P('rep', 'dom'), may hold values from 0 to 207
- edge_dst: int32 [4, 524288], P('rep', 'dom'), may hold values from 0 to 63
- edge_vec: float32 [4, 3, 524288], P('rep', None, 'dom'), may hold values from -3.4 to 3.4
- w_rad: float32 [8, 128], replicated, may hold values from -2 to 2
- w_mix: bfloat16 [384, 128], replicated, may hold values from -0.3125 to 0.3125
- out_cot: bfloat16 [4, 8192, 128], P('rep', 'dom'), may hold values from -6 to 6
Outputs:
- d_feat: float32 [4, 8192, 128], P('rep', 'dom')
- grad_mix: float32 [384, 128], replicated
- grad_rad: float32 [8, 128], replicated
Inputs may be any that keep to these rules, and one draw needn't show every extreme that they name: `send_lists`: own rows of the sending domain. `edge_src`: rows below 64 are owned atoms; then come six blocks of 24 rows, block g from the domain across face g. `edge_dst`: owned rows of the domain.
All inputs are finite; a program needn't handle non-finite values.
Results may differ from a plain program's by a relative error of at most 0.012.
The roundings to bfloat16 on the way count: a program that leaves them out, or rounds other values in their place, can miss the bound.
Values may be sent and summed in bfloat16 or wider, within the bound.
No kernel may reach another device: no remote copies, remote signals or barrier semaphores. Data moves between devices by JAX's collectives and lax.ppermute only.
A program may use at most 64 MiB of HBM per device.

v0:
```python
import jax
import jax.numpy as jnp
from jax import lax
from jax.sharding import PartitionSpec as P

msg_scale = 0.35
cutoff = 6.0
clip_norm = 256.0


def from_behind(block, axis, distance):
    devices = range(lax.axis_size(axis))
    route = [((i - distance) % len(devices), i) for i in devices]
    return lax.ppermute(block, axis, route)


def edge_geometry(vec, nbasis):
    radius = jnp.sqrt(vec[0] * vec[0] + vec[1] * vec[1] + vec[2] * vec[2] + 0.25)
    unit = vec / radius
    ux, uy, uz = (unit[0], unit[1], unit[2])
    root3 = jnp.sqrt(3.0)
    root5 = jnp.sqrt(5.0)
    root15 = jnp.sqrt(15.0)
    harm = jnp.stack(
        [
            jnp.ones_like(ux),
            root3 * ux,
            root3 * uy,
            root3 * uz,
            root15 * ux * uy,
            root15 * uy * uz,
            0.5 * root5 * (3.0 * uz * uz - 1.0),
            root15 * ux * uz,
            0.5 * root15 * (ux * ux - uy * uy),
        ]
    )
    scaled = radius / cutoff
    envelope = (1.0 - scaled * scaled) ** 2
    orders = (jnp.arange(nbasis, dtype=jnp.int32) + 1).astype(jnp.float32)[:, None]
    basis = (
        jnp.sin(orders * jnp.pi * radius[None, :] / cutoff) / radius[None, :] * envelope[None, :]
    )
    return (harm, basis)


def one_hot(index, count):
    return (index[:, None] == jnp.arange(count, dtype=jnp.int32)[None, :]).astype(jnp.float32)


def collect(hot, values):
    return lax.dot_general(hot, values, (((0,), (0,)), ((), ())), precision=lax.Precision.HIGHEST)


def spread(hot, values):
    return jnp.dot(hot, values, precision=lax.Precision.HIGHEST)


def edge_pass(source, dst_hot, vec, cot, w_rad, w_mix):
    chans = w_rad.shape[1]
    harm, basis = edge_geometry(vec, w_rad.shape[0])
    radial = lax.dot_general(
        basis, w_rad, (((0,), (0,)), ((), ())), precision=lax.Precision.HIGHEST
    )
    message = radial * source
    moments = [msg_scale * collect(dst_hot, harm[k][:, None] * message) for k in range(9)]
    group_zero = moments[0] * moments[0]
    group_one = moments[1] * moments[1] + moments[2] * moments[2] + moments[3] * moments[3]
    group_two = moments[4] * moments[4]
    for k in range(5, 9):
        group_two = group_two + moments[k] * moments[k]
    invariants = jnp.concatenate([group_zero, group_one, group_two], axis=1).astype(jnp.bfloat16)
    pre = jnp.dot(invariants, w_mix, preferred_element_type=jnp.float32)
    sigma = jax.nn.sigmoid(pre)
    slope = sigma * (1.0 + pre * (1.0 - sigma))
    dpre = (cot.astype(jnp.float32) * slope).astype(jnp.bfloat16)
    gmix = lax.dot_general(
        invariants, dpre, (((0,), (0,)), ((), ())), preferred_element_type=jnp.float32
    )
    dinv = lax.dot_general(
        dpre, w_mix, (((1,), (1,)), ((), ())), preferred_element_type=jnp.float32
    )
    groups = [0, 1, 1, 1, 2, 2, 2, 2, 2]
    dmessage = jnp.zeros_like(message)
    for k in range(9):
        start = groups[k] * chans
        dmoment = 2.0 * moments[k] * dinv[:, start : start + chans]
        dmessage = dmessage + harm[k][:, None] * spread(dst_hot, dmoment)
    dmessage = msg_scale * dmessage
    dradial = dmessage * source
    dsource = dmessage * radial
    grad_r = lax.dot_general(
        basis, dradial, (((1,), (0,)), ((), ())), precision=lax.Precision.HIGHEST
    )
    return (dsource, gmix, grad_r)


def face_offsets(domains):
    along_z = max(2, domains // 16)
    along_y = max(2, domains // along_z // 4)
    return [1, -1, along_z, -along_z, along_z * along_y, -along_z * along_y]


def on_device(
    feat, species, species_gain, send_lists, edge_src, edge_dst, edge_vec, w_rad, w_mix, out_cot
):
    atoms = feat.shape[1]
    ghosts = send_lists.shape[2]
    onehot = one_hot(species[0], species_gain.shape[0])
    gain = jnp.dot(onehot, species_gain, precision=lax.Precision.HIGHEST)
    own = (feat[0].astype(jnp.float32) * gain).astype(jnp.bfloat16)
    sends = send_lists[0]
    offsets = face_offsets(lax.axis_size("dom"))
    send_hots = [one_hot(sends[face], atoms) for face in range(6)]
    received = []
    for face in range(6):
        picked = jnp.dot(
            send_hots[face].astype(jnp.bfloat16), own, preferred_element_type=jnp.float32
        ).astype(jnp.bfloat16)
        received.append(from_behind(picked, "dom", offsets[face]))
    src = edge_src[0]
    width = atoms + 6 * ghosts
    src_hot = one_hot(src, width)
    extended = jnp.concatenate([own] + received, axis=0)
    source = jnp.dot(src_hot.astype(jnp.bfloat16), extended, preferred_element_type=jnp.float32)
    dst_hot = one_hot(edge_dst[0], atoms)
    dsource, gmix, grad_r = edge_pass(source, dst_hot, edge_vec[0], out_cot[0], w_rad, w_mix)
    dext = collect(src_hot, dsource)
    total = dext[:atoms]
    for face in range(6):
        start = atoms + face * ghosts
        returned = from_behind(dext[start : start + ghosts], "dom", -offsets[face])
        total = total + collect(send_hots[face], returned)
    d_feat = (total * gain)[None]
    gmix, grad_r = lax.psum((gmix, grad_r), ("dom", "rep"))
    norm = jnp.sqrt(jnp.sum(gmix * gmix) + jnp.sum(grad_r * grad_r))
    factor = clip_norm / jnp.maximum(norm, clip_norm)
    return (d_feat, factor * gmix, factor * grad_r)


def solution(mesh):
    in_specs = (
        P("rep", "dom", None),
        P("rep", "dom"),
        P(),
        P("rep", None, "dom"),
        P("rep", "dom"),
        P("rep", "dom"),
        P("rep", None, "dom"),
        P(),
        P(),
        P("rep", "dom", None),
    )
    out_specs = (P("rep", "dom", None), P(), P())
    return jax.shard_map(
        on_device, mesh=mesh, in_specs=in_specs, out_specs=out_specs, check_vma=False
    )
```

profile of v0, /device:TPU:1, one launch (start us, length us, event | category | flops | bytes accessed | tf_op | source)
XLA Modules:
  0.0 588.4 jit_solution(17073612376333913608)
XLA Ops:
  9.1 4.6 collective-permute-start
  13.9 6.1 %collective-permute-start.1 = (bf16[24,128]{1,0:T(8,128)(2,1)S(1)}, bf16[24,128]{1,0:T(8,128)(2,1)S(1)}, u32[]{:S(2)}, u32[]{:S(2)}) collective-permute-start(bf16[24,128]{1,0:T(8,128)(2,1)S(1)} %convolution_convert_fusion.4), channel_id=1, source_target_pairs={{4,0},{8,4},{12,8},{16,12},{20,16},{24,20},{28,24},{32,28},{36,32}... | collective-permute-start | bytes 18440 | tf_op jit(solution)/shard_map/ppermute | solution.py:14
  20.2 1.9 collective-permute-start.2
  22.3 7.3 %collective-permute-start.3 = (bf16[24,128]{1,0:T(8,128)(2,1)S(1)}, bf16[24,128]{1,0:T(8,128)(2,1)S(1)}, u32[]{:S(2)}, u32[]{:S(2)}) collective-permute-start(bf16[24,128]{1,0:T(8,128)(2,1)S(1)} %convolution_convert_fusion.2), channel_id=1, source_target_pairs={{32,0},{36,4},{40,8},{44,12},{48,16},{52,20},{56,24},{60,28},{64,3... | collective-permute-start | bytes 18440 | tf_op jit(solution)/shard_map/ppermute | solution.py:14
  29.8 1.9 collective-permute-start.4
  33.7 5.2 collective-permute-start.5
  39.6 2.5 fusion.10
  42.1 5.1 fusion.159
  47.3 2.6 multiply_convert_fusion
  49.8 3.0 fusion.16
  52.8 3.0 fusion.18
  55.8 3.3 fusion.20
  59.1 3.0 fusion.22
  62.1 3.0 fusion.26
  65.1 3.0 fusion.28
  68.1 3.1 add_convert_fusion.1
  71.2 3.0 add_convert_fusion
  76.7 1.3 fusion.8
  83.5 1.6 fusion.3
  86.4 1.4 fusion.1
  87.8 1.7 fusion.11
  89.5 4.0 fusion.9
  93.5 1.9 collective-permute-start.11
  95.5 5.4 collective-permute-start.10
  100.9 1.9 collective-permute-start.9
  102.8 7.3 %collective-permute-start.8 = (f32[24,128]{1,0:T(8,128)S(1)}, f32[24,128]{1,0:T(8,128)S(1)}, u32[]{:S(2)}, u32[]{:S(2)}) collective-permute-start(f32[24,128]{1,0:T(8,128)S(1)} %get-tuple-element.9), channel_id=1, source_target_pairs={{32,0},{36,4},{40,8},{44,12},{48,16},{52,20},{56,24},{60,28},{64,3... | collective-permute-start | bytes 36872 | tf_op jit(solution)/shard_map/ppermute | solution.py:14
  110.1 3.2 collective-permute-start.7
  113.3 115.5 %psum.15 = f32[8,128]{1,0:T(8,128)S(1)} all-reduce(f32[8,128]{1,0:T(8,128)S(1)} %fusion.11), channel_id=1, replica_groups=mesh['dom'=128,'rep'=4] {'dom','rep'}, use_global_device_ids=true, to_apply=%region_2.0 | all-reduce | flops 1024 | bytes 8192 | tf_op jit(solution)/shard_map/psum | solution.py:134
  229.5 2.9 collective-permute-start.6
  235.4 340.7 %all-reduce.2.cloned.1.call-done = f32[384,128]{1,0:T(8,128)} async-done(((f32[384,128]{1,0:T(8,128)}), f32[384,128]{1,0:T(8,128)}) %all-reduce.2.cloned.1.call-update) | async-done | bytes 196624 | tf_op jit(solution)/shard_map/psum | solution.py:134
  576.1 1.6 multiply_reduce_fusion
  579.6 1.6 broadcast_multiply_fusion
  (64 shorter events, 18.8 us)
Async XLA Ops:
  7.2 67.1 %copy-start = (bf16[384,128]{1,0:T(8,128)(2,1)S(1)}, bf16[384,128]{1,0:T(8,128)(2,1)}, u32[]{:S(2)}) copy-start(bf16[384,128]{1,0:T(8,128)(2,1)} %param.18) | copy-start | bytes 294916
  7.2 568.9 %all-reduce.2.cloned.1.call-start = ((), (), s32[]{:S(2)}) async-start(), calls=%async_computation | async-start | bytes 393216 | tf_op jit(solution)/shard_map/psum | solution.py:134
  9.1 24.6 %collective-permute-start = (bf16[24,128]{1,0:T(8,128)(2,1)S(1)}, bf16[24,128]{1,0:T(8,128)(2,1)S(1)}, u32[]{:S(2)}, u32[]{:S(2)}) collective-permute-start(bf16[24,128]{1,0:T(8,128)(2,1)S(1)} %convolution_convert_fusion.5), channel_id=1, source_target_pairs={{508,0},{0,4},{4,8},{8,12},{12,16},{16,20},{20,24},{24,28},{28,32}... | collective-permute-start | bytes 18440 | tf_op jit(solution)/shard_map/ppermute | solution.py:14
  13.9 25.0 %collective-permute-start.1 = (bf16[24,128]{1,0:T(8,128)(2,1)S(1)}, bf16[24,128]{1,0:T(8,128)(2,1)S(1)}, u32[]{:S(2)}, u32[]{:S(2)}) collective-permute-start(bf16[24,128]{1,0:T(8,128)(2,1)S(1)} %convolution_convert_fusion.4), channel_id=1, source_target_pairs={{4,0},{8,4},{12,8},{16,12},{20,16},{24,20},{28,24},{32,28},{36,32}... | collective-permute-start | bytes 18440 | tf_op jit(solution)/shard_map/ppermute | solution.py:14
  20.2 18.7 %collective-permute-start.2 = (bf16[24,128]{1,0:T(8,128)(2,1)S(1)}, bf16[24,128]{1,0:T(8,128)(2,1)S(1)}, u32[]{:S(2)}, u32[]{:S(2)}) collective-permute-start(bf16[24,128]{1,0:T(8,128)(2,1)S(1)} %convolution_convert_fusion.3), channel_id=1, source_target_pairs={{480,0},{484,4},{488,8},{492,12},{496,16},{500,20},{504,24},{508,2... | collective-permute-start | bytes 18440 | tf_op jit(solution)/shard_map/ppermute | solution.py:14
  22.1 20.0 %copy-start.5 = (f32[8,128]{1,0:T(8,128)S(1)}, f32[8,128]{1,0:T(8,128)}, u32[]{:S(2)}) copy-start(f32[8,128]{1,0:T(8,128)} %param.17) | copy-start | bytes 12292
  22.3 16.6 %collective-permute-start.3 = (bf16[24,128]{1,0:T(8,128)(2,1)S(1)}, bf16[24,128]{1,0:T(8,128)(2,1)S(1)}, u32[]{:S(2)}, u32[]{:S(2)}) collective-permute-start(bf16[24,128]{1,0:T(8,128)(2,1)S(1)} %convolution_convert_fusion.2), channel_id=1, source_target_pairs={{32,0},{36,4},{40,8},{44,12},{48,16},{52,20},{56,24},{60,28},{64,3... | collective-permute-start | bytes 18440 | tf_op jit(solution)/shard_map/ppermute | solution.py:14
  29.8 9.2 %collective-permute-start.4 = (bf16[24,128]{1,0:T(8,128)(2,1)S(1)}, bf16[24,128]{1,0:T(8,128)(2,1)S(1)}, u32[]{:S(2)}, u32[]{:S(2)}) collective-permute-start(bf16[24,128]{1,0:T(8,128)(2,1)S(1)} %convolution_convert_fusion.1), channel_id=1, source_target_pairs={{384,0},{388,4},{392,8},{396,12},{400,16},{404,20},{408,24},{412,2... | collective-permute-start | bytes 18440 | tf_op jit(solution)/shard_map/ppermute | solution.py:14
  33.7 5.9 %collective-permute-start.5 = (bf16[24,128]{1,0:T(8,128)(2,1)S(1)}, bf16[24,128]{1,0:T(8,128)(2,1)S(1)}, u32[]{:S(2)}, u32[]{:S(2)}) collective-permute-start(bf16[24,128]{1,0:T(8,128)(2,1)S(1)} %convolution_convert_fusion), channel_id=1, source_target_pairs={{128,0},{132,4},{136,8},{140,12},{144,16},{148,20},{152,24},{156,2... | collective-permute-start | bytes 18440 | tf_op jit(solution)/shard_map/ppermute | solution.py:14
  42.1 5.1 copy-start.2
  68.1 6.3 %copy-start.4 = (bf16[1,64,128]{2,1,0:T(8,128)(2,1)S(1)}, bf16[1,64,128]{2,1,0:T(8,128)(2,1)}, u32[]{:S(2)}) copy-start(bf16[1,64,128]{2,1,0:T(8,128)(2,1)} %param.19) | copy-start | bytes 49156
  87.8 1.7 copy-start.1
  87.8 1.7 copy-start.3
  93.5 135.9 %collective-permute-start.11 = (f32[24,128]{1,0:T(8,128)S(1)}, f32[24,128]{1,0:T(8,128)S(1)}, u32[]{:S(2)}, u32[]{:S(2)}) collective-permute-start(f32[24,128]{1,0:T(8,128)S(1)} %get-tuple-element.6), channel_id=1, source_target_pairs={{384,0},{388,4},{392,8},{396,12},{400,16},{404,20},{408,24},{412,2... | collective-permute-start | bytes 36872 | tf_op jit(solution)/shard_map/ppermute | solution.py:14
  95.5 137.2 %collective-permute-start.10 = (f32[24,128]{1,0:T(8,128)S(1)}, f32[24,128]{1,0:T(8,128)S(1)}, u32[]{:S(2)}, u32[]{:S(2)}) collective-permute-start(f32[24,128]{1,0:T(8,128)S(1)} %get-tuple-element.7), channel_id=1, source_target_pairs={{128,0},{132,4},{136,8},{140,12},{144,16},{148,20},{152,24},{156,2... | collective-permute-start | bytes 36872 | tf_op jit(solution)/shard_map/ppermute | solution.py:14
  100.9 132.1 %collective-permute-start.9 = (f32[24,128]{1,0:T(8,128)S(1)}, f32[24,128]{1,0:T(8,128)S(1)}, u32[]{:S(2)}, u32[]{:S(2)}) collective-permute-start(f32[24,128]{1,0:T(8,128)S(1)} %get-tuple-element.8), channel_id=1, source_target_pairs={{480,0},{484,4},{488,8},{492,12},{496,16},{500,20},{504,24},{508,2... | collective-permute-start | bytes 36872 | tf_op jit(solution)/shard_map/ppermute | solution.py:14
  102.8 130.4 %collective-permute-start.8 = (f32[24,128]{1,0:T(8,128)S(1)}, f32[24,128]{1,0:T(8,128)S(1)}, u32[]{:S(2)}, u32[]{:S(2)}) collective-permute-start(f32[24,128]{1,0:T(8,128)S(1)} %get-tuple-element.9), channel_id=1, source_target_pairs={{32,0},{36,4},{40,8},{44,12},{48,16},{52,20},{56,24},{60,28},{64,3... | collective-permute-start | bytes 36872 | tf_op jit(solution)/shard_map/ppermute | solution.py:14
  110.1 123.5 %collective-permute-start.7 = (f32[24,128]{1,0:T(8,128)S(1)}, f32[24,128]{1,0:T(8,128)S(1)}, u32[]{:S(2)}, u32[]{:S(2)}) collective-permute-start(f32[24,128]{1,0:T(8,128)S(1)} %get-tuple-element.10), channel_id=1, source_target_pairs={{508,0},{0,4},{4,8},{8,12},{12,16},{16,20},{20,24},{24,28},{28,32}... | collective-permute-start | bytes 36872 | tf_op jit(solution)/shard_map/ppermute | solution.py:14
  229.5 5.0 collective-permute-start.6
Sparse Core Ops, SparseCore 0:
  113.4 462.5 all-reduce.1
where the time goes:
time: 599 us; the launch traced here: 588 us
  waiting for transfers between devices  342 us (57%)
  blocking collectives  116 us (19%)
  matrix products  58.1 us (10%)
  starting transfers between devices  49.6 us (8%)
  between operations  16.2 us (3%)
  other arithmetic  6.18 us (1%)
    psum x1, waiting for transfers between devices, on_device(): gmix, grad_r = lax.psum((gmix, grad_r), ('dom', 'rep'))  341 us
    psum x1, blocking collectives, on_device(): gmix, grad_r = lax.psum((gmix, grad_r), ('dom', 'rep'))  116 us
    ppermute x12, starting transfers between devices, from_behind(): return lax.ppermute(block, axis, route)  49.5 us
    dot_general x16, matrix products, collect(): lax.dot_general(hot, values, (((0,), (0,)), ((), ())), precision=lax.Prec...  33.2 us
    dot_general x9, matrix products, spread(): return jnp.dot(hot, values, precision=lax.Precision.HIGHEST)  12.3 us
  transfers between devices with their start and end apart: 13, of which 3 were waited for; matrix products, arithmetic and copies ran while one was open for 1% of the time, Pallas kernels for 0%

commit v1 on v0

v1 whole, which is shorter than its diff:
```python
import jax
import jax.numpy as jnp
import numpy as np
from jax import lax
from jax.experimental import pallas as pl
from jax.experimental.pallas import tpu as pltpu
from jax.sharding import Mesh, PartitionSpec as P

msg_scale = 0.35
cutoff = 6.0
clip_norm = 256.0
f32, bf16 = jnp.float32, jnp.bfloat16

CHANS = 128
NB = 8
ATOMS = 64
FACES = 6
PAD = 32
GHOST = 24
ROWS = ATOMS + FACES * PAD
EDGES = 4096
CHUNK = 1024
GROUP = 32
SLOT = 16
SLAB = ("x", "y", "core")
LINE = ("zl", "rep")
DOM = ("zl", "x", "y", "core")
STEPS = (1, 8, 32)
HIGH = lax.Precision.HIGHEST
VMEM_LIMIT = 48 * 1024 * 1024


def dot(a, b, dims, precision=None):
    return lax.dot_general(
        a, b, (dims, ((), ())), precision=precision, preferred_element_type=f32
    )


def rows_iota(shape):
    return lax.broadcasted_iota(jnp.int32, shape, 0)


def call(kernel, outs, *args, scratch=(), cost=None):
    def spec(a):
        return pl.BlockSpec(memory_space=pltpu.VMEM)

    return pl.pallas_call(
        kernel,
        out_shape=outs,
        in_specs=[spec(a) for a in args],
        out_specs=[spec(o) for o in outs],
        scratch_shapes=list(scratch),
        cost_estimate=cost,
        compiler_params=pltpu.CompilerParams(vmem_limit_bytes=VMEM_LIMIT),
    )(*args)


def pre_kernel(feat_ref, species_ref, gain_ref, sends_ref, own_ref, gain_out, pick_ref):
    hot = (rows_iota((8, ATOMS)) == species_ref[...]).astype(f32)
    gains = jnp.concatenate([gain_ref[...], jnp.zeros((3, CHANS), f32)], axis=0)
    gain = dot(hot, gains, ((0,), (0,)), HIGH)
    own = (feat_ref[0].astype(f32) * gain).astype(bf16)
    own_ref[...] = own
    gain_out[...] = gain
    dom = domain()
    for face in range(FACES):
        hot = (rows_iota((ATOMS, GHOST)) == sends_ref[0, face : face + 1, :]).astype(f32)
        hot = jnp.concatenate([hot, jnp.zeros((ATOMS, PAD - GHOST), f32)], axis=1)
        picked = dot(hot.astype(bf16), own, ((0,), (0,)))
        bit = lax.rem(dom // STEPS[face // 2], 2)
        pick_ref[2 * (face // 2) + lax.rem(bit + face % 2, 2)] = picked.astype(bf16)


def domain():
    z, x, y, c = (lax.axis_index(a) for a in DOM)
    return ((z * 4 + x) * 4 + y) * 2 + c


def geo_kernel(vec_ref, harm_ref, basis_ref):
    vx, vy, vz = (vec_ref[0, i : i + 1, :] for i in range(3))
    square = vx * vx + vy * vy + vz * vz + 0.25
    inv_r = lax.rsqrt(square)
    radius = square * inv_r
    ux, uy, uz = vx * inv_r, vy * inv_r, vz * inv_r
    r3, r5, r15 = 3.0**0.5, 5.0**0.5, 15.0**0.5
    harms = [
        jnp.ones_like(ux),
        r3 * ux,
        r3 * uy,
        r3 * uz,
        r15 * ux * uy,
        r15 * uy * uz,
        0.5 * r5 * (3.0 * uz * uz - 1.0),
        r15 * ux * uz,
        0.5 * r15 * (ux * ux - uy * uy),
    ]
    for k, h in enumerate(harms):
        harm_ref[k : k + 1, :] = h
    scaled = radius * (1.0 / cutoff)
    envelope = 1.0 - scaled * scaled
    envelope = envelope * envelope * inv_r
    t = scaled * np.float32(np.pi) - np.float32(np.pi / 2)
    t2 = t * t
    sin_t = series(t2, 1) * t
    cos_t = series(t2, 0)
    twice = -2.0 * sin_t
    before, now = jnp.zeros_like(t), cos_t * envelope
    for b in range(NB):
        basis_ref[b : b + 1, :] = now
        before, now = now, twice * now - before


def series(square, odd):
    terms = [(-1.0) ** n / float(np.prod(np.arange(1, 2 * n + odd + 1.0))) for n in range(9)]
    total = jnp.full_like(square, terms[-1])
    for term in terms[-2::-1]:
        total = total * square + term
    return total


def split(values):
    top = values.astype(bf16).astype(f32)
    return top, values - top


def main_kernel(
    own_ref, r0, r1, r2, r3, r4, r5, src_ref, dst_ref, harm_ref, basis_ref, wrad_ref, wmix_ref, cot_ref,
    dext_ref, back_ref, grad_ref,
    hot_s, harm_s, radial_s, source_s, mom_s, dmom_s,
):
    dom = domain()
    got = (r0, r1, r2, r3, r4, r5)
    blocks = [own_ref[...].astype(f32)]
    bits = [lax.rem(dom // step, 2) for step in STEPS]
    for face in range(FACES):
        pair = face // 2
        a, b = got[2 * pair][...].astype(f32), got[2 * pair + 1][...].astype(f32)
        swapped = lax.rem(bits[pair] + face % 2, 2) == 0
        blocks.append(jnp.where(swapped, b, a))
    ext = jnp.concatenate(blocks, axis=0).T.astype(bf16)
    w_top, w_low = split(wrad_ref[...])
    wrad = jnp.concatenate([w_top, w_low, w_top], axis=0).T.astype(bf16)
    mom_s[...] = jnp.zeros_like(mom_s)
    for start in range(0, EDGES, CHUNK):
        at = pl.ds(start, CHUNK)
        src = src_ref[:, at]
        shift = jnp.zeros_like(src)
        for face in range(1, FACES):
            shift = shift + jnp.where(src >= ATOMS + face * GHOST, PAD - GHOST, 0)
        hot = jnp.where(rows_iota((ROWS, CHUNK)) == src + shift, 1.0, 0.0).astype(bf16)
        hot_s[:, at] = hot
        source = dot(ext, hot, ((1,), (0,)))
        source_s[:, at] = source.astype(bf16)
        b_top, b_low = split(basis_ref[:, at])
        basis = jnp.concatenate([b_top, b_top, b_low], axis=0).astype(bf16)
        radial = dot(wrad, basis, ((1,), (0,)))
        radial_s[:, at] = radial
        message = (radial * source).astype(bf16)
        own_hot = rows_iota((ATOMS, CHUNK)) == dst_ref[:, at]
        harm_s[0:ATOMS, at] = jnp.where(own_hot, 1.0, 0.0).astype(bf16)
        for k in range(1, 9):
            harm = harm_ref[k : k + 1, at]
            harm_s[k * ATOMS : (k + 1) * ATOMS, at] = jnp.where(own_hot, harm, 0.0).astype(bf16)
        mom_s[...] += dot(harm_s[:, at], message, ((1,), (1,)))
    moments = [msg_scale * mom_s[k * ATOMS : (k + 1) * ATOMS, :] for k in range(9)]
    squares = [m * m for m in moments]
    two = squares[4]
    for k in range(5, 9):
        two = two + squares[k]
    inv = jnp.concatenate([squares[0], squares[1] + squares[2] + squares[3], two], axis=1).astype(bf16)
    pre = dot(inv, wmix_ref[...], ((1,), (0,)))
    sigma = jax.nn.sigmoid(pre)
    slope = sigma * (1.0 + pre * (1.0 - sigma))
    dpre = (cot_ref[0].astype(f32) * slope).astype(bf16)
    grad_ref[0 : 3 * CHANS, :] = dot(inv, dpre, ((0,), (0,))).astype(bf16)
    dinv = dot(dpre, wmix_ref[...], ((1,), (1,)))
    groups = [0, 1, 1, 1, 2, 2, 2, 2, 2]
    for k in range(9):
        part = dinv[:, groups[k] * CHANS : (groups[k] + 1) * CHANS]
        mom_s[k * ATOMS : (k + 1) * ATOMS, :] = (2.0 * msg_scale) * moments[k] * part
    dmom_s[...] = mom_s[...].T.astype(bf16)
    dext = jnp.zeros((ROWS, CHANS), f32)
    gradr = jnp.zeros((2 * NB, CHANS), f32)
    for start in range(0, EDGES, CHUNK):
        at = pl.ds(start, CHUNK)
        dmsg = dot(dmom_s[...], harm_s[:, at], ((1,), (0,)))
        dradial = dmsg * source_s[:, at].astype(f32)
        dsource = (dmsg * radial_s[:, at]).astype(bf16)
        dext = dext + dot(hot_s[:, at], dsource, ((1,), (1,)))
        b_top, b_low = split(basis_ref[:, at])
        basis = jnp.concatenate([b_top, b_low], axis=0).astype(bf16)
        gradr = gradr + dot(basis, dradial.astype(bf16), ((1,), (1,)))
    gradr = jnp.concatenate([gradr[:NB] + gradr[NB:], jnp.zeros((NB, CHANS), f32)], axis=0)
    grad_ref[3 * CHANS : 3 * CHANS + 2 * NB, :] = gradr.astype(bf16)
    rest = GROUP * SLOT - 3 * CHANS - 2 * NB
    grad_ref[3 * CHANS + 2 * NB :, :] = jnp.zeros((rest, CHANS), bf16)
    dext_ref[...] = dext[:ATOMS]
    for face in range(FACES):
        pair = face // 2
        start = ATOMS + face * PAD
        slot = 2 * pair + lax.rem(bits[pair] + face % 2 + 1, 2)
        back_ref[slot] = dext[start : start + PAD].astype(bf16)


def post_kernel(dext_ref, gain_ref, sends_ref, r0, r1, r2, r3, r4, r5, sums_ref, dfeat_ref, gmix_ref, grad_ref):
    dom = domain()
    got = (r0, r1, r2, r3, r4, r5)
    total = dext_ref[...]
    for face in range(FACES):
        pair = face // 2
        bit = lax.rem(dom // STEPS[pair], 2)
        a, b = got[2 * pair][...].astype(f32), got[2 * pair + 1][...].astype(f32)
        values = jnp.where(lax.rem(bit + face % 2, 2) == 0, a, b)[:GHOST].astype(bf16)
        hot = (rows_iota((ATOMS, GHOST)) == sends_ref[0, face : face + 1, :]).astype(f32)
        total = total + dot(hot.astype(bf16), values, ((1,), (0,)))
    dfeat_ref[0] = total * gain_ref[...]
    sums = sums_ref[0 : 3 * CHANS + 2 * NB, :].astype(f32)
    gmix, grad = sums[: 3 * CHANS], sums[3 * CHANS : 3 * CHANS + NB]
    norm = jnp.sqrt(jnp.sum(gmix * gmix, keepdims=True) + jnp.sum(grad * grad, keepdims=True))
    factor = clip_norm / jnp.maximum(norm, clip_norm)
    gmix_ref[...] = factor * gmix
    grad_ref[...] = factor * grad


def swap(block, step, parity):
    pairs = []
    for i in range(128):
        if (i // step) % 2 == parity:
            j = (i + step) % 128
            pairs += [(i, j), (j, i)]
    return lax.ppermute(block, DOM, pairs)


def reduce_all(grads):
    parts = lax.all_to_all(grads, SLAB, 0, 0, tiled=True)
    mine = parts.reshape(GROUP, SLOT, CHANS).astype(f32).sum(0).astype(bf16)
    parts = lax.all_to_all(jnp.tile(mine, (16, 1)), LINE, 0, 0, tiled=True)
    mine = parts.reshape(16, SLOT, CHANS).astype(f32).sum(0).astype(bf16)
    return lax.all_to_all(jnp.tile(mine, (GROUP, 1)), SLAB, 0, 0, tiled=True)


def on_device(feat, species, species_gain, send_lists, edge_src, edge_dst, edge_vec, w_rad, w_mix, out_cot):
    shape = jax.ShapeDtypeStruct
    own, gain, picks = call(
        pre_kernel,
        [shape((ATOMS, CHANS), bf16), shape((ATOMS, CHANS), f32), shape((FACES, PAD, CHANS), bf16)],
        feat, species, species_gain, send_lists,
    )
    got = [swap(picks[2 * p + q], STEPS[p], q) for p in range(3) for q in range(2)]
    harm, basis = call(
        geo_kernel,
        [shape((16, EDGES), f32), shape((NB, EDGES), f32)],
        edge_vec,
        cost=pl.CostEstimate(flops=1000000, bytes_accessed=400000, transcendentals=0),
    )
    dext, back, grads = call(
        main_kernel,
        [shape((ATOMS, CHANS), f32), shape((FACES, PAD, CHANS), bf16), shape((GROUP * SLOT, CHANS), bf16)],
        own, *got, edge_src, edge_dst, harm, basis, w_rad, w_mix, out_cot,
        scratch=[
            pltpu.VMEM((ROWS, EDGES), bf16),
            pltpu.VMEM((9 * ATOMS, EDGES), bf16),
            pltpu.VMEM((CHANS, EDGES), f32),
            pltpu.VMEM((CHANS, EDGES), bf16),
            pltpu.VMEM((9 * ATOMS, CHANS), f32),
            pltpu.VMEM((CHANS, 9 * ATOMS), bf16),
        ],
    )
    returned = [swap(back[2 * p + q], STEPS[p], q) for p in range(3) for q in range(2)]
    sums = reduce_all(grads)
    d_feat, gmix, grad_r = call(
        post_kernel,
        [shape((1, ATOMS, CHANS), f32), shape((3 * CHANS, CHANS), f32), shape((NB, CHANS), f32)],
        dext, gain, send_lists, *returned, sums,
    )
    return d_feat, gmix, grad_r


def solution(mesh):
    fine = Mesh(mesh.devices.reshape(4, 4, 4, 2, 4), DOM + ("rep",))
    in_specs = (
        P("rep", DOM, None),
        P("rep", DOM),
        P(),
        P("rep", None, DOM),
        P("rep", DOM),
        P("rep", DOM),
        P("rep", None, DOM),
        P(),
        P(),
        P("rep", DOM, None),
    )
    out_specs = (P("rep", DOM, None), P(), P())
    return jax.shard_map(
        on_device, mesh=fine, in_specs=in_specs, out_specs=out_specs, check_vma=False
    )
```

time: 599 us -> 102 us (0.17); the launches traced: 588 us -> 101 us
  waiting for transfers between devices: 342 us -> 1.37 us
  blocking collectives: 116 us -> 37.5 us
  matrix products: 58.1 us -> 0 us
  between operations: 16.2 us -> 0.95 us
  Pallas kernels: 0 us -> 7.37 us
  other arithmetic: 6.18 us -> 0.06 us
    psum x1 -> x0, waiting for transfers between devices: 341 us -> none  [on_device(): gmix, grad_r = lax.psum((gmix, grad_r), ('dom', 'rep'))]
    psum x1 -> x0, blocking collectives: 116 us -> none  [on_device(): gmix, grad_r = lax.psum((gmix, grad_r), ('dom', 'rep'))]
    dot_general x38 -> x0, matrix products: 58.1 us -> none  [the longest x16 33.2 us: collect(): lax.dot_general(hot, values, (((0,), (0,)), ((), ())), precision=lax.Prec...]
    all_to_all x0 -> x2, blocking collectives: none -> 37.5 us  [the longest x1 25 us: reduce_all(): parts = lax.all_to_all(jnp.tile(mine, (16, 1)), LINE, 0, 0, tiled=True)]
    pallas_call x0 -> x4, Pallas kernels: none -> 7.37 us  [call(): pl.pallas_call(kernel, out_shape=outs, in_specs=[spec(a) for a in args],...]
  transfers between devices with their start and end apart: 13 -> 13, of which waited for: 3 -> 2; matrix products, arithmetic and copies ran while one was open for 1% -> 0% of each run, Pallas kernels for 0% -> 0%
where the time goes in v1:
time: 102 us; the launch traced here: 101 us
  starting transfers between devices  51.6 us (51%)
  blocking collectives  37.5 us (37%)
  Pallas kernels  7.37 us (7%)
  local copies, waits for them, and re-layouts  2.24 us (2%)
  waiting for transfers between devices  1.37 us (1%)
    ppermute x12, starting transfers between devices, swap(): return lax.ppermute(block, DOM, pairs)  46.1 us
    all_to_all x1, blocking collectives, reduce_all(): parts = lax.all_to_all(jnp.tile(mine, (16, 1)), LINE, 0, 0, tiled=True)  25 us
    all_to_all x1, blocking collectives, reduce_all(): parts = lax.all_to_all(grads, SLAB, 0, 0, tiled=True)  12.5 us
    pallas_call x4, Pallas kernels, call(): pl.pallas_call(kernel, out_shape=outs, in_specs=[spec(a) for a in args],...  7.37 us
    all_to_all x1, starting transfers between devices, reduce_all(): return lax.all_to_all(jnp.tile(mine, (GROUP, 1)), SLAB, 0, 0, tiled=True)  5.5 us
  transfers between devices with their start and end apart: 13, of which 2 were waited for; matrix products, arithmetic and copies ran while one was open for 0% of the time, Pallas kernels for 0%

profile of v1, /device:TPU:1, one launch (start us, length us, event | category | flops | bytes accessed | tf_op | source)
XLA Modules:
  0.0 101.1 jit_solution(17619006672129355709)
XLA Ops:
  0.7 0.7 copy.16.sends_ref
  1.4 0.7 copy-done.4
  2.1 0.4 shard_map.121
  2.5 0.0 copy-start.8
  2.5 0.0 copy-start
  2.5 7.2 %collective-permute-start.5 = (bf16[32,128]{1,0:T(8,128)(2,1)S(1)}, bf16[32,128]{1,0:T(8,128)(2,1)S(1)}, u32[]{:S(2)}, u32[]{:S(2)}) collective-permute-start(bf16[32,128]{1,0:T(8,128)(2,1)S(1)} %get-tuple-element.25), channel_id=1, source_target_pairs={{128,256},{256,128},{132,260},{260,132},{136,264},{264,136},{140,2... | collective-permute-start | bytes 24584 | tf_op jit(solution)/shard_map/ppermute | solution.py:231
  9.7 1.9 %collective-permute-start.4 = (bf16[32,128]{1,0:T(8,128)(2,1)S(1)}, bf16[32,128]{1,0:T(8,128)(2,1)S(1)}, u32[]{:S(2)}, u32[]{:S(2)}) collective-permute-start(bf16[32,128]{1,0:T(8,128)(2,1)S(1)} %get-tuple-element.26), channel_id=1, source_target_pairs={{0,128},{128,0},{4,132},{132,4},{8,136},{136,8},{12,140},{140,12},... | collective-permute-start | bytes 24584 | tf_op jit(solution)/shard_map/ppermute | solution.py:231
  11.7 4.1 %collective-permute-start.3 = (bf16[32,128]{1,0:T(8,128)(2,1)S(1)}, bf16[32,128]{1,0:T(8,128)(2,1)S(1)}, u32[]{:S(2)}, u32[]{:S(2)}) collective-permute-start(bf16[32,128]{1,0:T(8,128)(2,1)S(1)} %get-tuple-element.27), channel_id=1, source_target_pairs={{32,64},{64,32},{36,68},{68,36},{40,72},{72,40},{44,76},{76,44},{4... | collective-permute-start | bytes 24584 | tf_op jit(solution)/shard_map/ppermute | solution.py:231
  15.8 2.1 %collective-permute-start.2 = (bf16[32,128]{1,0:T(8,128)(2,1)S(1)}, bf16[32,128]{1,0:T(8,128)(2,1)S(1)}, u32[]{:S(2)}, u32[]{:S(2)}) collective-permute-start(bf16[32,128]{1,0:T(8,128)(2,1)S(1)} %get-tuple-element.28), channel_id=1, source_target_pairs={{0,32},{32,0},{4,36},{36,4},{8,40},{40,8},{12,44},{44,12},{16,48},... | collective-permute-start | bytes 24584 | tf_op jit(solution)/shard_map/ppermute | solution.py:231
  17.9 4.6 %collective-permute-start.1 = (bf16[32,128]{1,0:T(8,128)(2,1)S(1)}, bf16[32,128]{1,0:T(8,128)(2,1)S(1)}, u32[]{:S(2)}, u32[]{:S(2)}) collective-permute-start(bf16[32,128]{1,0:T(8,128)(2,1)S(1)} %get-tuple-element.29), channel_id=1, source_target_pairs={{4,8},{8,4},{12,16},{16,12},{20,24},{24,20},{28,32},{32,28},{36,40... | collective-permute-start | bytes 24584 | tf_op jit(solution)/shard_map/ppermute | solution.py:231
  22.5 0.0 collective-permute-done.5.r5
  22.5 5.0 %collective-permute-start = (bf16[32,128]{1,0:T(8,128)(2,1)S(1)}, bf16[32,128]{1,0:T(8,128)(2,1)S(1)}, u32[]{:S(2)}, u32[]{:S(2)}) collective-permute-start(bf16[32,128]{1,0:T(8,128)(2,1)S(1)} %get-tuple-element.30), channel_id=1, source_target_pairs={{0,4},{4,0},{8,12},{12,8},{16,20},{20,16},{24,28},{28,24},{32,36},... | collective-permute-start | bytes 24584 | tf_op jit(solution)/shard_map/ppermute | solution.py:231
  27.6 0.0 copy-start.1
  27.6 0.0 copy-start.2
  27.6 0.0 copy-start.3
  27.7 0.1 shard_map.122
  27.7 0.0 copy-start.5
  27.8 0.6 collective-permute-done.r0
  28.4 0.0 copy-done.5
  28.4 6.0 %shard_map.123 = (f32[64,128]{1,0:T(8,128)S(1)}, bf16[6,32,128]{2,1,0:T(8,128)(2,1)S(1)}, bf16[512,128]{1,0:T(8,128)(2,1)S(1)}) custom-call(bf16[64,128]{1,0:T(8,128)(2,1)S(1)} %get-tuple-element.11.own_ref, bf16[32,128]{1,0:T(8,128)(2,1)S(1)} %collective-permute-done.r0, bf16[32,128]{1,0:T(8,128)(2,1)S(1)} %collective-permute-done.1.r1, ...), custom_call_target="tpu_custom_call" | custom-call | tf_op jit(solution)/shard_map/pallas_call | solution.py:47
  34.4 12.5 %all_to_all.23 = bf16[32,16,128]{2,1,0:T(8,128)(2,1)S(1)} all-to-all(bf16[32,16,128]{2,1,0:T(8,128)(2,1)S(1)} %bitcast.27), channel_id=1, replica_groups=mesh['zl'=4,'x'=4,'y'=4,'core'=2,'rep'=4] {'x','y','core'}, dimensions={0} | all-to-all | bytes 262144 | tf_op jit(solution)/shard_map/all_to_all | solution.py:235
  47.0 25.0 %all_to_all.24 = bf16[16,16,128]{2,1,0:T(8,128)(2,1)S(1)} all-to-all(bf16[16,16,128]{2,1,0:T(8,128)(2,1)S(1)} %tile.4), channel_id=1, replica_groups=mesh['zl'=4,'x'=4,'y'=4,'core'=2,'rep'=4] {'zl','rep'}, dimensions={0} | all-to-all | bytes 131072 | tf_op jit(solution)/shard_map/all_to_all | solution.py:237
  72.0 0.7 tile.5
  72.7 5.5 %all-to-all-start.2 = ((bf16[32,16,128]{2,1,0:T(8,128)(2,1)}), bf16[32,16,128]{2,1,0:T(8,128)(2,1)S(1)}, u32[]{:S(2)}, u32[]{:S(2)}) async-start(bf16[32,16,128]{2,1,0:T(8,128)(2,1)} %tile.5), calls=%async_computation.2 | async-start | bytes 262144 | tf_op jit(solution)/shard_map/all_to_all | solution.py:239
  78.2 3.1 %collective-permute-start.11 = (bf16[32,128]{1,0:T(8,128)(2,1)S(1)}, bf16[32,128]{1,0:T(8,128)(2,1)S(1)}, u32[]{:S(2)}, u32[]{:S(2)}) collective-permute-start(bf16[32,128]{1,0:T(8,128)(2,1)S(1)} %get-tuple-element.19), channel_id=1, source_target_pairs={{128,256},{256,128},{132,260},{260,132},{136,264},{264,136},{140,2... | collective-permute-start | bytes 24584 | tf_op jit(solution)/shard_map/ppermute | solution.py:231
  81.3 2.2 %collective-permute-start.10 = (bf16[32,128]{1,0:T(8,128)(2,1)S(1)}, bf16[32,128]{1,0:T(8,128)(2,1)S(1)}, u32[]{:S(2)}, u32[]{:S(2)}) collective-permute-start(bf16[32,128]{1,0:T(8,128)(2,1)S(1)} %get-tuple-element.20), channel_id=1, source_target_pairs={{0,128},{128,0},{4,132},{132,4},{8,136},{136,8},{12,140},{140,12},... | collective-permute-start | bytes 24584 | tf_op jit(solution)/shard_map/ppermute | solution.py:231
  83.6 6.2 %collective-permute-start.9 = (bf16[32,128]{1,0:T(8,128)(2,1)S(1)}, bf16[32,128]{1,0:T(8,128)(2,1)S(1)}, u32[]{:S(2)}, u32[]{:S(2)}) collective-permute-start(bf16[32,128]{1,0:T(8,128)(2,1)S(1)} %get-tuple-element.21), channel_id=1, source_target_pairs={{32,64},{64,32},{36,68},{68,36},{40,72},{72,40},{44,76},{76,44},{4... | collective-permute-start | bytes 24584 | tf_op jit(solution)/shard_map/ppermute | solution.py:231
  89.7 1.9 %collective-permute-start.8 = (bf16[32,128]{1,0:T(8,128)(2,1)S(1)}, bf16[32,128]{1,0:T(8,128)(2,1)S(1)}, u32[]{:S(2)}, u32[]{:S(2)}) collective-permute-start(bf16[32,128]{1,0:T(8,128)(2,1)S(1)} %get-tuple-element.22), channel_id=1, source_target_pairs={{0,32},{32,0},{4,36},{36,4},{8,40},{40,8},{12,44},{44,12},{16,48},... | collective-permute-start | bytes 24584 | tf_op jit(solution)/shard_map/ppermute | solution.py:231
  91.7 4.2 %collective-permute-start.7 = (bf16[32,128]{1,0:T(8,128)(2,1)S(1)}, bf16[32,128]{1,0:T(8,128)(2,1)S(1)}, u32[]{:S(2)}, u32[]{:S(2)}) collective-permute-start(bf16[32,128]{1,0:T(8,128)(2,1)S(1)} %get-tuple-element.23), channel_id=1, source_target_pairs={{4,8},{8,4},{12,16},{16,12},{20,24},{24,20},{28,32},{32,28},{36,40... | collective-permute-start | bytes 24584 | tf_op jit(solution)/shard_map/ppermute | solution.py:231
  95.9 3.5 %collective-permute-start.6 = (bf16[32,128]{1,0:T(8,128)(2,1)S(1)}, bf16[32,128]{1,0:T(8,128)(2,1)S(1)}, u32[]{:S(2)}, u32[]{:S(2)}) collective-permute-start(bf16[32,128]{1,0:T(8,128)(2,1)S(1)} %get-tuple-element.24), channel_id=1, source_target_pairs={{0,4},{4,0},{8,12},{12,8},{16,20},{20,16},{24,28},{28,24},{32,36},... | collective-permute-start | bytes 24584 | tf_op jit(solution)/shard_map/ppermute | solution.py:231
  99.4 0.8 collective-permute-done.6.r0
  100.2 0.9 shard_map.124
  (26 shorter events, 0.2 us)
Async XLA Ops:
  0.6 0.7 copy-start.6
  0.6 0.7 copy-start.7
  1.4 0.7 copy-start.4
  2.5 25.1 %copy-start.8 = (f32[1,3,4096]{2,0,1:T(1,128)S(1)}, f32[1,3,4096]{2,0,1:T(1,128)}, u32[]{:S(2)}) copy-start(f32[1,3,4096]{2,0,1:T(1,128)} %param.16) | copy-start | bytes 147460
  2.5 25.9 %copy-start = (bf16[384,128]{1,0:T(8,128)(2,1)S(1)}, bf16[384,128]{1,0:T(8,128)(2,1)}, u32[]{:S(2)}) copy-start(bf16[384,128]{1,0:T(8,128)(2,1)} %wmix_ref.1) | copy-start | bytes 294916
  2.5 20.0 %collective-permute-start.5 = (bf16[32,128]{1,0:T(8,128)(2,1)S(1)}, bf16[32,128]{1,0:T(8,128)(2,1)S(1)}, u32[]{:S(2)}, u32[]{:S(2)}) collective-permute-start(bf16[32,128]{1,0:T(8,128)(2,1)S(1)} %get-tuple-element.25), channel_id=1, source_target_pairs={{128,256},{256,128},{132,260},{260,132},{136,264},{264,136},{140,2... | collective-permute-start | bytes 24584 | tf_op jit(solution)/shard_map/ppermute | solution.py:231
  9.7 18.0 %collective-permute-start.4 = (bf16[32,128]{1,0:T(8,128)(2,1)S(1)}, bf16[32,128]{1,0:T(8,128)(2,1)S(1)}, u32[]{:S(2)}, u32[]{:S(2)}) collective-permute-start(bf16[32,128]{1,0:T(8,128)(2,1)S(1)} %get-tuple-element.26), channel_id=1, source_target_pairs={{0,128},{128,0},{4,132},{132,4},{8,136},{136,8},{12,140},{140,12},... | collective-permute-start | bytes 24584 | tf_op jit(solution)/shard_map/ppermute | solution.py:231
  11.7 16.1 %collective-permute-start.3 = (bf16[32,128]{1,0:T(8,128)(2,1)S(1)}, bf16[32,128]{1,0:T(8,128)(2,1)S(1)}, u32[]{:S(2)}, u32[]{:S(2)}) collective-permute-start(bf16[32,128]{1,0:T(8,128)(2,1)S(1)} %get-tuple-element.27), channel_id=1, source_target_pairs={{32,64},{64,32},{36,68},{68,36},{40,72},{72,40},{44,76},{76,44},{4... | collective-permute-start | bytes 24584 | tf_op jit(solution)/shard_map/ppermute | solution.py:231
  15.8 12.0 %collective-permute-start.2 = (bf16[32,128]{1,0:T(8,128)(2,1)S(1)}, bf16[32,128]{1,0:T(8,128)(2,1)S(1)}, u32[]{:S(2)}, u32[]{:S(2)}) collective-permute-start(bf16[32,128]{1,0:T(8,128)(2,1)S(1)} %get-tuple-element.28), channel_id=1, source_target_pairs={{0,32},{32,0},{4,36},{36,4},{8,40},{40,8},{12,44},{44,12},{16,48},... | collective-permute-start | bytes 24584 | tf_op jit(solution)/shard_map/ppermute | solution.py:231
  17.9 9.9 %collective-permute-start.1 = (bf16[32,128]{1,0:T(8,128)(2,1)S(1)}, bf16[32,128]{1,0:T(8,128)(2,1)S(1)}, u32[]{:S(2)}, u32[]{:S(2)}) collective-permute-start(bf16[32,128]{1,0:T(8,128)(2,1)S(1)} %get-tuple-element.29), channel_id=1, source_target_pairs={{4,8},{8,4},{12,16},{16,12},{20,24},{24,20},{28,32},{32,28},{36,40... | collective-permute-start | bytes 24584 | tf_op jit(solution)/shard_map/ppermute | solution.py:231
  22.5 5.8 %collective-permute-start = (bf16[32,128]{1,0:T(8,128)(2,1)S(1)}, bf16[32,128]{1,0:T(8,128)(2,1)S(1)}, u32[]{:S(2)}, u32[]{:S(2)}) collective-permute-start(bf16[32,128]{1,0:T(8,128)(2,1)S(1)} %get-tuple-element.30), channel_id=1, source_target_pairs={{0,4},{4,0},{8,12},{12,8},{16,20},{20,16},{24,28},{28,24},{32,36},... | collective-permute-start | bytes 24584 | tf_op jit(solution)/shard_map/ppermute | solution.py:231
  27.6 0.8 copy-start.1
  27.6 0.7 copy-start.2
  27.6 0.7 copy-start.3
  27.7 0.7 copy-start.5
  72.7 27.5 %all-to-all-start.2 = ((bf16[32,16,128]{2,1,0:T(8,128)(2,1)}), bf16[32,16,128]{2,1,0:T(8,128)(2,1)S(1)}, u32[]{:S(2)}, u32[]{:S(2)}) async-start(bf16[32,16,128]{2,1,0:T(8,128)(2,1)} %tile.5), calls=%async_computation.2 | async-start | bytes 262144 | tf_op jit(solution)/shard_map/all_to_all | solution.py:239
  78.2 17.7 %collective-permute-start.11 = (bf16[32,128]{1,0:T(8,128)(2,1)S(1)}, bf16[32,128]{1,0:T(8,128)(2,1)S(1)}, u32[]{:S(2)}, u32[]{:S(2)}) collective-permute-start(bf16[32,128]{1,0:T(8,128)(2,1)S(1)} %get-tuple-element.19), channel_id=1, source_target_pairs={{128,256},{256,128},{132,260},{260,132},{136,264},{264,136},{140,2... | collective-permute-start | bytes 24584 | tf_op jit(solution)/shard_map/ppermute | solution.py:231
  81.3 18.0 %collective-permute-start.10 = (bf16[32,128]{1,0:T(8,128)(2,1)S(1)}, bf16[32,128]{1,0:T(8,128)(2,1)S(1)}, u32[]{:S(2)}, u32[]{:S(2)}) collective-permute-start(bf16[32,128]{1,0:T(8,128)(2,1)S(1)} %get-tuple-element.20), channel_id=1, source_target_pairs={{0,128},{128,0},{4,132},{132,4},{8,136},{136,8},{12,140},{140,12},... | collective-permute-start | bytes 24584 | tf_op jit(solution)/shard_map/ppermute | solution.py:231
  83.6 15.8 %collective-permute-start.9 = (bf16[32,128]{1,0:T(8,128)(2,1)S(1)}, bf16[32,128]{1,0:T(8,128)(2,1)S(1)}, u32[]{:S(2)}, u32[]{:S(2)}) collective-permute-start(bf16[32,128]{1,0:T(8,128)(2,1)S(1)} %get-tuple-element.21), channel_id=1, source_target_pairs={{32,64},{64,32},{36,68},{68,36},{40,72},{72,40},{44,76},{76,44},{4... | collective-permute-start | bytes 24584 | tf_op jit(solution)/shard_map/ppermute | solution.py:231
  89.7 9.7 %collective-permute-start.8 = (bf16[32,128]{1,0:T(8,128)(2,1)S(1)}, bf16[32,128]{1,0:T(8,128)(2,1)S(1)}, u32[]{:S(2)}, u32[]{:S(2)}) collective-permute-start(bf16[32,128]{1,0:T(8,128)(2,1)S(1)} %get-tuple-element.22), channel_id=1, source_target_pairs={{0,32},{32,0},{4,36},{36,4},{8,40},{40,8},{12,44},{44,12},{16,48},... | collective-permute-start | bytes 24584 | tf_op jit(solution)/shard_map/ppermute | solution.py:231
  91.7 7.7 %collective-permute-start.7 = (bf16[32,128]{1,0:T(8,128)(2,1)S(1)}, bf16[32,128]{1,0:T(8,128)(2,1)S(1)}, u32[]{:S(2)}, u32[]{:S(2)}) collective-permute-start(bf16[32,128]{1,0:T(8,128)(2,1)S(1)} %get-tuple-element.23), channel_id=1, source_target_pairs={{4,8},{8,4},{12,16},{16,12},{20,24},{24,20},{28,32},{32,28},{36,40... | collective-permute-start | bytes 24584 | tf_op jit(solution)/shard_map/ppermute | solution.py:231
  95.9 4.3 %collective-permute-start.6 = (bf16[32,128]{1,0:T(8,128)(2,1)S(1)}, bf16[32,128]{1,0:T(8,128)(2,1)S(1)}, u32[]{:S(2)}, u32[]{:S(2)}) collective-permute-start(bf16[32,128]{1,0:T(8,128)(2,1)S(1)} %get-tuple-element.24), channel_id=1, source_target_pairs={{0,4},{4,0},{8,12},{12,8},{16,20},{20,16},{24,28},{28,24},{32,36},... | collective-permute-start | bytes 24584 | tf_op jit(solution)/shard_map/ppermute | solution.py:231

commit v2 on v1

--- a/solution.py
+++ b/solution.py
@@ -20,12 +20,13 @@
 ROWS = ATOMS + FACES * PAD
 EDGES = 4096
 CHUNK = 1024
-GROUP = 32
-SLOT = 16
-SLAB = ("x", "y", "core")
-LINE = ("zl", "rep")
+SHARD = 32
+BLOCKS = 16
+PLANE = ("zl", "x")
+REST = ("y", "core", "rep")
+PEERS = 32
 DOM = ("zl", "x", "y", "core")
-STEPS = (1, 8, 32)
+STRIDES = (1, -1, 4, -4)
 HIGH = lax.Precision.HIGHEST
 VMEM_LIMIT = 48 * 1024 * 1024
 
@@ -55,29 +56,31 @@
     )(*args)
 
 
-def pre_kernel(feat_ref, species_ref, gain_ref, sends_ref, own_ref, gain_out, pick_ref):
+def pre_kernel(feat_ref, species_ref, gain_ref, sends_ref, own_ref, gain_out, pair_ref, pick_ref):
     hot = (rows_iota((8, ATOMS)) == species_ref[...]).astype(f32)
     gains = jnp.concatenate([gain_ref[...], jnp.zeros((3, CHANS), f32)], axis=0)
     gain = dot(hot, gains, ((0,), (0,)), HIGH)
     own = (feat_ref[0].astype(f32) * gain).astype(bf16)
     own_ref[...] = own
     gain_out[...] = gain
-    dom = domain()
+    plane, bit = position()
+    pick_ref[...] = jnp.zeros_like(pick_ref)
     for face in range(FACES):
-        hot = (rows_iota((ATOMS, GHOST)) == sends_ref[0, face : face + 1, :]).astype(f32)
+        hot = (rows_iota((ATOMS, GHOST)) == sends_ref[face]).astype(f32)
         hot = jnp.concatenate([hot, jnp.zeros((ATOMS, PAD - GHOST), f32)], axis=1)
-        picked = dot(hot.astype(bf16), own, ((0,), (0,)))
-        bit = lax.rem(dom // STEPS[face // 2], 2)
-        pick_ref[2 * (face // 2) + lax.rem(bit + face % 2, 2)] = picked.astype(bf16)
-
-
-def domain():
-    z, x, y, c = (lax.axis_index(a) for a in DOM)
-    return ((z * 4 + x) * 4 + y) * 2 + c
+        picked = dot(hot.astype(bf16), own, ((0,), (0,))).astype(bf16)
+        if face < 2:
+            pair_ref[lax.rem(bit + face, 2)] = picked
+        else:
+            pick_ref[lax.rem(plane + STRIDES[face - 2] + BLOCKS, BLOCKS)] = picked
+
+
+def position():
+    return lax.axis_index("zl") * 4 + lax.axis_index("x"), lax.axis_index("core")
 
 
 def geo_kernel(vec_ref, harm_ref, basis_ref):
-    vx, vy, vz = (vec_ref[0, i : i + 1, :] for i in range(3))
+    vx, vy, vz = (vec_ref[i] for i in range(3))
     square = vx * vx + vy * vy + vz * vz + 0.25
     inv_r = lax.rsqrt(square)
     radius = square * inv_r
@@ -124,19 +127,15 @@
 
 
 def main_kernel(
-    own_ref, r0, r1, r2, r3, r4, r5, src_ref, dst_ref, harm_ref, basis_ref, wrad_ref, wmix_ref, cot_ref,
-    dext_ref, back_ref, grad_ref,
+    own_ref, p0, p1, got_ref, src_ref, dst_ref, harm_ref, basis_ref, wrad_ref, wmix_ref, cot_ref,
+    dext_ref, pair_ref, send_ref,
     hot_s, harm_s, radial_s, source_s, mom_s, dmom_s,
 ):
-    dom = domain()
-    got = (r0, r1, r2, r3, r4, r5)
-    blocks = [own_ref[...].astype(f32)]
-    bits = [lax.rem(dom // step, 2) for step in STEPS]
-    for face in range(FACES):
-        pair = face // 2
-        a, b = got[2 * pair][...].astype(f32), got[2 * pair + 1][...].astype(f32)
-        swapped = lax.rem(bits[pair] + face % 2, 2) == 0
-        blocks.append(jnp.where(swapped, b, a))
+    plane, bit = position()
+    a, b = p0[...].astype(f32), p1[...].astype(f32)
+    blocks = [own_ref[...].astype(f32), jnp.where(bit == 0, b, a), jnp.where(bit == 0, a, b)]
+    for stride in STRIDES:
+        blocks.append(got_ref[lax.rem(plane - stride + BLOCKS, BLOCKS)].astype(f32))
     ext = jnp.concatenate(blocks, axis=0).T.astype(bf16)
     w_top, w_low = split(wrad_ref[...])
     wrad = jnp.concatenate([w_top, w_low, w_top], axis=0).T.astype(bf16)
@@ -172,7 +171,9 @@
     sigma = jax.nn.sigmoid(pre)
     slope = sigma * (1.0 + pre * (1.0 - sigma))
     dpre = (cot_ref[0].astype(f32) * slope).astype(bf16)
-    grad_ref[0 : 3 * CHANS, :] = dot(inv, dpre, ((0,), (0,))).astype(bf16)
+    gmix = dot(inv, dpre, ((0,), (0,))).astype(bf16)
+    for i in range(3 * CHANS // SHARD):
+        send_ref[i, 0:SHARD] = gmix[i * SHARD : (i + 1) * SHARD]
     dinv = dot(dpre, wmix_ref[...], ((1,), (1,)))
     groups = [0, 1, 1, 1, 2, 2, 2, 2, 2]
     for k in range(9):
@@ -190,73 +191,101 @@
         b_top, b_low = split(basis_ref[:, at])
         basis = jnp.concatenate([b_top, b_low], axis=0).astype(bf16)
         gradr = gradr + dot(basis, dradial.astype(bf16), ((1,), (1,)))
-    gradr = jnp.concatenate([gradr[:NB] + gradr[NB:], jnp.zeros((NB, CHANS), f32)], axis=0)
-    grad_ref[3 * CHANS : 3 * CHANS + 2 * NB, :] = gradr.astype(bf16)
-    rest = GROUP * SLOT - 3 * CHANS - 2 * NB
-    grad_ref[3 * CHANS + 2 * NB :, :] = jnp.zeros((rest, CHANS), bf16)
+    gradr = jnp.concatenate([gradr[:NB] + gradr[NB:], jnp.zeros((SHARD - NB, CHANS), f32)], axis=0)
+    send_ref[3 * CHANS // SHARD, 0:SHARD] = gradr.astype(bf16)
+    for i in range(3 * CHANS // SHARD + 1, BLOCKS):
+        send_ref[i, 0:SHARD] = jnp.zeros((SHARD, CHANS), bf16)
+    for i in range(BLOCKS):
+        send_ref[i, SHARD:] = jnp.zeros((PAD, CHANS), bf16)
     dext_ref[...] = dext[:ATOMS]
     for face in range(FACES):
-        pair = face // 2
         start = ATOMS + face * PAD
-        slot = 2 * pair + lax.rem(bits[pair] + face % 2 + 1, 2)
-        back_ref[slot] = dext[start : start + PAD].astype(bf16)
-
-
-def post_kernel(dext_ref, gain_ref, sends_ref, r0, r1, r2, r3, r4, r5, sums_ref, dfeat_ref, gmix_ref, grad_ref):
-    dom = domain()
-    got = (r0, r1, r2, r3, r4, r5)
+        block = dext[start : start + PAD].astype(bf16)
+        if face < 2:
+            pair_ref[lax.rem(bit + face + 1, 2)] = block
+        else:
+            to = lax.rem(plane - STRIDES[face - 2] + BLOCKS, BLOCKS)
+            send_ref[to, SHARD:] = block
+
+
+def total_kernel(parts_ref, out_ref):
+    total = parts_ref[0, :SHARD].astype(f32)
+    for i in range(1, parts_ref.shape[0]):
+        total = total + parts_ref[i, :SHARD].astype(f32)
+    total = total.astype(bf16)
+    for i in range(out_ref.shape[0]):
+        out_ref[i] = total
+
+
+def post_kernel(
+    dext_ref, gain_ref, sends_ref, p0, p1, got_ref, sums_ref, dfeat_ref, gmix_ref, grad_ref
+):
+    plane, bit = position()
+    a, b = p0[...].astype(f32), p1[...].astype(f32)
+    blocks = [jnp.where(bit == 0, a, b), jnp.where(bit == 0, b, a)]
+    for stride in STRIDES:
+        blocks.append(got_ref[lax.rem(plane + stride + BLOCKS, BLOCKS), SHARD:].astype(f32))
     total = dext_ref[...]
     for face in range(FACES):
-        pair = face // 2
-        bit = lax.rem(dom // STEPS[pair], 2)
-        a, b = got[2 * pair][...].astype(f32), got[2 * pair + 1][...].astype(f32)
-        values = jnp.where(lax.rem(bit + face % 2, 2) == 0, a, b)[:GHOST].astype(bf16)
-        hot = (rows_iota((ATOMS, GHOST)) == sends_ref[0, face : face + 1, :]).astype(f32)
+        hot = (rows_iota((ATOMS, GHOST)) == sends_ref[face]).astype(f32)
+        values = blocks[face][:GHOST].astype(bf16)
         total = total + dot(hot.astype(bf16), values, ((1,), (0,)))
     dfeat_ref[0] = total * gain_ref[...]
-    sums = sums_ref[0 : 3 * CHANS + 2 * NB, :].astype(f32)
-    gmix, grad = sums[: 3 * CHANS], sums[3 * CHANS : 3 * CHANS + NB]
-    norm = jnp.sqrt(jnp.sum(gmix * gmix, keepdims=True) + jnp.sum(grad * grad, keepdims=True))
+    whole = 3 * CHANS // SHARD
+    parts = [sums_ref[i].astype(f32) for i in range(whole)]
+    grad = sums_ref[whole].astype(f32)[:NB]
+    square = grad * grad
+    for part in parts:
+        for i in range(0, SHARD, NB):
+            square = square + part[i : i + NB] * part[i : i + NB]
+    norm = jnp.sqrt(jnp.sum(square, keepdims=True))
     factor = clip_norm / jnp.maximum(norm, clip_norm)
-    gmix_ref[...] = factor * gmix
+    for i, part in enumerate(parts):
+        gmix_ref[i * SHARD : (i + 1) * SHARD, :] = factor * part
     grad_ref[...] = factor * grad
 
 
-def swap(block, step, parity):
+def swap(block, parity):
     pairs = []
-    for i in range(128):
-        if (i // step) % 2 == parity:
-            j = (i + step) % 128
-            pairs += [(i, j), (j, i)]
+    for i in range(parity, 128, 2):
+        j = (i + 1) % 128
+        pairs += [(i, j), (j, i)]
     return lax.ppermute(block, DOM, pairs)
 
 
-def reduce_all(grads):
-    parts = lax.all_to_all(grads, SLAB, 0, 0, tiled=True)
-    mine = parts.reshape(GROUP, SLOT, CHANS).astype(f32).sum(0).astype(bf16)
-    parts = lax.all_to_all(jnp.tile(mine, (16, 1)), LINE, 0, 0, tiled=True)
-    mine = parts.reshape(16, SLOT, CHANS).astype(f32).sum(0).astype(bf16)
-    return lax.all_to_all(jnp.tile(mine, (GROUP, 1)), SLAB, 0, 0, tiled=True)
+def exchange(blocks, axes):
+    return lax.all_to_all(blocks, axes, 0, 0, tiled=True)
 
 
 def on_device(feat, species, species_gain, send_lists, edge_src, edge_dst, edge_vec, w_rad, w_mix, out_cot):
     shape = jax.ShapeDtypeStruct
-    own, gain, picks = call(
+    sends = send_lists.reshape(FACES, 1, GHOST)
+    own, gain, pair, picks = call(
         pre_kernel,
-        [shape((ATOMS, CHANS), bf16), shape((ATOMS, CHANS), f32), shape((FACES, PAD, CHANS), bf16)],
-        feat, species, species_gain, send_lists,
-    )
-    got = [swap(picks[2 * p + q], STEPS[p], q) for p in range(3) for q in range(2)]
+        [
+            shape((ATOMS, CHANS), bf16),
+            shape((ATOMS, CHANS), f32),
+            shape((2, PAD, CHANS), bf16),
+            shape((BLOCKS, PAD, CHANS), bf16),
+        ],
+        feat, species, species_gain, sends,
+    )
+    near = [swap(pair[q], q) for q in range(2)]
+    far = exchange(picks, PLANE)
     harm, basis = call(
         geo_kernel,
         [shape((16, EDGES), f32), shape((NB, EDGES), f32)],
-        edge_vec,
+        edge_vec.reshape(3, 1, EDGES),
         cost=pl.CostEstimate(flops=1000000, bytes_accessed=400000, transcendentals=0),
     )
-    dext, back, grads = call(
+    dext, pair, blocks = call(
         main_kernel,
-        [shape((ATOMS, CHANS), f32), shape((FACES, PAD, CHANS), bf16), shape((GROUP * SLOT, CHANS), bf16)],
-        own, *got, edge_src, edge_dst, harm, basis, w_rad, w_mix, out_cot,
+        [
+            shape((ATOMS, CHANS), f32),
+            shape((2, PAD, CHANS), bf16),
+            shape((BLOCKS, SHARD + PAD, CHANS), bf16),
+        ],
+        own, *near, far, edge_src, edge_dst, harm, basis, w_rad, w_mix, out_cot,
         scratch=[
             pltpu.VMEM((ROWS, EDGES), bf16),
             pltpu.VMEM((9 * ATOMS, EDGES), bf16),
@@ -266,12 +295,16 @@
             pltpu.VMEM((CHANS, 9 * ATOMS), bf16),
         ],
     )
-    returned = [swap(back[2 * p + q], STEPS[p], q) for p in range(3) for q in range(2)]
-    sums = reduce_all(grads)
+    near = [swap(pair[q], q) for q in range(2)]
+    far = exchange(blocks, PLANE)
+    (parts,) = call(total_kernel, [shape((PEERS, SHARD, CHANS), bf16)], far)
+    parts = exchange(parts, REST)
+    (parts,) = call(total_kernel, [shape((BLOCKS, SHARD, CHANS), bf16)], parts)
+    sums = exchange(parts, PLANE)
     d_feat, gmix, grad_r = call(
         post_kernel,
         [shape((1, ATOMS, CHANS), f32), shape((3 * CHANS, CHANS), f32), shape((NB, CHANS), f32)],
-        dext, gain, send_lists, *returned, sums,
+        dext, gain, sends, *near, far, sums,
     )
     return d_feat, gmix, grad_r
 

time: 102 us -> 100 us (0.980)
  starting transfers between devices: 51.6 us -> 37.6 us
  blocking collectives: 37.5 us -> 48.2 us
  Pallas kernels: 7.37 us -> 8.77 us
    ppermute x12 -> x4, starting transfers between devices: 46.1 us -> 22 us  [swap(): return lax.ppermute(block, DOM, pairs)]
    all_to_all x2, blocking collectives: 37.5 us -> 48.2 us  [exchange(): return lax.all_to_all(blocks, axes, 0, 0, tiled=True)]
    all_to_all x1 -> x2, starting transfers between devices: 5.5 us -> 15.6 us  [exchange(): return lax.all_to_all(blocks, axes, 0, 0, tiled=True)]
    pallas_call x4 -> x6, Pallas kernels: 7.37 us -> 8.77 us  [call(): pl.pallas_call(kernel, out_shape=outs, in_specs=[spec(a) for a in args],...]
    unnamed x20 -> x22, local copies, waits for them, and re-layouts: 1.54 us -> 2.77 us
  transfers between devices with their start and end apart: 13 -> 6, of which waited for: 2 -> 2; matrix products, arithmetic and copies ran while one was open for 0% -> 0% of each run, Pallas kernels for 0% -> 0%
where the time goes in v2:
time: 100 us; the launch traced here: 99.7 us
  blocking collectives  48.2 us (48%)
  starting transfers between devices  37.6 us (38%)
  Pallas kernels  8.77 us (9%)
  local copies, waits for them, and re-layouts  2.78 us (3%)
  waiting for transfers between devices  1.46 us (1%)
    all_to_all x2, blocking collectives, exchange(): return lax.all_to_all(blocks, axes, 0, 0, tiled=True)  48.2 us
    ppermute x4, starting transfers between devices, swap(): return lax.ppermute(block, DOM, pairs)  22 us
    all_to_all x2, starting transfers between devices, exchange(): return lax.all_to_all(blocks, axes, 0, 0, tiled=True)  15.6 us
    pallas_call x6, Pallas kernels, call(): pl.pallas_call(kernel, out_shape=outs, in_specs=[spec(a) for a in args],...  8.77 us
    unnamed x22, local copies, waits for them, and re-layouts  2.77 us
  transfers between devices with their start and end apart: 6, of which 2 were waited for; matrix products, arithmetic and copies ran while one was open for 0% of the time, Pallas kernels for 0%

profile of v2, /device:TPU:1, one launch (start us, length us, event | category | flops | bytes accessed | tf_op | source)
XLA Modules:
  0.0 99.7 jit_solution(3372760865235486959)
XLA Ops:
  0.6 0.0 copy-start.10
  0.6 0.6 copy-done.10
  1.3 0.7 copy-done.5
  2.0 0.7 copy-done.6
  2.7 0.7 copy-done.9
  3.4 1.1 %shard_map.121 = (bf16[64,128]{1,0:T(8,128)(2,1)S(1)}, f32[64,128]{1,0:T(8,128)S(1)}, bf16[2,32,128]{2,1,0:T(8,128)(2,1)S(1)}, bf16[16,32,128]{2,1,0:T(8,128)(2,1)}) custom-call(bf16[1,64,128]{2,1,0:T(8,128)(2,1)S(1)} %copy-done.5, s32[1,64]{1,0:T(1,128)S(1)} %copy-done.10, f32[5,128]{1,0:T(8,128)S(1)} %copy-done.9, s32[6,1,24]{2,1,0:T(1,128)S(1)} %bitcast.11), custom_call_target="tpu_custom_call" | custom-call | tf_op jit(solution)/shard_map/pallas_call | solution.py:48
  4.4 9.1 %all-to-all-start = ((bf16[16,32,128]{2,1,0:T(8,128)(2,1)}), bf16[16,32,128]{2,1,0:T(8,128)(2,1)S(1)}, u32[]{:S(2)}, u32[]{:S(2)}) async-start(bf16[16,32,128]{2,1,0:T(8,128)(2,1)} %get-tuple-element.14), calls=%async_computation | async-start | bytes 262144 | tf_op jit(solution)/shard_map/all_to_all | solution.py:257
  13.6 4.0 %collective-permute-start.1 = (bf16[32,128]{1,0:T(8,128)(2,1)S(1)}, bf16[32,128]{1,0:T(8,128)(2,1)S(1)}, u32[]{:S(2)}, u32[]{:S(2)}) collective-permute-start(bf16[32,128]{1,0:T(8,128)(2,1)S(1)} %get-tuple-element.23), channel_id=1, source_target_pairs={{4,8},{8,4},{12,16},{16,12},{20,24},{24,20},{28,32},{32,28},{36,40... | collective-permute-start | bytes 24584 | tf_op jit(solution)/shard_map/ppermute | solution.py:253
  17.7 7.9 %collective-permute-start = (bf16[32,128]{1,0:T(8,128)(2,1)S(1)}, bf16[32,128]{1,0:T(8,128)(2,1)S(1)}, u32[]{:S(2)}, u32[]{:S(2)}) collective-permute-start(bf16[32,128]{1,0:T(8,128)(2,1)S(1)} %get-tuple-element.24), channel_id=1, source_target_pairs={{0,4},{4,0},{8,12},{12,8},{16,20},{20,16},{24,28},{28,24},{32,36},... | collective-permute-start | bytes 24584 | tf_op jit(solution)/shard_map/ppermute | solution.py:253
  25.6 0.0 copy-done.1
  25.6 0.0 copy-start.2
  25.6 0.0 copy-start.3
  25.6 0.0 copy-start.4
  25.6 0.1 shard_map.122
  25.7 0.0 copy-start.8
  25.7 0.0 collective-permute-done.1.p1
  25.7 0.7 collective-permute-done.p0
  26.4 0.0 all-to-all-done.got_ref
  26.4 0.0 copy-done
  26.4 6.0 %shard_map.123 = (f32[64,128]{1,0:T(8,128)S(1)}, bf16[2,32,128]{2,1,0:T(8,128)(2,1)S(1)}, bf16[16,64,128]{2,1,0:T(8,128)(2,1)S(1)}) custom-call(bf16[64,128]{1,0:T(8,128)(2,1)S(1)} %get-tuple-element.12.own_ref, bf16[32,128]{1,0:T(8,128)(2,1)S(1)} %collective-permute-done.p0, bf16[32,128]{1,0:T(8,128)(2,1)S(1)} %collective-permute-done.1.p1, ...), custom_call_target="tpu_custom_call" | custom-call | tf_op jit(solution)/shard_map/pallas_call | solution.py:48
  32.4 12.7 %all_to_all.20.parts_ref.got_ref = bf16[16,64,128]{2,1,0:T(8,128)(2,1)S(1)} all-to-all(bf16[16,64,128]{2,1,0:T(8,128)(2,1)S(1)} %get-tuple-element.20), channel_id=1, replica_groups=mesh['zl'=4,'x'=4,'y'=4,'core'=2,'rep'=4] {'zl','x'}, dimensions={0} | all-to-all | bytes 524288 | tf_op jit(solution)/shard_map/all_to_all | solution.py:257
  45.2 35.5 %all_to_all.21.parts_ref = bf16[32,32,128]{2,1,0:T(8,128)(2,1)S(1)} all-to-all(bf16[32,32,128]{2,1,0:T(8,128)(2,1)S(1)} %shard_map.124), channel_id=1, replica_groups=mesh['zl'=4,'x'=4,'y'=4,'core'=2,'rep'=4] {'y','core','rep'}, dimensions={0} | all-to-all | bytes 524288 | tf_op jit(solution)/shard_map/all_to_all | solution.py:257
  80.7 0.7 shard_map.125
  81.4 6.4 %all-to-all-start.3 = ((bf16[16,32,128]{2,1,0:T(8,128)(2,1)}), bf16[16,32,128]{2,1,0:T(8,128)(2,1)S(1)}, u32[]{:S(2)}, u32[]{:S(2)}) async-start(bf16[16,32,128]{2,1,0:T(8,128)(2,1)} %shard_map.125), calls=%async_computation.3 | async-start | bytes 262144 | tf_op jit(solution)/shard_map/all_to_all | solution.py:257
  87.8 0.0 copy-start.7
  87.8 1.9 %collective-permute-start.3 = (bf16[32,128]{1,0:T(8,128)(2,1)S(1)}, bf16[32,128]{1,0:T(8,128)(2,1)S(1)}, u32[]{:S(2)}, u32[]{:S(2)}) collective-permute-start(bf16[32,128]{1,0:T(8,128)(2,1)S(1)} %get-tuple-element.21), channel_id=1, source_target_pairs={{4,8},{8,4},{12,16},{16,12},{20,24},{24,20},{28,32},{32,28},{36,40... | collective-permute-start | bytes 24584 | tf_op jit(solution)/shard_map/ppermute | solution.py:253
  89.8 8.2 %collective-permute-start.2 = (bf16[32,128]{1,0:T(8,128)(2,1)S(1)}, bf16[32,128]{1,0:T(8,128)(2,1)S(1)}, u32[]{:S(2)}, u32[]{:S(2)}) collective-permute-start(bf16[32,128]{1,0:T(8,128)(2,1)S(1)} %get-tuple-element.22), channel_id=1, source_target_pairs={{0,4},{4,0},{8,12},{12,8},{16,20},{20,16},{24,28},{28,24},{32,36},... | collective-permute-start | bytes 24584 | tf_op jit(solution)/shard_map/ppermute | solution.py:253
  97.9 0.0 collective-permute-done.3.p1
  98.0 0.8 collective-permute-done.2.p0
  98.8 0.0 all-to-all-done.3.sums_ref
  98.8 0.0 copy-done.7
  98.8 0.9 shard_map.126
  (12 shorter events, 0.1 us)
Async XLA Ops:
  0.6 0.7 copy-start.10
  1.3 0.7 copy-start.5
  2.0 0.7 copy-start.6
  2.7 0.7 copy-start.9
  4.4 21.1 %copy-start.1 = (f32[1,3,4096]{2,0,1:T(1,128)S(1)}, f32[1,3,4096]{2,0,1:T(1,128)}, u32[]{:S(2)}) copy-start(f32[1,3,4096]{2,0,1:T(1,128)} %param.16) | copy-start | bytes 147460
  4.4 21.9 %copy-start = (bf16[384,128]{1,0:T(8,128)(2,1)S(1)}, bf16[384,128]{1,0:T(8,128)(2,1)}, u32[]{:S(2)}) copy-start(bf16[384,128]{1,0:T(8,128)(2,1)} %wmix_ref.1) | copy-start | bytes 294916
  4.4 21.9 %all-to-all-start = ((bf16[16,32,128]{2,1,0:T(8,128)(2,1)}), bf16[16,32,128]{2,1,0:T(8,128)(2,1)S(1)}, u32[]{:S(2)}, u32[]{:S(2)}) async-start(bf16[16,32,128]{2,1,0:T(8,128)(2,1)} %get-tuple-element.14), calls=%async_computation | async-start | bytes 262144 | tf_op jit(solution)/shard_map/all_to_all | solution.py:257
  13.6 12.1 %collective-permute-start.1 = (bf16[32,128]{1,0:T(8,128)(2,1)S(1)}, bf16[32,128]{1,0:T(8,128)(2,1)S(1)}, u32[]{:S(2)}, u32[]{:S(2)}) collective-permute-start(bf16[32,128]{1,0:T(8,128)(2,1)S(1)} %get-tuple-element.23), channel_id=1, source_target_pairs={{4,8},{8,4},{12,16},{16,12},{20,24},{24,20},{28,32},{32,28},{36,40... | collective-permute-start | bytes 24584 | tf_op jit(solution)/shard_map/ppermute | solution.py:253
  17.7 8.7 %collective-permute-start = (bf16[32,128]{1,0:T(8,128)(2,1)S(1)}, bf16[32,128]{1,0:T(8,128)(2,1)S(1)}, u32[]{:S(2)}, u32[]{:S(2)}) collective-permute-start(bf16[32,128]{1,0:T(8,128)(2,1)S(1)} %get-tuple-element.24), channel_id=1, source_target_pairs={{0,4},{4,0},{8,12},{12,8},{16,20},{20,16},{24,28},{28,24},{32,36},... | collective-permute-start | bytes 24584 | tf_op jit(solution)/shard_map/ppermute | solution.py:253
  25.6 0.8 copy-start.2
  25.6 0.8 copy-start.3
  25.6 0.8 copy-start.4
  25.7 0.7 copy-start.8
  81.4 17.4 %all-to-all-start.3 = ((bf16[16,32,128]{2,1,0:T(8,128)(2,1)}), bf16[16,32,128]{2,1,0:T(8,128)(2,1)S(1)}, u32[]{:S(2)}, u32[]{:S(2)}) async-start(bf16[16,32,128]{2,1,0:T(8,128)(2,1)} %shard_map.125), calls=%async_computation.3 | async-start | bytes 262144 | tf_op jit(solution)/shard_map/all_to_all | solution.py:257
  87.8 10.9 %copy-start.7 = (s32[1,6,24]{2,0,1:T(1,128)S(1)}, s32[1,6,24]{2,0,1:T(1,128)}, u32[]{:S(2)}) copy-start(s32[1,6,24]{2,0,1:T(1,128)} %param.13) | copy-start | bytes 1732
  87.8 10.1 %collective-permute-start.3 = (bf16[32,128]{1,0:T(8,128)(2,1)S(1)}, bf16[32,128]{1,0:T(8,128)(2,1)S(1)}, u32[]{:S(2)}, u32[]{:S(2)}) collective-permute-start(bf16[32,128]{1,0:T(8,128)(2,1)S(1)} %get-tuple-element.21), channel_id=1, source_target_pairs={{4,8},{8,4},{12,16},{16,12},{20,24},{24,20},{28,32},{32,28},{36,40... | collective-permute-start | bytes 24584 | tf_op jit(solution)/shard_map/ppermute | solution.py:253
  89.8 9.0 %collective-permute-start.2 = (bf16[32,128]{1,0:T(8,128)(2,1)S(1)}, bf16[32,128]{1,0:T(8,128)(2,1)S(1)}, u32[]{:S(2)}, u32[]{:S(2)}) collective-permute-start(bf16[32,128]{1,0:T(8,128)(2,1)S(1)} %get-tuple-element.22), channel_id=1, source_target_pairs={{0,4},{4,0},{8,12},{12,8},{16,20},{20,16},{24,28},{28,24},{32,36},... | collective-permute-start | bytes 24584 | tf_op jit(solution)/shard_map/ppermute | solution.py:253

commit v3 on v2

v3 whole, which is shorter than its diff:
```python
import jax
import jax.numpy as jnp
import numpy as np
from jax import lax
from jax.experimental import pallas as pl
from jax.experimental.pallas import tpu as pltpu
from jax.sharding import Mesh, PartitionSpec as P

msg_scale = 0.35
cutoff = 6.0
clip_norm = 256.0
f32, bf16 = jnp.float32, jnp.bfloat16

CHANS = 128
NB = 8
ATOMS = 64
FACES = 6
PAD = 32
GHOST = 24
ROWS = ATOMS + FACES * PAD
EDGES = 4096
CHUNK = 1024
SHARD = 16
RING = 16
PLANE = ("zl", "x", "core")
PEERS = 32
REST = ("y", "rep")
OTHERS = 16
DOM = ("zl", "x", "y", "core")
STRIDES = (1, -1, 4, -4)
HIGH = lax.Precision.HIGHEST


def dot(a, b, dims, precision=None):
    return lax.dot_general(
        a, b, (dims, ((), ())), precision=precision, preferred_element_type=f32
    )


def rows_iota(shape):
    return lax.broadcasted_iota(jnp.int32, shape, 0)


def call(kernel, outs, *args, scratch=(), cost=None, space=pltpu.VMEM, limit=32):
    return pl.pallas_call(
        kernel,
        out_shape=outs,
        in_specs=[pl.BlockSpec(memory_space=space) for _ in args],
        out_specs=[pl.BlockSpec(memory_space=pltpu.VMEM) for _ in outs],
        scratch_shapes=list(scratch),
        cost_estimate=cost,
        compiler_params=pltpu.CompilerParams(vmem_limit_bytes=limit * 1024 * 1024),
    )(*args)


def position():
    ring = lax.axis_index("zl") * 4 + lax.axis_index("x")
    return ring, lax.axis_index("core")


def peer(ring, stride, core):
    return lax.rem(ring + stride + RING, RING) * 2 + core


def pre_kernel(
    feat_hbm, species_hbm, gain_hbm, sends_hbm, own_ref, gain_out, next_ref, pick_ref,
    feat_ref, species_ref, gain_ref, sends_ref, sems,
):
    copies = [
        pltpu.make_async_copy(src, dst, sems.at[i])
        for i, (src, dst) in enumerate(
            [
                (feat_hbm, feat_ref),
                (species_hbm, species_ref),
                (gain_hbm, gain_ref),
                (sends_hbm, sends_ref),
            ]
        )
    ]
    for copy in copies:
        copy.start()
    pick_ref[...] = jnp.zeros_like(pick_ref)
    for copy in copies:
        copy.wait()
    hot = (rows_iota((8, ATOMS)) == species_ref[...]).astype(f32)
    gains = jnp.concatenate([gain_ref[...], jnp.zeros((3, CHANS), f32)], axis=0)
    gain = dot(hot, gains, ((0,), (0,)), HIGH)
    own = (feat_ref[0].astype(f32) * gain).astype(bf16)
    own_ref[...] = own
    gain_out[...] = gain
    ring, core = position()
    picked = []
    for face in range(FACES):
        hot = (rows_iota((ATOMS, GHOST)) == sends_ref[face]).astype(f32)
        hot = jnp.concatenate([hot, jnp.zeros((ATOMS, PAD - GHOST), f32)], axis=1)
        picked.append(dot(hot.astype(bf16), own, ((0,), (0,))))
    next_ref[...] = jnp.where(core == 0, picked[1], picked[0]).astype(bf16)
    pick_ref[peer(ring, 0, 1 - core)] = jnp.where(core == 0, picked[0], picked[1]).astype(bf16)
    for stride, block in zip(STRIDES, picked[2:]):
        pick_ref[peer(ring, stride, core)] = block.astype(bf16)


def prep_kernel(
    vec_ref, src_ref, dst_ref, wrad_ref, hot_ref, harm_ref, radial_ref, basis_ref, harm_s, basis_s
):
    geometry(vec_ref, harm_s, basis_s)
    w_top, w_low = split(wrad_ref[...])
    wrad = jnp.concatenate([w_top, w_low, w_top], axis=0).T.astype(bf16)
    for start in range(0, EDGES, CHUNK):
        at = pl.ds(start, CHUNK)
        src = src_ref[:, at]
        shift = jnp.zeros_like(src)
        for face in range(1, FACES):
            shift = shift + jnp.where(src >= ATOMS + face * GHOST, PAD - GHOST, 0)
        hot = jnp.where(rows_iota((ROWS, CHUNK)) == src + shift, 1.0, 0.0)
        hot_ref[:, at] = hot.astype(bf16)
        b_top, b_low = split(basis_s[:, at])
        basis = jnp.concatenate([b_top, b_top, b_low], axis=0).astype(bf16)
        radial_ref[:, at] = dot(wrad, basis, ((1,), (0,)))
        basis_ref[:, at] = jnp.concatenate([b_top, b_low], axis=0).astype(bf16)
        own_hot = rows_iota((ATOMS, CHUNK)) == dst_ref[:, at]
        harm_ref[0:ATOMS, at] = jnp.where(own_hot, 1.0, 0.0).astype(bf16)
        for k in range(1, 9):
            harm = harm_s[k : k + 1, at]
            harm_ref[k * ATOMS : (k + 1) * ATOMS, at] = jnp.where(own_hot, harm, 0.0).astype(bf16)


def geometry(vec_ref, harm_ref, basis_ref):
    vx, vy, vz = (vec_ref[i] for i in range(3))
    square = vx * vx + vy * vy + vz * vz + 0.25
    inv_r = lax.rsqrt(square)
    radius = square * inv_r
    ux, uy, uz = vx * inv_r, vy * inv_r, vz * inv_r
    r3, r5, r15 = 3.0**0.5, 5.0**0.5, 15.0**0.5
    harms = [
        jnp.ones_like(ux),
        r3 * ux,
        r3 * uy,
        r3 * uz,
        r15 * ux * uy,
        r15 * uy * uz,
        0.5 * r5 * (3.0 * uz * uz - 1.0),
        r15 * ux * uz,
        0.5 * r15 * (ux * ux - uy * uy),
    ]
    for k, h in enumerate(harms):
        harm_ref[k : k + 1, :] = h
    scaled = radius * (1.0 / cutoff)
    envelope = 1.0 - scaled * scaled
    envelope = envelope * envelope * inv_r
    t = scaled * np.float32(np.pi) - np.float32(np.pi / 2)
    t2 = t * t
    sin_t = series(t2, 1) * t
    cos_t = series(t2, 0)
    twice = -2.0 * sin_t
    before, now = jnp.zeros_like(t), cos_t * envelope
    for b in range(NB):
        basis_ref[b : b + 1, :] = now
        before, now = now, twice * now - before


def series(square, odd):
    terms = [(-1.0) ** n / float(np.prod(np.arange(1, 2 * n + odd + 1.0))) for n in range(9)]
    total = jnp.full_like(square, terms[-1])
    for term in terms[-2::-1]:
        total = total * square + term
    return total


def split(values):
    top = values.astype(bf16).astype(f32)
    return top, values - top


def main_kernel(
    own_ref, next_ref, got_ref, hot_ref, harm_ref, radial_ref, basis_ref, wmix_ref, cot_ref,
    dext_ref, back_ref, send_ref,
    source_s, mom_s, dmom_s,
):
    ring, core = position()
    near = got_ref[peer(ring, 0, 1 - core)].astype(f32)
    other = next_ref[...].astype(f32)
    blocks = [own_ref[...].astype(f32)]
    blocks += [jnp.where(core == 0, other, near), jnp.where(core == 0, near, other)]
    for stride in STRIDES:
        blocks.append(got_ref[peer(ring, -stride, core)].astype(f32))
    ext = jnp.concatenate(blocks, axis=0).T.astype(bf16)
    mom_s[...] = jnp.zeros_like(mom_s)
    for start in range(0, EDGES, CHUNK):
        at = pl.ds(start, CHUNK)
        source = dot(ext, hot_ref[:, at], ((1,), (0,)))
        source_s[:, at] = source.astype(bf16)
        message = (radial_ref[:, at] * source).astype(bf16)
        mom_s[...] += dot(harm_ref[:, at], message, ((1,), (1,)))
    moments = [msg_scale * mom_s[k * ATOMS : (k + 1) * ATOMS, :] for k in range(9)]
    squares = [m * m for m in moments]
    two = squares[4]
    for k in range(5, 9):
        two = two + squares[k]
    inv = jnp.concatenate([squares[0], squares[1] + squares[2] + squares[3], two], axis=1).astype(bf16)
    pre = dot(inv, wmix_ref[...], ((1,), (0,)))
    sigma = jax.nn.sigmoid(pre)
    slope = sigma * (1.0 + pre * (1.0 - sigma))
    dpre = (cot_ref[0].astype(f32) * slope).astype(bf16)
    gmix = dot(inv, dpre, ((0,), (0,))).astype(bf16)
    for i in range(3 * CHANS // SHARD):
        send_ref[i, 0:SHARD] = gmix[i * SHARD : (i + 1) * SHARD]
    dinv = dot(dpre, wmix_ref[...], ((1,), (1,)))
    groups = [0, 1, 1, 1, 2, 2, 2, 2, 2]
    for k in range(9):
        part = dinv[:, groups[k] * CHANS : (groups[k] + 1) * CHANS]
        mom_s[k * ATOMS : (k + 1) * ATOMS, :] = (2.0 * msg_scale) * moments[k] * part
    dmom_s[...] = mom_s[...].T.astype(bf16)
    dext = jnp.zeros((ROWS, CHANS), f32)
    gradr = jnp.zeros((2 * NB, CHANS), f32)
    for start in range(0, EDGES, CHUNK):
        at = pl.ds(start, CHUNK)
        dmsg = dot(dmom_s[...], harm_ref[:, at], ((1,), (0,)))
        dradial = dmsg * source_s[:, at].astype(f32)
        dsource = (dmsg * radial_ref[:, at]).astype(bf16)
        dext = dext + dot(hot_ref[:, at], dsource, ((1,), (1,)))
        gradr = gradr + dot(basis_ref[:, at], dradial.astype(bf16), ((1,), (1,)))
    gradr = jnp.concatenate([gradr[:NB] + gradr[NB:], jnp.zeros((SHARD - NB, CHANS), f32)], axis=0)
    send_ref[3 * CHANS // SHARD, 0:SHARD] = gradr.astype(bf16)
    for i in range(3 * CHANS // SHARD + 1, PEERS):
        send_ref[i, 0:SHARD] = jnp.zeros((SHARD, CHANS), bf16)
    for i in range(PEERS):
        send_ref[i, SHARD:] = jnp.zeros((PAD, CHANS), bf16)
    dext_ref[...] = dext[:ATOMS]
    ghosts = [dext[ATOMS + face * PAD : ATOMS + (face + 1) * PAD] for face in range(FACES)]
    back_ref[...] = jnp.where(core == 0, ghosts[0], ghosts[1]).astype(bf16)
    near = jnp.where(core == 0, ghosts[1], ghosts[0])
    send_ref[peer(ring, 0, 1 - core), SHARD:] = near.astype(bf16)
    for stride, block in zip(STRIDES, ghosts[2:]):
        send_ref[peer(ring, -stride, core), SHARD:] = block.astype(bf16)


def total_kernel(parts_ref, out_ref):
    total = parts_ref[0, :SHARD].astype(f32)
    for i in range(1, parts_ref.shape[0]):
        total = total + parts_ref[i, :SHARD].astype(f32)
    total = total.astype(bf16)
    for i in range(out_ref.shape[0]):
        out_ref[i] = total


def post_kernel(
    dext_ref, gain_ref, sends_ref, next_ref, got_ref, sums_ref, dfeat_ref, gmix_ref, grad_ref
):
    ring, core = position()
    near = got_ref[peer(ring, 0, 1 - core), SHARD:].astype(f32)
    other = next_ref[...].astype(f32)
    blocks = [jnp.where(core == 0, near, other), jnp.where(core == 0, other, near)]
    for stride in STRIDES:
        blocks.append(got_ref[peer(ring, stride, core), SHARD:].astype(f32))
    total = dext_ref[...]
    for face in range(FACES):
        hot = (rows_iota((ATOMS, GHOST)) == sends_ref[face]).astype(f32)
        values = blocks[face][:GHOST].astype(bf16)
        total = total + dot(hot.astype(bf16), values, ((1,), (0,)))
    dfeat_ref[0] = total * gain_ref[...]
    whole = 3 * CHANS // SHARD
    parts = [sums_ref[i].astype(f32) for i in range(whole)]
    grad = sums_ref[whole].astype(f32)[:NB]
    square = grad * grad
    for part in parts:
        for i in range(0, SHARD, NB):
            square = square + part[i : i + NB] * part[i : i + NB]
    norm = jnp.sqrt(jnp.sum(square, keepdims=True))
    factor = clip_norm / jnp.maximum(norm, clip_norm)
    for i, part in enumerate(parts):
        gmix_ref[i * SHARD : (i + 1) * SHARD, :] = factor * part
    grad_ref[...] = factor * grad


def swap(block):
    pairs = []
    for i in range(1, 128, 2):
        j = (i + 1) % 128
        pairs += [(i, j), (j, i)]
    return lax.ppermute(block, DOM, pairs)


def exchange(blocks, axes):
    return lax.all_to_all(blocks, axes, 0, 0, tiled=True)


def on_device(feat, species, species_gain, send_lists, edge_src, edge_dst, edge_vec, w_rad, w_mix, out_cot):
    shape = jax.ShapeDtypeStruct
    sends = send_lists.reshape(FACES, 1, GHOST)
    own, gain, block, picks = call(
        pre_kernel,
        [
            shape((ATOMS, CHANS), bf16),
            shape((ATOMS, CHANS), f32),
            shape((PAD, CHANS), bf16),
            shape((PEERS, PAD, CHANS), bf16),
        ],
        feat, species, species_gain, sends,
        scratch=[
            pltpu.VMEM((1, ATOMS, CHANS), bf16),
            pltpu.VMEM((1, ATOMS), jnp.int32),
            pltpu.VMEM((5, CHANS), f32),
            pltpu.VMEM((FACES, 1, GHOST), jnp.int32),
            pltpu.SemaphoreType.DMA((4,)),
        ],
        space=pl.ANY,
        limit=60,
    )
    near = swap(block)
    far = exchange(picks, PLANE)
    edges = call(
        prep_kernel,
        [
            shape((ROWS, EDGES), bf16),
            shape((9 * ATOMS, EDGES), bf16),
            shape((CHANS, EDGES), f32),
            shape((2 * NB, EDGES), bf16),
        ],
        edge_vec.reshape(3, 1, EDGES), edge_src, edge_dst, w_rad,
        scratch=[pltpu.VMEM((16, EDGES), f32), pltpu.VMEM((NB, EDGES), f32)],
        cost=pl.CostEstimate(flops=2000000000, bytes_accessed=9000000, transcendentals=0),
    )
    dext, block, blocks = call(
        main_kernel,
        [
            shape((ATOMS, CHANS), f32),
            shape((PAD, CHANS), bf16),
            shape((PEERS, SHARD + PAD, CHANS), bf16),
        ],
        own, near, far, *edges, w_mix, out_cot,
        scratch=[
            pltpu.VMEM((CHANS, EDGES), bf16),
            pltpu.VMEM((9 * ATOMS, CHANS), f32),
            pltpu.VMEM((CHANS, 9 * ATOMS), bf16),
        ],
    )
    near = swap(block)
    far = exchange(blocks, PLANE)
    (parts,) = call(total_kernel, [shape((OTHERS, SHARD, CHANS), bf16)], far)
    parts = exchange(parts, REST)
    (parts,) = call(total_kernel, [shape((PEERS, SHARD, CHANS), bf16)], parts)
    sums = exchange(parts, PLANE)
    d_feat, gmix, grad_r = call(
        post_kernel,
        [shape((1, ATOMS, CHANS), f32), shape((3 * CHANS, CHANS), f32), shape((NB, CHANS), f32)],
        dext, gain, sends, near, far, sums,
    )
    return d_feat, gmix, grad_r


def solution(mesh):
    fine = Mesh(mesh.devices.reshape(4, 4, 4, 2, 4), DOM + ("rep",))
    in_specs = (
        P("rep", DOM, None),
        P("rep", DOM),
        P(),
        P("rep", None, DOM),
        P("rep", DOM),
        P("rep", DOM),
        P("rep", None, DOM),
        P(),
        P(),
        P("rep", DOM, None),
    )
    out_specs = (P("rep", DOM, None), P(), P())
    return jax.shard_map(
        on_device, mesh=fine, in_specs=in_specs, out_specs=out_specs, check_vma=False
    )
```

time: 100 us -> 100 us (level)
  starting transfers between devices: 37.6 us -> 20.4 us
  local copies, waits for them, and re-layouts: 2.78 us -> 10.3 us
  waiting for transfers between devices: 1.46 us -> 6.45 us
  Pallas kernels: 8.77 us -> 11.8 us
  blocking collectives: 48.2 us -> 49.8 us
    ppermute x4 -> x2, starting transfers between devices: 22 us -> 5.04 us  [swap(): return lax.ppermute(block, DOM, pairs)]
    unnamed x22 -> x26, local copies, waits for them, and re-layouts: 2.77 us -> 10.3 us
    all_to_all x2, waiting for transfers between devices: 0.01 us -> 3.28 us  [exchange(): return lax.all_to_all(blocks, axes, 0, 0, tiled=True)]
    pallas_call x6, Pallas kernels: 8.77 us -> 11.8 us  [call(): pl.pallas_call(kernel, out_shape=outs, in_specs=[pl.BlockSpec(memory_spac...]
    ppermute x4 -> x2, waiting for transfers between devices: 1.46 us -> 3.16 us  [swap(): return lax.ppermute(block, DOM, pairs)]
    all_to_all x2, blocking collectives: 48.2 us -> 49.8 us  [exchange(): return lax.all_to_all(blocks, axes, 0, 0, tiled=True)]
  transfers between devices with their start and end apart: 6 -> 4, of which waited for: 2 -> 2; matrix products, arithmetic and copies ran while one was open for 0% -> 0% of each run, Pallas kernels for 0% -> 2%
where the time goes in v3:
time: 100 us; the launch traced here: 99.6 us
  blocking collectives  49.8 us (50%)
  starting transfers between devices  20.4 us (20%)
  Pallas kernels  11.8 us (12%)
  local copies, waits for them, and re-layouts  10.3 us (10%)
  waiting for transfers between devices  6.45 us (6%)
    all_to_all x2, blocking collectives, exchange(): return lax.all_to_all(blocks, axes, 0, 0, tiled=True)  49.8 us
    all_to_all x2, starting transfers between devices, exchange(): return lax.all_to_all(blocks, axes, 0, 0, tiled=True)  15.4 us
    pallas_call x6, Pallas kernels, call(): pl.pallas_call(kernel, out_shape=outs, in_specs=[pl.BlockSpec(memory_spac...  11.8 us
    unnamed x26, local copies, waits for them, and re-layouts  10.3 us
    ppermute x2, starting transfers between devices, swap(): return lax.ppermute(block, DOM, pairs)  5.04 us
    all_to_all x2, waiting for transfers between devices, exchange(): return lax.all_to_all(blocks, axes, 0, 0, tiled=True)  3.28 us
    ppermute x2, waiting for transfers between devices, swap(): return lax.ppermute(block, DOM, pairs)  3.16 us
  transfers between devices with their start and end apart: 4, of which 2 were waited for; matrix products, arithmetic and copies ran while one was open for 0% of the time, Pallas kernels for 2%

profile of v3, /device:TPU:1, one launch (start us, length us, event | category | flops | bytes accessed | tf_op | source)
XLA Modules:
  0.0 99.6 jit_solution(11492108853795298612)
XLA Ops:
  0.6 1.9 %shard_map.121 = (bf16[64,128]{1,0:T(8,128)(2,1)}, f32[64,128]{1,0:T(8,128)}, bf16[32,128]{1,0:T(8,128)(2,1)}, bf16[32,32,128]{2,1,0:T(8,128)(2,1)}) custom-call(bf16[1,64,128]{2,1,0:T(8,128)(2,1)} %feat_hbm.1, s32[1,64]{1,0:T(1,128)} %species_hbm.1, f32[5,128]{1,0:T(8,128)} %gain_hbm.1, s32[6,1,24]{2,1,0:T(1,128)} %bitcast.2), custom_call_target="tpu_custom_call" | custom-call | tf_op jit(solution)/shard_map/pallas_call | solution.py:45
  2.5 10.4 %all-to-all-start = ((bf16[32,32,128]{2,1,0:T(8,128)(2,1)}), bf16[32,32,128]{2,1,0:T(8,128)(2,1)S(1)}, u32[]{:S(2)}, u32[]{:S(2)}) async-start(bf16[32,32,128]{2,1,0:T(8,128)(2,1)} %get-tuple-element.16), calls=%async_computation | async-start | bytes 524288 | tf_op jit(solution)/shard_map/all_to_all | solution.py:285
  12.9 2.9 %collective-permute-start = (bf16[32,128]{1,0:T(8,128)(2,1)}, bf16[32,128]{1,0:T(8,128)(2,1)S(1)}, u32[]{:S(2)}, u32[]{:S(2)}) collective-permute-start(bf16[32,128]{1,0:T(8,128)(2,1)} %get-tuple-element.15), channel_id=1, source_target_pairs={{4,8},{8,4},{12,16},{16,12},{20,24},{24,20},{28,32},{32,28},{36,40... | collective-permute-start | bytes 24584 | tf_op jit(solution)/shard_map/ppermute | solution.py:281
  15.9 0.0 copy-start.9
  15.9 0.8 copy-done.9
  16.7 0.0 copy-start.10
  16.7 0.7 copy-done.10
  17.4 0.7 copy-done.11
  18.1 0.7 copy-done.12
  18.8 2.3 %shard_map.122 = (bf16[256,4096]{1,0:T(8,128)(2,1)S(1)}, bf16[576,4096]{1,0:T(8,128)(2,1)S(1)}, f32[128,4096]{1,0:T(8,128)S(1)}, bf16[16,4096]{1,0:T(8,128)(2,1)S(1)}) custom-call(f32[3,1,4096]{2,1,0:T(1,128)S(1)} %bitcast.4, s32[1,4096]{1,0:T(1,128)S(1)} %copy-done.10, s32[1,4096]{1,0:T(1,128)S(1)} %copy-done.11, f32[8,128]{1,0:T(8,128)S(1)} %copy-done.12), custom_call_target="tpu_custom_call" | custom-call | flops 2000000000 | bytes 9000000 | tf_op jit(solution)/shard_map/pallas_call | solution.py:45
  21.1 0.0 copy-start
  21.1 2.1 %copy-done = bf16[576,4096]{1,0:T(8,128)(2,1)} copy-done((bf16[576,4096]{1,0:T(8,128)(2,1)}, bf16[576,4096]{1,0:T(8,128)(2,1)S(1)}, u32[]{:S(2)}) %copy-start) | copy-done | bytes 4718616
  23.3 1.4 %copy-done.2 = f32[128,4096]{1,0:T(8,128)} copy-done((f32[128,4096]{1,0:T(8,128)}, f32[128,4096]{1,0:T(8,128)S(1)}, u32[]{:S(2)}) %copy-start.2) | copy-done | bytes 2097176
  24.6 0.0 collective-permute-done.next_ref
  24.6 0.0 all-to-all-done.got_ref
  24.6 0.0 copy-done.4
  24.6 0.0 copy-done.6
  24.6 0.0 copy-done.7
  24.6 0.0 copy-start.1
  24.6 2.3 %copy-done.1 = bf16[576,4096]{1,0:T(8,128)(2,1)S(1)} copy-done((bf16[576,4096]{1,0:T(8,128)(2,1)S(1)}, bf16[576,4096]{1,0:T(8,128)(2,1)}, u32[]{:S(2)}) %copy-start.1) | copy-done | bytes 4718616
  27.0 1.6 %copy-done.3 = f32[128,4096]{1,0:T(8,128)S(1)} copy-done((f32[128,4096]{1,0:T(8,128)S(1)}, f32[128,4096]{1,0:T(8,128)}, u32[]{:S(2)}) %copy-start.3) | copy-done | bytes 2097176
  28.6 6.0 %shard_map.123 = (f32[64,128]{1,0:T(8,128)S(1)}, bf16[32,128]{1,0:T(8,128)(2,1)S(1)}, bf16[32,48,128]{2,1,0:T(8,128)(2,1)S(1)}) custom-call(bf16[64,128]{1,0:T(8,128)(2,1)S(1)} %copy-done.7, bf16[32,128]{1,0:T(8,128)(2,1)S(1)} %collective-permute-done.next_ref, bf16[32,32,128]{2,1,0:T(8,128)(2,1)S(1)} %all-to-all-done.got_ref, ...), custom_call_target="tpu_custom_call" | custom-call | tf_op jit(solution)/shard_map/pallas_call | solution.py:45
  34.5 23.3 %all_to_all.20.parts_ref.got_ref = bf16[32,48,128]{2,1,0:T(8,128)(2,1)S(1)} all-to-all(bf16[32,48,128]{2,1,0:T(8,128)(2,1)S(1)} %get-tuple-element.24), channel_id=1, replica_groups=mesh['zl'=4,'x'=4,'y'=4,'core'=2,'rep'=4] {'zl','x','core'}, dimensions={0} | all-to-all | bytes 786432 | tf_op jit(solution)/shard_map/all_to_all | solution.py:285
  57.9 26.5 %all_to_all.21.parts_ref = bf16[16,16,128]{2,1,0:T(8,128)(2,1)S(1)} all-to-all(bf16[16,16,128]{2,1,0:T(8,128)(2,1)S(1)} %shard_map.124), channel_id=1, replica_groups=mesh['zl'=4,'x'=4,'y'=4,'core'=2,'rep'=4] {'y','rep'}, dimensions={0} | all-to-all | bytes 131072 | tf_op jit(solution)/shard_map/all_to_all | solution.py:285
  84.4 0.7 shard_map.125
  85.1 5.0 %all-to-all-start.3 = ((bf16[32,16,128]{2,1,0:T(8,128)(2,1)}), bf16[32,16,128]{2,1,0:T(8,128)(2,1)S(1)}, u32[]{:S(2)}, u32[]{:S(2)}) async-start(bf16[32,16,128]{2,1,0:T(8,128)(2,1)} %shard_map.125), calls=%async_computation.3 | async-start | bytes 262144 | tf_op jit(solution)/shard_map/all_to_all | solution.py:285
  90.1 2.1 %collective-permute-start.1 = (bf16[32,128]{1,0:T(8,128)(2,1)S(1)}, bf16[32,128]{1,0:T(8,128)(2,1)S(1)}, u32[]{:S(2)}, u32[]{:S(2)}) collective-permute-start(bf16[32,128]{1,0:T(8,128)(2,1)S(1)} %get-tuple-element.23), channel_id=1, source_target_pairs={{4,8},{8,4},{12,16},{16,12},{20,24},{24,20},{28,32},{32,28},{36,40... | collective-permute-start | bytes 24584 | tf_op jit(solution)/shard_map/ppermute | solution.py:281
  92.2 3.2 %collective-permute-done.1.next_ref = bf16[32,128]{1,0:T(8,128)(2,1)S(1)} collective-permute-done((bf16[32,128]{1,0:T(8,128)(2,1)S(1)}, bf16[32,128]{1,0:T(8,128)(2,1)S(1)}, u32[]{:S(2)}, u32[]{:S(2)}) %collective-permute-start.1) | collective-permute-done | bytes 8224 | tf_op jit(solution)/shard_map/ppermute | solution.py:281
  95.4 3.3 %all-to-all-done.3.sums_ref = bf16[32,16,128]{2,1,0:T(8,128)(2,1)S(1)} async-done(((bf16[32,16,128]{2,1,0:T(8,128)(2,1)}), bf16[32,16,128]{2,1,0:T(8,128)(2,1)S(1)}, u32[]{:S(2)}, u32[]{:S(2)}) %all-to-all-start.3) | async-done | bytes 131104 | tf_op jit(solution)/shard_map/all_to_all | solution.py:285
  98.6 0.0 copy-done.5
  98.6 0.0 copy-done.8
  98.6 0.9 shard_map.126
  (10 shorter events, 0.1 us)
Async XLA Ops:
  2.5 22.1 %all-to-all-start = ((bf16[32,32,128]{2,1,0:T(8,128)(2,1)}), bf16[32,32,128]{2,1,0:T(8,128)(2,1)S(1)}, u32[]{:S(2)}, u32[]{:S(2)}) async-start(bf16[32,32,128]{2,1,0:T(8,128)(2,1)} %get-tuple-element.16), calls=%async_computation | async-start | bytes 524288 | tf_op jit(solution)/shard_map/all_to_all | solution.py:285
  12.9 11.7 %collective-permute-start = (bf16[32,128]{1,0:T(8,128)(2,1)}, bf16[32,128]{1,0:T(8,128)(2,1)S(1)}, u32[]{:S(2)}, u32[]{:S(2)}) collective-permute-start(bf16[32,128]{1,0:T(8,128)(2,1)} %get-tuple-element.15), channel_id=1, source_target_pairs={{4,8},{8,4},{12,16},{16,12},{20,24},{24,20},{28,32},{32,28},{36,40... | collective-permute-start | bytes 24584 | tf_op jit(solution)/shard_map/ppermute | solution.py:281
  15.9 0.8 copy-start.9
  16.7 0.7 copy-start.10
  17.4 0.7 copy-start.11
  18.1 0.7 copy-start.12
  18.8 5.8 %copy-start.4 = (bf16[384,128]{1,0:T(8,128)(2,1)S(1)}, bf16[384,128]{1,0:T(8,128)(2,1)}, u32[]{:S(2)}) copy-start(bf16[384,128]{1,0:T(8,128)(2,1)} %wmix_ref.1) | copy-start | bytes 294916
  18.8 5.8 %copy-start.6 = (bf16[1,64,128]{2,1,0:T(8,128)(2,1)S(1)}, bf16[1,64,128]{2,1,0:T(8,128)(2,1)}, u32[]{:S(2)}) copy-start(bf16[1,64,128]{2,1,0:T(8,128)(2,1)} %cot_ref.1) | copy-start | bytes 49156
  18.8 5.8 %copy-start.7 = (bf16[64,128]{1,0:T(8,128)(2,1)S(1)}, bf16[64,128]{1,0:T(8,128)(2,1)}, u32[]{:S(2)}) copy-start(bf16[64,128]{1,0:T(8,128)(2,1)} %get-tuple-element.14.own_ref) | copy-start | bytes 49156
  21.1 2.1 %copy-start = (bf16[576,4096]{1,0:T(8,128)(2,1)}, bf16[576,4096]{1,0:T(8,128)(2,1)S(1)}, u32[]{:S(2)}) copy-start(bf16[576,4096]{1,0:T(8,128)(2,1)S(1)} %get-tuple-element.18.harm_ref) | copy-start | bytes 14155780
  23.2 1.4 %copy-start.2 = (f32[128,4096]{1,0:T(8,128)}, f32[128,4096]{1,0:T(8,128)S(1)}, u32[]{:S(2)}) copy-start(f32[128,4096]{1,0:T(8,128)S(1)} %get-tuple-element.19.radial_ref) | copy-start | bytes 6291460
  24.6 2.3 %copy-start.1 = (bf16[576,4096]{1,0:T(8,128)(2,1)S(1)}, bf16[576,4096]{1,0:T(8,128)(2,1)}, u32[]{:S(2)}) copy-start(bf16[576,4096]{1,0:T(8,128)(2,1)} %copy-done) | copy-start | bytes 14155780
  27.0 1.6 %copy-start.3 = (f32[128,4096]{1,0:T(8,128)S(1)}, f32[128,4096]{1,0:T(8,128)}, u32[]{:S(2)}) copy-start(f32[128,4096]{1,0:T(8,128)} %copy-done.2) | copy-start | bytes 6291460
  28.6 70.1 %copy-start.5 = (f32[64,128]{1,0:T(8,128)S(1)}, f32[64,128]{1,0:T(8,128)}, u32[]{:S(2)}) copy-start(f32[64,128]{1,0:T(8,128)} %get-tuple-element.22.gain_ref) | copy-start | bytes 98308
  28.6 70.1 %copy-start.8 = (s32[1,6,24]{2,0,1:T(1,128)S(1)}, s32[1,6,24]{2,0,1:T(1,128)}, u32[]{:S(2)}) copy-start(s32[1,6,24]{2,0,1:T(1,128)} %param.13) | copy-start | bytes 1732
  85.1 13.5 %all-to-all-start.3 = ((bf16[32,16,128]{2,1,0:T(8,128)(2,1)}), bf16[32,16,128]{2,1,0:T(8,128)(2,1)S(1)}, u32[]{:S(2)}, u32[]{:S(2)}) async-start(bf16[32,16,128]{2,1,0:T(8,128)(2,1)} %shard_map.125), calls=%async_computation.3 | async-start | bytes 262144 | tf_op jit(solution)/shard_map/all_to_all | solution.py:285
  90.1 5.3 %collective-permute-start.1 = (bf16[32,128]{1,0:T(8,128)(2,1)S(1)}, bf16[32,128]{1,0:T(8,128)(2,1)S(1)}, u32[]{:S(2)}, u32[]{:S(2)}) collective-permute-start(bf16[32,128]{1,0:T(8,128)(2,1)S(1)} %get-tuple-element.23), channel_id=1, source_target_pairs={{4,8},{8,4},{12,16},{16,12},{20,24},{24,20},{28,32},{32,28},{36,40... | collective-permute-start | bytes 24584 | tf_op jit(solution)/shard_map/ppermute | solution.py:281

commit v4 on v3

--- a/solution.py
+++ b/solution.py
@@ -24,8 +24,10 @@
 RING = 16
 PLANE = ("zl", "x", "core")
 PEERS = 32
-REST = ("y", "rep")
-OTHERS = 16
+SLAB = ("x", "y", "core")
+LINE = ("zl", "rep")
+LINES = 16
+MOVES = (-1, 1, -8, 8)
 DOM = ("zl", "x", "y", "core")
 STRIDES = (1, -1, 4, -4)
 HIGH = lax.Precision.HIGHEST
@@ -41,7 +43,7 @@
     return lax.broadcasted_iota(jnp.int32, shape, 0)
 
 
-def call(kernel, outs, *args, scratch=(), cost=None, space=pltpu.VMEM, limit=32):
+def call(kernel, outs, *args, scratch=(), cost=None, space=pltpu.VMEM, limit=48):
     return pl.pallas_call(
         kernel,
         out_shape=outs,
@@ -100,32 +102,7 @@
         pick_ref[peer(ring, stride, core)] = block.astype(bf16)
 
 
-def prep_kernel(
-    vec_ref, src_ref, dst_ref, wrad_ref, hot_ref, harm_ref, radial_ref, basis_ref, harm_s, basis_s
-):
-    geometry(vec_ref, harm_s, basis_s)
-    w_top, w_low = split(wrad_ref[...])
-    wrad = jnp.concatenate([w_top, w_low, w_top], axis=0).T.astype(bf16)
-    for start in range(0, EDGES, CHUNK):
-        at = pl.ds(start, CHUNK)
-        src = src_ref[:, at]
-        shift = jnp.zeros_like(src)
-        for face in range(1, FACES):
-            shift = shift + jnp.where(src >= ATOMS + face * GHOST, PAD - GHOST, 0)
-        hot = jnp.where(rows_iota((ROWS, CHUNK)) == src + shift, 1.0, 0.0)
-        hot_ref[:, at] = hot.astype(bf16)
-        b_top, b_low = split(basis_s[:, at])
-        basis = jnp.concatenate([b_top, b_top, b_low], axis=0).astype(bf16)
-        radial_ref[:, at] = dot(wrad, basis, ((1,), (0,)))
-        basis_ref[:, at] = jnp.concatenate([b_top, b_low], axis=0).astype(bf16)
-        own_hot = rows_iota((ATOMS, CHUNK)) == dst_ref[:, at]
-        harm_ref[0:ATOMS, at] = jnp.where(own_hot, 1.0, 0.0).astype(bf16)
-        for k in range(1, 9):
-            harm = harm_s[k : k + 1, at]
-            harm_ref[k * ATOMS : (k + 1) * ATOMS, at] = jnp.where(own_hot, harm, 0.0).astype(bf16)
-
-
-def geometry(vec_ref, harm_ref, basis_ref):
+def geo_kernel(vec_ref, harm_ref, basis_ref):
     vx, vy, vz = (vec_ref[i] for i in range(3))
     square = vx * vx + vy * vy + vz * vz + 0.25
     inv_r = lax.rsqrt(square)
@@ -173,9 +150,9 @@
 
 
 def main_kernel(
-    own_ref, next_ref, got_ref, hot_ref, harm_ref, radial_ref, basis_ref, wmix_ref, cot_ref,
-    dext_ref, back_ref, send_ref,
-    source_s, mom_s, dmom_s,
+    own_ref, next_ref, got_ref, src_ref, dst_ref, harm_ref, basis_ref, wrad_ref, wmix_ref, cot_ref,
+    dext_ref, line_ref, send_ref,
+    hot_s, harm_s, radial_s, source_s, mom_s, dmom_s,
 ):
     ring, core = position()
     near = got_ref[peer(ring, 0, 1 - core)].astype(f32)
@@ -185,13 +162,30 @@
     for stride in STRIDES:
         blocks.append(got_ref[peer(ring, -stride, core)].astype(f32))
     ext = jnp.concatenate(blocks, axis=0).T.astype(bf16)
+    w_top, w_low = split(wrad_ref[...])
+    wrad = jnp.concatenate([w_top, w_low, w_top], axis=0).T.astype(bf16)
     mom_s[...] = jnp.zeros_like(mom_s)
     for start in range(0, EDGES, CHUNK):
         at = pl.ds(start, CHUNK)
-        source = dot(ext, hot_ref[:, at], ((1,), (0,)))
+        src = src_ref[:, at]
+        shift = jnp.zeros_like(src)
+        for face in range(1, FACES):
+            shift = shift + jnp.where(src >= ATOMS + face * GHOST, PAD - GHOST, 0)
+        hot = jnp.where(rows_iota((ROWS, CHUNK)) == src + shift, 1.0, 0.0).astype(bf16)
+        hot_s[:, at] = hot
+        source = dot(ext, hot, ((1,), (0,)))
         source_s[:, at] = source.astype(bf16)
-        message = (radial_ref[:, at] * source).astype(bf16)
-        mom_s[...] += dot(harm_ref[:, at], message, ((1,), (1,)))
+        b_top, b_low = split(basis_ref[:, at])
+        basis = jnp.concatenate([b_top, b_top, b_low], axis=0).astype(bf16)
+        radial = dot(wrad, basis, ((1,), (0,)))
+        radial_s[:, at] = radial
+        message = (radial * source).astype(bf16)
+        own_hot = rows_iota((ATOMS, CHUNK)) == dst_ref[:, at]
+        harm_s[0:ATOMS, at] = jnp.where(own_hot, 1.0, 0.0).astype(bf16)
+        for k in range(1, 9):
+            harm = harm_ref[k : k + 1, at]
+            harm_s[k * ATOMS : (k + 1) * ATOMS, at] = jnp.where(own_hot, harm, 0.0).astype(bf16)
+        mom_s[...] += dot(harm_s[:, at], message, ((1,), (1,)))
     moments = [msg_scale * mom_s[k * ATOMS : (k + 1) * ATOMS, :] for k in range(9)]
     squares = [m * m for m in moments]
     two = squares[4]
@@ -215,11 +209,13 @@
     gradr = jnp.zeros((2 * NB, CHANS), f32)
     for start in range(0, EDGES, CHUNK):
         at = pl.ds(start, CHUNK)
-        dmsg = dot(dmom_s[...], harm_ref[:, at], ((1,), (0,)))
+        dmsg = dot(dmom_s[...], harm_s[:, at], ((1,), (0,)))
         dradial = dmsg * source_s[:, at].astype(f32)
-        dsource = (dmsg * radial_ref[:, at]).astype(bf16)
-        dext = dext + dot(hot_ref[:, at], dsource, ((1,), (1,)))
-        gradr = gradr + dot(basis_ref[:, at], dradial.astype(bf16), ((1,), (1,)))
+        dsource = (dmsg * radial_s[:, at]).astype(bf16)
+        dext = dext + dot(hot_s[:, at], dsource, ((1,), (1,)))
+        b_top, b_low = split(basis_ref[:, at])
+        basis = jnp.concatenate([b_top, b_low], axis=0).astype(bf16)
+        gradr = gradr + dot(basis, dradial.astype(bf16), ((1,), (1,)))
     gradr = jnp.concatenate([gradr[:NB] + gradr[NB:], jnp.zeros((SHARD - NB, CHANS), f32)], axis=0)
     send_ref[3 * CHANS // SHARD, 0:SHARD] = gradr.astype(bf16)
     for i in range(3 * CHANS // SHARD + 1, PEERS):
@@ -228,14 +224,23 @@
         send_ref[i, SHARD:] = jnp.zeros((PAD, CHANS), bf16)
     dext_ref[...] = dext[:ATOMS]
     ghosts = [dext[ATOMS + face * PAD : ATOMS + (face + 1) * PAD] for face in range(FACES)]
-    back_ref[...] = jnp.where(core == 0, ghosts[0], ghosts[1]).astype(bf16)
-    near = jnp.where(core == 0, ghosts[1], ghosts[0])
-    send_ref[peer(ring, 0, 1 - core), SHARD:] = near.astype(bf16)
-    for stride, block in zip(STRIDES, ghosts[2:]):
-        send_ref[peer(ring, -stride, core), SHARD:] = block.astype(bf16)
-
-
-def total_kernel(parts_ref, out_ref):
+    spot = place()
+    for move, block in zip(MOVES, ghosts[:4]):
+        send_ref[lax.rem(spot + move + PEERS, PEERS), SHARD:] = block.astype(bf16)
+    line_ref[0] = ghosts[4].astype(bf16)
+    line_ref[1] = ghosts[5].astype(bf16)
+
+
+def place():
+    return (lax.axis_index("x") * 4 + lax.axis_index("y")) * 2 + lax.axis_index("core")
+
+
+def passed(got_ref):
+    spot = place()
+    return [got_ref[lax.rem(spot - move + PEERS, PEERS), SHARD:] for move in MOVES]
+
+
+def add_up(parts_ref, out_ref):
     total = parts_ref[0, :SHARD].astype(f32)
     for i in range(1, parts_ref.shape[0]):
         total = total + parts_ref[i, :SHARD].astype(f32)
@@ -244,15 +249,28 @@
         out_ref[i] = total
 
 
+def slab_kernel(parts_ref, line_ref, out_ref, down_ref, up_ref):
+    add_up(parts_ref, out_ref)
+    blocks = passed(parts_ref)
+    down_ref[0], up_ref[0] = line_ref[0], line_ref[1]
+    down_ref[1], up_ref[1] = blocks[0], blocks[1]
+    down_ref[2], up_ref[2] = blocks[2], blocks[3]
+
+
+def line_kernel(parts_ref, out_ref):
+    add_up(parts_ref, out_ref)
+
+
 def post_kernel(
-    dext_ref, gain_ref, sends_ref, next_ref, got_ref, sums_ref, dfeat_ref, gmix_ref, grad_ref
+    dext_ref, gain_ref, sends_ref, got_ref, down_ref, up_ref, sums_ref, dfeat_ref, gmix_ref, grad_ref
 ):
-    ring, core = position()
-    near = got_ref[peer(ring, 0, 1 - core), SHARD:].astype(f32)
-    other = next_ref[...].astype(f32)
-    blocks = [jnp.where(core == 0, near, other), jnp.where(core == 0, other, near)]
-    for stride in STRIDES:
-        blocks.append(got_ref[peer(ring, stride, core), SHARD:].astype(f32))
+    spot = place()
+    local = passed(got_ref)
+    blocks = []
+    for move, block, other in zip(MOVES, local, (down_ref[1], up_ref[1], down_ref[2], up_ref[2])):
+        crossed = spot - move >= PEERS if move < 0 else spot < move
+        blocks.append(jnp.where(crossed, other.astype(f32), block.astype(f32)))
+    blocks += [down_ref[0].astype(f32), up_ref[0].astype(f32)]
     total = dext_ref[...]
     for face in range(FACES):
         hot = (rows_iota((ATOMS, GHOST)) == sends_ref[face]).astype(f32)
@@ -309,42 +327,44 @@
     )
     near = swap(block)
     far = exchange(picks, PLANE)
-    edges = call(
-        prep_kernel,
-        [
-            shape((ROWS, EDGES), bf16),
-            shape((9 * ATOMS, EDGES), bf16),
-            shape((CHANS, EDGES), f32),
-            shape((2 * NB, EDGES), bf16),
-        ],
-        edge_vec.reshape(3, 1, EDGES), edge_src, edge_dst, w_rad,
-        scratch=[pltpu.VMEM((16, EDGES), f32), pltpu.VMEM((NB, EDGES), f32)],
-        cost=pl.CostEstimate(flops=2000000000, bytes_accessed=9000000, transcendentals=0),
-    )
-    dext, block, blocks = call(
+    harm, basis = call(
+        geo_kernel,
+        [shape((16, EDGES), f32), shape((NB, EDGES), f32)],
+        edge_vec.reshape(3, 1, EDGES),
+        cost=pl.CostEstimate(flops=1000000, bytes_accessed=400000, transcendentals=0),
+    )
+    dext, line, blocks = call(
         main_kernel,
         [
             shape((ATOMS, CHANS), f32),
-            shape((PAD, CHANS), bf16),
+            shape((2, PAD, CHANS), bf16),
             shape((PEERS, SHARD + PAD, CHANS), bf16),
         ],
-        own, near, far, *edges, w_mix, out_cot,
+        own, near, far, edge_src, edge_dst, harm, basis, w_rad, w_mix, out_cot,
         scratch=[
+            pltpu.VMEM((ROWS, EDGES), bf16),
+            pltpu.VMEM((9 * ATOMS, EDGES), bf16),
+            pltpu.VMEM((CHANS, EDGES), f32),
             pltpu.VMEM((CHANS, EDGES), bf16),
             pltpu.VMEM((9 * ATOMS, CHANS), f32),
             pltpu.VMEM((CHANS, 9 * ATOMS), bf16),
         ],
     )
-    near = swap(block)
-    far = exchange(blocks, PLANE)
-    (parts,) = call(total_kernel, [shape((OTHERS, SHARD, CHANS), bf16)], far)
-    parts = exchange(parts, REST)
-    (parts,) = call(total_kernel, [shape((PEERS, SHARD, CHANS), bf16)], parts)
-    sums = exchange(parts, PLANE)
+    far = exchange(blocks, SLAB)
+    parts, down, up = call(
+        slab_kernel,
+        [shape((LINES, SHARD, CHANS), bf16)] + [shape((3, PAD, CHANS), bf16)] * 2,
+        far, line,
+    )
+    down = lax.ppermute(down, "zl", [(i, (i + 3) % 4) for i in range(4)])
+    up = lax.ppermute(up, "zl", [(i, (i + 1) % 4) for i in range(4)])
+    parts = exchange(parts, LINE)
+    (parts,) = call(line_kernel, [shape((PEERS, SHARD, CHANS), bf16)], parts)
+    sums = exchange(parts, SLAB)
     d_feat, gmix, grad_r = call(
         post_kernel,
         [shape((1, ATOMS, CHANS), f32), shape((3 * CHANS, CHANS), f32), shape((NB, CHANS), f32)],
-        dext, gain, sends, near, far, sums,
+        dext, gain, sends, far, down, up, sums,
     )
     return d_feat, gmix, grad_r
 

time: 100 us -> 88.5 us (0.89)
  local copies, waits for them, and re-layouts: 10.3 us -> 0.06 us
  blocking collectives: 49.8 us -> 40.2 us
  waiting for transfers between devices: 6.45 us -> 12.5 us
  starting transfers between devices: 20.4 us -> 24.3 us
  Pallas kernels: 11.8 us -> 9.61 us
    unnamed x26 -> x20, local copies, waits for them, and re-layouts: 10.3 us -> 0.06 us
    all_to_all x2, blocking collectives: 49.8 us -> 40.2 us  [exchange(): return lax.all_to_all(blocks, axes, 0, 0, tiled=True)]
    ppermute x0 -> x2, starting transfers between devices: none -> 5.28 us  [the longest x1 3.29 us: on_device(): down = lax.ppermute(down, 'zl', [(i, (i + 3) % 4) for i in range(4)])]
    ppermute x0 -> x2, waiting for transfers between devices: none -> 4.36 us  [the longest x1 4.36 us: on_device(): up = lax.ppermute(up, 'zl', [(i, (i + 1) % 4) for i in range(4)])]
    all_to_all x2, waiting for transfers between devices: 3.28 us -> 5.94 us  [exchange(): return lax.all_to_all(blocks, axes, 0, 0, tiled=True)]
    pallas_call x6, Pallas kernels: 11.8 us -> 9.61 us  [call(): pl.pallas_call(kernel, out_shape=outs, in_specs=[pl.BlockSpec(memory_spac...]
    ppermute x2 -> x1, starting transfers between devices: 5.04 us -> 2.95 us  [swap(): return lax.ppermute(block, DOM, pairs)]
    ppermute x2 -> x1, waiting for transfers between devices: 3.16 us -> 2.17 us  [swap(): return lax.ppermute(block, DOM, pairs)]
  transfers between devices with their start and end apart: 4 -> 5, of which waited for: 2 -> 3; matrix products, arithmetic and copies ran while one was open for 0% -> 0% of each run, Pallas kernels for 2% -> 0%
where the time goes in v4:
time: 88.5 us; the launch traced here: 87.4 us
  blocking collectives  40.2 us (45%)
  starting transfers between devices  24.3 us (27%)
  waiting for transfers between devices  12.5 us (14%)
  Pallas kernels  9.61 us (11%)
    all_to_all x2, blocking collectives, exchange(): return lax.all_to_all(blocks, axes, 0, 0, tiled=True)  40.2 us
    all_to_all x2, starting transfers between devices, exchange(): return lax.all_to_all(blocks, axes, 0, 0, tiled=True)  16.1 us
    pallas_call x6, Pallas kernels, call(): pl.pallas_call(kernel, out_shape=outs, in_specs=[pl.BlockSpec(memory_spac...  9.61 us
    all_to_all x2, waiting for transfers between devices, exchange(): return lax.all_to_all(blocks, axes, 0, 0, tiled=True)  5.94 us
    ppermute x1, waiting for transfers between devices, on_device(): up = lax.ppermute(up, 'zl', [(i, (i + 1) % 4) for i in range(4)])  4.36 us
    ppermute x1, starting transfers between devices, on_device(): down = lax.ppermute(down, 'zl', [(i, (i + 3) % 4) for i in range(4)])  3.29 us
    ppermute x1, starting transfers between devices, swap(): return lax.ppermute(block, DOM, pairs)  2.95 us
    ppermute x1, waiting for transfers between devices, swap(): return lax.ppermute(block, DOM, pairs)  2.17 us
  transfers between devices with their start and end apart: 5, of which 3 were waited for; matrix products, arithmetic and copies ran while one was open for 0% of the time, Pallas kernels for 0%

profile of v4, /device:TPU:1, one launch (start us, length us, event | category | flops | bytes accessed | tf_op | source)
XLA Modules:
  0.0 87.4 jit_solution(2254065155764448507)
XLA Ops:
  0.6 1.9 %shard_map.121 = (bf16[64,128]{1,0:T(8,128)(2,1)}, f32[64,128]{1,0:T(8,128)}, bf16[32,128]{1,0:T(8,128)(2,1)}, bf16[32,32,128]{2,1,0:T(8,128)(2,1)}) custom-call(bf16[1,64,128]{2,1,0:T(8,128)(2,1)} %feat_hbm.1, s32[1,64]{1,0:T(1,128)} %species_hbm.1, f32[5,128]{1,0:T(8,128)} %gain_hbm.1, s32[6,1,24]{2,1,0:T(1,128)} %bitcast.3), custom_call_target="tpu_custom_call" | custom-call | tf_op jit(solution)/shard_map/pallas_call | solution.py:47
  2.5 0.0 copy-start.9
  2.5 0.0 copy-start.1
  2.5 0.0 copy-start
  2.5 0.0 copy-start.6
  2.6 10.5 %all-to-all-start = ((bf16[32,32,128]{2,1,0:T(8,128)(2,1)}), bf16[32,32,128]{2,1,0:T(8,128)(2,1)S(1)}, u32[]{:S(2)}, u32[]{:S(2)}) async-start(bf16[32,32,128]{2,1,0:T(8,128)(2,1)} %get-tuple-element.17), calls=%async_computation | async-start | bytes 524288 | tf_op jit(solution)/shard_map/all_to_all | solution.py:303
  13.1 0.0 copy-done.9
  13.1 2.9 %collective-permute-start = (bf16[32,128]{1,0:T(8,128)(2,1)S(1)}, bf16[32,128]{1,0:T(8,128)(2,1)S(1)}, u32[]{:S(2)}, u32[]{:S(2)}) collective-permute-start(bf16[32,128]{1,0:T(8,128)(2,1)S(1)} %copy-done.9), channel_id=1, source_target_pairs={{4,8},{8,4},{12,16},{16,12},{20,24},{24,20},{28,32},{32,28},{36,40... | collective-permute-start | bytes 24584 | tf_op jit(solution)/shard_map/ppermute | solution.py:299
  16.1 0.0 copy-done.1
  16.1 0.0 copy-start.3
  16.1 0.0 copy-start.4
  16.1 0.0 copy-start.5
  16.1 0.1 shard_map.122
  16.2 0.0 copy-start.8
  16.2 2.2 %collective-permute-done.next_ref = bf16[32,128]{1,0:T(8,128)(2,1)S(1)} collective-permute-done((bf16[32,128]{1,0:T(8,128)(2,1)S(1)}, bf16[32,128]{1,0:T(8,128)(2,1)S(1)}, u32[]{:S(2)}, u32[]{:S(2)}) %collective-permute-start) | collective-permute-done | bytes 8224 | tf_op jit(solution)/shard_map/ppermute | solution.py:299
  18.4 5.9 %all-to-all-done.got_ref = bf16[32,32,128]{2,1,0:T(8,128)(2,1)S(1)} async-done(((bf16[32,32,128]{2,1,0:T(8,128)(2,1)}), bf16[32,32,128]{2,1,0:T(8,128)(2,1)S(1)}, u32[]{:S(2)}, u32[]{:S(2)}) %all-to-all-start) | async-done | bytes 262176 | tf_op jit(solution)/shard_map/all_to_all | solution.py:303
  24.3 0.0 copy-done
  24.3 0.0 copy-done.6
  24.3 0.0 copy-done.3
  24.4 6.0 %shard_map.123 = (f32[64,128]{1,0:T(8,128)S(1)}, bf16[2,32,128]{2,1,0:T(8,128)(2,1)S(1)}, bf16[32,48,128]{2,1,0:T(8,128)(2,1)S(1)}) custom-call(bf16[64,128]{1,0:T(8,128)(2,1)S(1)} %copy-done.6, bf16[32,128]{1,0:T(8,128)(2,1)S(1)} %collective-permute-done.next_ref, bf16[32,32,128]{2,1,0:T(8,128)(2,1)S(1)} %all-to-all-done.got_ref, s32[1,4096]{1,0:T(1,128)S(1)} %copy-done.3, ...), custom_call_target="tpu_custom_call" | custom-call | tf_op jit(solution)/shard_map/pallas_call | solution.py:47
  30.4 15.2 %all_to_all.20.parts_ref.got_ref = bf16[32,48,128]{2,1,0:T(8,128)(2,1)S(1)} all-to-all(bf16[32,48,128]{2,1,0:T(8,128)(2,1)S(1)} %get-tuple-element.22), channel_id=1, replica_groups=mesh['zl'=4,'x'=4,'y'=4,'core'=2,'rep'=4] {'x','y','core'}, dimensions={0} | all-to-all | bytes 786432 | tf_op jit(solution)/shard_map/all_to_all | solution.py:303
  45.6 25.0 %all_to_all.21.parts_ref = bf16[16,16,128]{2,1,0:T(8,128)(2,1)S(1)} all-to-all(bf16[16,16,128]{2,1,0:T(8,128)(2,1)S(1)} %get-tuple-element.26), channel_id=1, replica_groups=mesh['zl'=4,'x'=4,'y'=4,'core'=2,'rep'=4] {'zl','rep'}, dimensions={0} | all-to-all | bytes 131072 | tf_op jit(solution)/shard_map/all_to_all | solution.py:303
  70.6 0.7 shard_map.125
  71.3 5.5 %all-to-all-start.3 = ((bf16[32,16,128]{2,1,0:T(8,128)(2,1)}), bf16[32,16,128]{2,1,0:T(8,128)(2,1)S(1)}, u32[]{:S(2)}, u32[]{:S(2)}) async-start(bf16[32,16,128]{2,1,0:T(8,128)(2,1)} %shard_map.125), calls=%async_computation.3 | async-start | bytes 262144 | tf_op jit(solution)/shard_map/all_to_all | solution.py:303
  76.8 0.0 copy-start.7
  76.8 3.3 %collective-permute-start.1 = (bf16[3,32,128]{2,1,0:T(8,128)(2,1)S(1)}, bf16[3,32,128]{2,1,0:T(8,128)(2,1)S(1)}, u32[]{:S(2)}, u32[]{:S(2)}) collective-permute-start(bf16[3,32,128]{2,1,0:T(8,128)(2,1)S(1)} %get-tuple-element.24), channel_id=1, source_target_pairs={{0,384},{128,0},{256,128},{384,256},{1,385},{129,1},{257,129},{385... | collective-permute-start | bytes 73736 | tf_op jit(solution)/shard_map/ppermute | solution.py:359
  80.1 2.0 %collective-permute-start.2 = (bf16[3,32,128]{2,1,0:T(8,128)(2,1)S(1)}, bf16[3,32,128]{2,1,0:T(8,128)(2,1)S(1)}, u32[]{:S(2)}, u32[]{:S(2)}) collective-permute-start(bf16[3,32,128]{2,1,0:T(8,128)(2,1)S(1)} %get-tuple-element.25), channel_id=1, source_target_pairs={{0,128},{128,256},{256,384},{384,0},{1,129},{129,257},{257,385},{3... | collective-permute-start | bytes 73736 | tf_op jit(solution)/shard_map/ppermute | solution.py:360
  82.1 0.0 collective-permute-done.1.down_ref
  82.2 4.4 %collective-permute-done.2.up_ref = bf16[3,32,128]{2,1,0:T(8,128)(2,1)S(1)} collective-permute-done((bf16[3,32,128]{2,1,0:T(8,128)(2,1)S(1)}, bf16[3,32,128]{2,1,0:T(8,128)(2,1)S(1)}, u32[]{:S(2)}, u32[]{:S(2)}) %collective-permute-start.2) | collective-permute-done | bytes 24608 | tf_op jit(solution)/shard_map/ppermute | solution.py:360
  86.5 0.0 all-to-all-done.3.sums_ref
  86.5 0.0 copy-done.7
  86.5 0.9 %shard_map.126 = (f32[1,64,128]{2,1,0:T(8,128)}, f32[384,128]{1,0:T(8,128)}, f32[8,128]{1,0:T(8,128)}) custom-call(f32[64,128]{1,0:T(8,128)S(1)} %get-tuple-element.20.dext_ref, f32[64,128]{1,0:T(8,128)S(1)} %copy-done.2, s32[6,1,24]{2,1,0:T(1,128)S(1)} %bitcast.4, bf16[32,48,128]{2,1,0:T(8,128)(2,1)S(1)} %all_to_all.20.parts_ref.got_ref, ...), custom_call_target="tpu_custom_call" | custom-call | tf_op jit(solution)/shard_map/pallas_call | solution.py:47
  (6 shorter events, 0.1 us)
Async XLA Ops:
  2.5 10.6 %copy-start.9 = (bf16[32,128]{1,0:T(8,128)(2,1)S(1)}, bf16[32,128]{1,0:T(8,128)(2,1)}, u32[]{:S(2)}) copy-start(bf16[32,128]{1,0:T(8,128)(2,1)} %get-tuple-element.16) | copy-start | bytes 24580
  2.5 13.6 %copy-start.1 = (f32[1,3,4096]{2,0,1:T(1,128)S(1)}, f32[1,3,4096]{2,0,1:T(1,128)}, u32[]{:S(2)}) copy-start(f32[1,3,4096]{2,0,1:T(1,128)} %param.16) | copy-start | bytes 147460
  2.5 21.8 %copy-start = (bf16[384,128]{1,0:T(8,128)(2,1)S(1)}, bf16[384,128]{1,0:T(8,128)(2,1)}, u32[]{:S(2)}) copy-start(bf16[384,128]{1,0:T(8,128)(2,1)} %wmix_ref.1) | copy-start | bytes 294916
  2.5 21.8 %copy-start.6 = (bf16[64,128]{1,0:T(8,128)(2,1)S(1)}, bf16[64,128]{1,0:T(8,128)(2,1)}, u32[]{:S(2)}) copy-start(bf16[64,128]{1,0:T(8,128)(2,1)} %get-tuple-element.15.own_ref) | copy-start | bytes 49156
  2.6 21.8 %all-to-all-start = ((bf16[32,32,128]{2,1,0:T(8,128)(2,1)}), bf16[32,32,128]{2,1,0:T(8,128)(2,1)S(1)}, u32[]{:S(2)}, u32[]{:S(2)}) async-start(bf16[32,32,128]{2,1,0:T(8,128)(2,1)} %get-tuple-element.17), calls=%async_computation | async-start | bytes 524288 | tf_op jit(solution)/shard_map/all_to_all | solution.py:303
  13.1 5.3 %collective-permute-start = (bf16[32,128]{1,0:T(8,128)(2,1)S(1)}, bf16[32,128]{1,0:T(8,128)(2,1)S(1)}, u32[]{:S(2)}, u32[]{:S(2)}) collective-permute-start(bf16[32,128]{1,0:T(8,128)(2,1)S(1)} %copy-done.9), channel_id=1, source_target_pairs={{4,8},{8,4},{12,16},{16,12},{20,24},{24,20},{28,32},{32,28},{36,40... | collective-permute-start | bytes 24584 | tf_op jit(solution)/shard_map/ppermute | solution.py:299
  16.1 8.2 %copy-start.3 = (s32[1,4096]{1,0:T(1,128)S(1)}, s32[1,4096]{1,0:T(1,128)}, u32[]{:S(2)}) copy-start(s32[1,4096]{1,0:T(1,128)} %src_ref.1) | copy-start | bytes 49156
  16.1 8.2 %copy-start.4 = (s32[1,4096]{1,0:T(1,128)S(1)}, s32[1,4096]{1,0:T(1,128)}, u32[]{:S(2)}) copy-start(s32[1,4096]{1,0:T(1,128)} %dst_ref.1) | copy-start | bytes 49156
  16.1 8.2 %copy-start.5 = (bf16[1,64,128]{2,1,0:T(8,128)(2,1)S(1)}, bf16[1,64,128]{2,1,0:T(8,128)(2,1)}, u32[]{:S(2)}) copy-start(bf16[1,64,128]{2,1,0:T(8,128)(2,1)} %cot_ref.1) | copy-start | bytes 49156
  16.2 8.2 %copy-start.8 = (f32[8,128]{1,0:T(8,128)S(1)}, f32[8,128]{1,0:T(8,128)}, u32[]{:S(2)}) copy-start(f32[8,128]{1,0:T(8,128)} %wrad_ref.1) | copy-start | bytes 12292
  71.3 15.2 %copy-start.2 = (f32[64,128]{1,0:T(8,128)S(1)}, f32[64,128]{1,0:T(8,128)}, u32[]{:S(2)}) copy-start(f32[64,128]{1,0:T(8,128)} %get-tuple-element.21.gain_ref) | copy-start | bytes 98308
  71.3 15.2 %all-to-all-start.3 = ((bf16[32,16,128]{2,1,0:T(8,128)(2,1)}), bf16[32,16,128]{2,1,0:T(8,128)(2,1)S(1)}, u32[]{:S(2)}, u32[]{:S(2)}) async-start(bf16[32,16,128]{2,1,0:T(8,128)(2,1)} %shard_map.125), calls=%async_computation.3 | async-start | bytes 262144 | tf_op jit(solution)/shard_map/all_to_all | solution.py:303
  76.8 9.7 %copy-start.7 = (s32[1,6,24]{2,0,1:T(1,128)S(1)}, s32[1,6,24]{2,0,1:T(1,128)}, u32[]{:S(2)}) copy-start(s32[1,6,24]{2,0,1:T(1,128)} %param.13) | copy-start | bytes 1732
  76.8 5.3 %collective-permute-start.1 = (bf16[3,32,128]{2,1,0:T(8,128)(2,1)S(1)}, bf16[3,32,128]{2,1,0:T(8,128)(2,1)S(1)}, u32[]{:S(2)}, u32[]{:S(2)}) collective-permute-start(bf16[3,32,128]{2,1,0:T(8,128)(2,1)S(1)} %get-tuple-element.24), channel_id=1, source_target_pairs={{0,384},{128,0},{256,128},{384,256},{1,385},{129,1},{257,129},{385... | collective-permute-start | bytes 73736 | tf_op jit(solution)/shard_map/ppermute | solution.py:359
  80.1 6.4 %collective-permute-start.2 = (bf16[3,32,128]{2,1,0:T(8,128)(2,1)S(1)}, bf16[3,32,128]{2,1,0:T(8,128)(2,1)S(1)}, u32[]{:S(2)}, u32[]{:S(2)}) collective-permute-start(bf16[3,32,128]{2,1,0:T(8,128)(2,1)S(1)} %get-tuple-element.25), channel_id=1, source_target_pairs={{0,128},{128,256},{256,384},{384,0},{1,129},{129,257},{257,385},{3... | collective-permute-start | bytes 73736 | tf_op jit(solution)/shard_map/ppermute | solution.py:360

commit v5 on v4

--- a/solution.py
+++ b/solution.py
@@ -15,14 +15,13 @@
 NB = 8
 ATOMS = 64
 FACES = 6
-PAD = 32
 GHOST = 24
-ROWS = ATOMS + FACES * PAD
+ROWS = ATOMS + FACES * GHOST
 EDGES = 4096
 CHUNK = 1024
 SHARD = 16
 RING = 16
-PLANE = ("zl", "x", "core")
+PLANE = ("zl", "x")
 PEERS = 32
 SLAB = ("x", "y", "core")
 LINE = ("zl", "rep")
@@ -60,12 +59,12 @@
     return ring, lax.axis_index("core")
 
 
-def peer(ring, stride, core):
-    return lax.rem(ring + stride + RING, RING) * 2 + core
+def peer(ring, stride):
+    return lax.rem(ring + stride + RING, RING)
 
 
 def pre_kernel(
-    feat_hbm, species_hbm, gain_hbm, sends_hbm, own_ref, gain_out, next_ref, pick_ref,
+    feat_hbm, species_hbm, gain_hbm, sends_hbm, own_ref, gain_out, pair_ref, pick_ref,
     feat_ref, species_ref, gain_ref, sends_ref, sems,
 ):
     copies = [
@@ -91,15 +90,13 @@
     own_ref[...] = own
     gain_out[...] = gain
     ring, core = position()
-    picked = []
     for face in range(FACES):
         hot = (rows_iota((ATOMS, GHOST)) == sends_ref[face]).astype(f32)
-        hot = jnp.concatenate([hot, jnp.zeros((ATOMS, PAD - GHOST), f32)], axis=1)
-        picked.append(dot(hot.astype(bf16), own, ((0,), (0,))))
-    next_ref[...] = jnp.where(core == 0, picked[1], picked[0]).astype(bf16)
-    pick_ref[peer(ring, 0, 1 - core)] = jnp.where(core == 0, picked[0], picked[1]).astype(bf16)
-    for stride, block in zip(STRIDES, picked[2:]):
-        pick_ref[peer(ring, stride, core)] = block.astype(bf16)
+        picked = dot(hot.astype(bf16), own, ((0,), (0,))).astype(bf16)
+        if face < 2:
+            pair_ref[lax.rem(core + face, 2)] = picked
+        else:
+            pick_ref[peer(ring, STRIDES[face - 2])] = picked
 
 
 def geo_kernel(vec_ref, harm_ref, basis_ref):
@@ -150,17 +147,15 @@
 
 
 def main_kernel(
-    own_ref, next_ref, got_ref, src_ref, dst_ref, harm_ref, basis_ref, wrad_ref, wmix_ref, cot_ref,
+    own_ref, p0, p1, got_ref, src_ref, dst_ref, harm_ref, basis_ref, wrad_ref, wmix_ref, cot_ref,
     dext_ref, line_ref, send_ref,
     hot_s, harm_s, radial_s, source_s, mom_s, dmom_s,
 ):
     ring, core = position()
-    near = got_ref[peer(ring, 0, 1 - core)].astype(f32)
-    other = next_ref[...].astype(f32)
-    blocks = [own_ref[...].astype(f32)]
-    blocks += [jnp.where(core == 0, other, near), jnp.where(core == 0, near, other)]
+    a, b = p0[...].astype(f32), p1[...].astype(f32)
+    blocks = [own_ref[...].astype(f32), jnp.where(core == 0, b, a), jnp.where(core == 0, a, b)]
     for stride in STRIDES:
-        blocks.append(got_ref[peer(ring, -stride, core)].astype(f32))
+        blocks.append(got_ref[peer(ring, -stride)].astype(f32))
     ext = jnp.concatenate(blocks, axis=0).T.astype(bf16)
     w_top, w_low = split(wrad_ref[...])
     wrad = jnp.concatenate([w_top, w_low, w_top], axis=0).T.astype(bf16)
@@ -168,10 +163,7 @@
     for start in range(0, EDGES, CHUNK):
         at = pl.ds(start, CHUNK)
         src = src_ref[:, at]
-        shift = jnp.zeros_like(src)
-        for face in range(1, FACES):
-            shift = shift + jnp.where(src >= ATOMS + face * GHOST, PAD - GHOST, 0)
-        hot = jnp.where(rows_iota((ROWS, CHUNK)) == src + shift, 1.0, 0.0).astype(bf16)
+        hot = jnp.where(rows_iota((ROWS, CHUNK)) == src, 1.0, 0.0).astype(bf16)
         hot_s[:, at] = hot
         source = dot(ext, hot, ((1,), (0,)))
         source_s[:, at] = source.astype(bf16)
@@ -196,9 +188,11 @@
     sigma = jax.nn.sigmoid(pre)
     slope = sigma * (1.0 + pre * (1.0 - sigma))
     dpre = (cot_ref[0].astype(f32) * slope).astype(bf16)
-    gmix = dot(inv, dpre, ((0,), (0,))).astype(bf16)
+    gmix = dot(inv, dpre, ((0,), (0,)))
+    nothing = jnp.zeros((GHOST, CHANS), f32)
     for i in range(3 * CHANS // SHARD):
-        send_ref[i, 0:SHARD] = gmix[i * SHARD : (i + 1) * SHARD]
+        shard = gmix[i * SHARD : (i + 1) * SHARD]
+        send_ref[i] = jnp.concatenate([shard, nothing], axis=0).astype(bf16)
     dinv = dot(dpre, wmix_ref[...], ((1,), (1,)))
     groups = [0, 1, 1, 1, 2, 2, 2, 2, 2]
     for k in range(9):
@@ -216,17 +210,17 @@
         b_top, b_low = split(basis_ref[:, at])
         basis = jnp.concatenate([b_top, b_low], axis=0).astype(bf16)
         gradr = gradr + dot(basis, dradial.astype(bf16), ((1,), (1,)))
-    gradr = jnp.concatenate([gradr[:NB] + gradr[NB:], jnp.zeros((SHARD - NB, CHANS), f32)], axis=0)
-    send_ref[3 * CHANS // SHARD, 0:SHARD] = gradr.astype(bf16)
+    gradr = jnp.concatenate([gradr[:NB] + gradr[NB:], nothing, nothing[:NB]], axis=0)
+    send_ref[3 * CHANS // SHARD] = gradr.astype(bf16)
     for i in range(3 * CHANS // SHARD + 1, PEERS):
-        send_ref[i, 0:SHARD] = jnp.zeros((SHARD, CHANS), bf16)
-    for i in range(PEERS):
-        send_ref[i, SHARD:] = jnp.zeros((PAD, CHANS), bf16)
+        send_ref[i] = jnp.zeros((SHARD + GHOST, CHANS), bf16)
     dext_ref[...] = dext[:ATOMS]
-    ghosts = [dext[ATOMS + face * PAD : ATOMS + (face + 1) * PAD] for face in range(FACES)]
+    ghosts = [dext[ATOMS + face * GHOST : ATOMS + (face + 1) * GHOST] for face in range(FACES)]
     spot = place()
     for move, block in zip(MOVES, ghosts[:4]):
-        send_ref[lax.rem(spot + move + PEERS, PEERS), SHARD:] = block.astype(bf16)
+        to = lax.rem(spot + move + PEERS, PEERS)
+        shard = send_ref[to].astype(f32)[:SHARD]
+        send_ref[to] = jnp.concatenate([shard, block], axis=0).astype(bf16)
     line_ref[0] = ghosts[4].astype(bf16)
     line_ref[1] = ghosts[5].astype(bf16)
 
@@ -237,13 +231,13 @@
 
 def passed(got_ref):
     spot = place()
-    return [got_ref[lax.rem(spot - move + PEERS, PEERS), SHARD:] for move in MOVES]
+    return [got_ref[lax.rem(spot - move + PEERS, PEERS)].astype(f32)[SHARD:] for move in MOVES]
 
 
 def add_up(parts_ref, out_ref):
-    total = parts_ref[0, :SHARD].astype(f32)
+    total = parts_ref[0].astype(f32)[:SHARD]
     for i in range(1, parts_ref.shape[0]):
-        total = total + parts_ref[i, :SHARD].astype(f32)
+        total = total + parts_ref[i].astype(f32)[:SHARD]
     total = total.astype(bf16)
     for i in range(out_ref.shape[0]):
         out_ref[i] = total
@@ -253,30 +247,30 @@
     add_up(parts_ref, out_ref)
     blocks = passed(parts_ref)
     down_ref[0], up_ref[0] = line_ref[0], line_ref[1]
-    down_ref[1], up_ref[1] = blocks[0], blocks[1]
-    down_ref[2], up_ref[2] = blocks[2], blocks[3]
-
-
-def line_kernel(parts_ref, out_ref):
+    down_ref[1], up_ref[1] = blocks[0].astype(bf16), blocks[1].astype(bf16)
+    down_ref[2], up_ref[2] = blocks[2].astype(bf16), blocks[3].astype(bf16)
+
+
+def line_kernel(parts_ref, down_ref, up_ref, out_ref):
     add_up(parts_ref, out_ref)
 
 
-def post_kernel(
-    dext_ref, gain_ref, sends_ref, got_ref, down_ref, up_ref, sums_ref, dfeat_ref, gmix_ref, grad_ref
-):
+def feat_kernel(dext_ref, gain_ref, sends_ref, got_ref, down_ref, up_ref, dfeat_ref):
     spot = place()
     local = passed(got_ref)
     blocks = []
     for move, block, other in zip(MOVES, local, (down_ref[1], up_ref[1], down_ref[2], up_ref[2])):
         crossed = spot - move >= PEERS if move < 0 else spot < move
-        blocks.append(jnp.where(crossed, other.astype(f32), block.astype(f32)))
+        blocks.append(jnp.where(crossed, other.astype(f32), block))
     blocks += [down_ref[0].astype(f32), up_ref[0].astype(f32)]
     total = dext_ref[...]
     for face in range(FACES):
         hot = (rows_iota((ATOMS, GHOST)) == sends_ref[face]).astype(f32)
-        values = blocks[face][:GHOST].astype(bf16)
-        total = total + dot(hot.astype(bf16), values, ((1,), (0,)))
+        total = total + dot(hot.astype(bf16), blocks[face].astype(bf16), ((1,), (0,)))
     dfeat_ref[0] = total * gain_ref[...]
+
+
+def post_kernel(sums_ref, gmix_ref, grad_ref):
     whole = 3 * CHANS // SHARD
     parts = [sums_ref[i].astype(f32) for i in range(whole)]
     grad = sums_ref[whole].astype(f32)[:NB]
@@ -291,9 +285,9 @@
     grad_ref[...] = factor * grad
 
 
-def swap(block):
+def swap(block, parity):
     pairs = []
-    for i in range(1, 128, 2):
+    for i in range(parity, 128, 2):
         j = (i + 1) % 128
         pairs += [(i, j), (j, i)]
     return lax.ppermute(block, DOM, pairs)
@@ -306,13 +300,13 @@
 def on_device(feat, species, species_gain, send_lists, edge_src, edge_dst, edge_vec, w_rad, w_mix, out_cot):
     shape = jax.ShapeDtypeStruct
     sends = send_lists.reshape(FACES, 1, GHOST)
-    own, gain, block, picks = call(
+    own, gain, pair, picks = call(
         pre_kernel,
         [
             shape((ATOMS, CHANS), bf16),
             shape((ATOMS, CHANS), f32),
-            shape((PAD, CHANS), bf16),
-            shape((PEERS, PAD, CHANS), bf16),
+            shape((2, GHOST, CHANS), bf16),
+            shape((RING, GHOST, CHANS), bf16),
         ],
         feat, species, species_gain, sends,
         scratch=[
@@ -325,7 +319,7 @@
         space=pl.ANY,
         limit=60,
     )
-    near = swap(block)
+    near = [swap(pair[q], q) for q in range(2)]
     far = exchange(picks, PLANE)
     harm, basis = call(
         geo_kernel,
@@ -337,10 +331,10 @@
         main_kernel,
         [
             shape((ATOMS, CHANS), f32),
-            shape((2, PAD, CHANS), bf16),
-            shape((PEERS, SHARD + PAD, CHANS), bf16),
+            shape((2, GHOST, CHANS), bf16),
+            shape((PEERS, SHARD + GHOST, CHANS), bf16),
         ],
-        own, near, far, edge_src, edge_dst, harm, basis, w_rad, w_mix, out_cot,
+        own, *near, far, edge_src, edge_dst, harm, basis, w_rad, w_mix, out_cot,
         scratch=[
             pltpu.VMEM((ROWS, EDGES), bf16),
             pltpu.VMEM((9 * ATOMS, EDGES), bf16),
@@ -353,18 +347,22 @@
     far = exchange(blocks, SLAB)
     parts, down, up = call(
         slab_kernel,
-        [shape((LINES, SHARD, CHANS), bf16)] + [shape((3, PAD, CHANS), bf16)] * 2,
+        [shape((LINES, SHARD, CHANS), bf16)] + [shape((3, GHOST, CHANS), bf16)] * 2,
         far, line,
     )
     down = lax.ppermute(down, "zl", [(i, (i + 3) % 4) for i in range(4)])
     up = lax.ppermute(up, "zl", [(i, (i + 1) % 4) for i in range(4)])
     parts = exchange(parts, LINE)
-    (parts,) = call(line_kernel, [shape((PEERS, SHARD, CHANS), bf16)], parts)
+    (parts,) = call(line_kernel, [shape((PEERS, SHARD, CHANS), bf16)], parts, down, up)
     sums = exchange(parts, SLAB)
-    d_feat, gmix, grad_r = call(
-        post_kernel,
-        [shape((1, ATOMS, CHANS), f32), shape((3 * CHANS, CHANS), f32), shape((NB, CHANS), f32)],
-        dext, gain, sends, far, down, up, sums,
+    (d_feat,) = call(
+        feat_kernel,
+        [shape((1, ATOMS, CHANS), f32)],
+        dext, gain, sends, far, down, up,
+        cost=pl.CostEstimate(flops=10000000, bytes_accessed=500000, transcendentals=0),
+    )
+    gmix, grad_r = call(
+        post_kernel, [shape((3 * CHANS, CHANS), f32), shape((NB, CHANS), f32)], sums
     )
     return d_feat, gmix, grad_r
 

time: 88.5 us -> 85.1 us (0.962)
  blocking collectives: 40.2 us -> 12.7 us
  starting transfers between devices: 24.3 us -> 47.6 us
  Pallas kernels: 9.61 us -> 10.8 us
  waiting for transfers between devices: 12.5 us -> 11.6 us
    all_to_all x2 -> x1, blocking collectives: 40.2 us -> 12.7 us  [exchange(): return lax.all_to_all(blocks, axes, 0, 0, tiled=True)]
    all_to_all x2 -> x3, starting transfers between devices: 16.1 us -> 28.7 us  [exchange(): return lax.all_to_all(blocks, axes, 0, 0, tiled=True)]
    ppermute x1 -> x2, starting transfers between devices: 2.95 us -> 11.9 us  [swap(): return lax.ppermute(block, DOM, pairs)]
    ppermute x1, starting transfers between devices: 3.29 us -> 5.07 us  [on_device(): down = lax.ppermute(down, 'zl', [(i, (i + 3) % 4) for i in range(4)])]
    ppermute x1 -> x2, waiting for transfers between devices: 2.17 us -> 0.65 us  [swap(): return lax.ppermute(block, DOM, pairs)]
    pallas_call x6 -> x7, Pallas kernels: 9.61 us -> 10.8 us  [call(): pl.pallas_call(kernel, out_shape=outs, in_specs=[pl.BlockSpec(memory_spac...]
    all_to_all x2 -> x3, waiting for transfers between devices: 5.94 us -> 6.31 us  [exchange(): return lax.all_to_all(blocks, axes, 0, 0, tiled=True)]
  transfers between devices with their start and end apart: 5 -> 7, of which waited for: 3 -> 3; matrix products, arithmetic and copies ran while one was open for 0% -> 0% of each run, Pallas kernels for 0% -> 1%
where the time goes in v5:
time: 85.1 us; the launch traced here: 84.4 us
  starting transfers between devices  47.6 us (56%)
  blocking collectives  12.7 us (15%)
  waiting for transfers between devices  11.6 us (14%)
  Pallas kernels  10.8 us (13%)
    all_to_all x3, starting transfers between devices, exchange(): return lax.all_to_all(blocks, axes, 0, 0, tiled=True)  28.7 us
    all_to_all x1, blocking collectives, exchange(): return lax.all_to_all(blocks, axes, 0, 0, tiled=True)  12.7 us
    ppermute x2, starting transfers between devices, swap(): return lax.ppermute(block, DOM, pairs)  11.9 us
    pallas_call x7, Pallas kernels, call(): pl.pallas_call(kernel, out_shape=outs, in_specs=[pl.BlockSpec(memory_spac...  10.8 us
    all_to_all x3, waiting for transfers between devices, exchange(): return lax.all_to_all(blocks, axes, 0, 0, tiled=True)  6.31 us
    ppermute x1, starting transfers between devices, on_device(): down = lax.ppermute(down, 'zl', [(i, (i + 3) % 4) for i in range(4)])  5.07 us
    ppermute x1, waiting for transfers between devices, on_device(): up = lax.ppermute(up, 'zl', [(i, (i + 1) % 4) for i in range(4)])  4.68 us
    ppermute x1, starting transfers between devices, on_device(): up = lax.ppermute(up, 'zl', [(i, (i + 1) % 4) for i in range(4)])  1.92 us
  transfers between devices with their start and end apart: 7, of which 3 were waited for; matrix products, arithmetic and copies ran while one was open for 0% of the time, Pallas kernels for 1%

profile of v5, /device:TPU:1, one launch (start us, length us, event | category | flops | bytes accessed | tf_op | source)
XLA Modules:
  0.0 84.4 jit_solution(18298705369485082002)
XLA Ops:
  0.6 1.8 %shard_map.121 = (bf16[64,128]{1,0:T(8,128)(2,1)}, f32[64,128]{1,0:T(8,128)}, bf16[2,24,128]{2,1,0:T(8,128)(2,1)}, bf16[16,24,128]{2,1,0:T(8,128)(2,1)}) custom-call(bf16[1,64,128]{2,1,0:T(8,128)(2,1)} %feat_hbm.1, s32[1,64]{1,0:T(1,128)} %species_hbm.1, f32[5,128]{1,0:T(8,128)} %gain_hbm.1, s32[6,1,24]{2,1,0:T(1,128)} %bitcast.7), custom_call_target="tpu_custom_call" | custom-call | tf_op jit(solution)/shard_map/pallas_call | solution.py:46
  2.5 0.0 copy-start.1
  2.5 0.0 copy-start
  2.5 9.2 %all-to-all-start = ((bf16[16,24,128]{2,1,0:T(8,128)(2,1)}), bf16[16,24,128]{2,1,0:T(8,128)(2,1)S(1)}, u32[]{:S(2)}, u32[]{:S(2)}) async-start(bf16[16,24,128]{2,1,0:T(8,128)(2,1)} %get-tuple-element.19), calls=%async_computation | async-start | bytes 196608 | tf_op jit(solution)/shard_map/all_to_all | solution.py:297
  11.7 0.0 copy-done.9
  11.7 0.0 copy-start.6
  11.7 4.0 %collective-permute-start.1 = (bf16[24,128]{1,0:T(8,128)(2,1)S(1)}, bf16[24,128]{1,0:T(8,128)(2,1)S(1)}, u32[]{:S(2)}, u32[]{:S(2)}) collective-permute-start(bf16[24,128]{1,0:T(8,128)(2,1)S(1)} %get-tuple-element.31), channel_id=1, source_target_pairs={{4,8},{8,4},{12,16},{16,12},{20,24},{24,20},{28,32},{32,28},{36,40... | collective-permute-start | bytes 18440 | tf_op jit(solution)/shard_map/ppermute | solution.py:293
  15.7 7.9 %collective-permute-start = (bf16[24,128]{1,0:T(8,128)(2,1)S(1)}, bf16[24,128]{1,0:T(8,128)(2,1)S(1)}, u32[]{:S(2)}, u32[]{:S(2)}) collective-permute-start(bf16[24,128]{1,0:T(8,128)(2,1)S(1)} %get-tuple-element.32), channel_id=1, source_target_pairs={{0,4},{4,0},{8,12},{12,8},{16,20},{20,16},{24,28},{28,24},{32,36},... | collective-permute-start | bytes 18440 | tf_op jit(solution)/shard_map/ppermute | solution.py:293
  23.7 0.0 copy-start.3
  23.7 0.0 copy-start.4
  23.7 0.0 copy-start.5
  23.7 0.1 shard_map.122
  23.8 0.0 copy-start.8
  23.8 0.0 collective-permute-done.1.p1
  23.8 0.7 collective-permute-done.p0
  24.4 0.0 all-to-all-done.got_ref
  24.5 5.9 %shard_map.123 = (f32[64,128]{1,0:T(8,128)S(1)}, bf16[2,24,128]{2,1,0:T(8,128)(2,1)S(1)}, bf16[32,40,128]{2,1,0:T(8,128)(2,1)S(1)}) custom-call(bf16[64,128]{1,0:T(8,128)(2,1)S(1)} %copy-done.6, bf16[24,128]{1,0:T(8,128)(2,1)S(1)} %collective-permute-done.p0, bf16[24,128]{1,0:T(8,128)(2,1)S(1)} %collective-permute-done.1.p1, ...), custom_call_target="tpu_custom_call" | custom-call | tf_op jit(solution)/shard_map/pallas_call | solution.py:46
  30.4 12.7 %all_to_all.20.parts_ref.got_ref = bf16[32,40,128]{2,1,0:T(8,128)(2,1)S(1)} all-to-all(bf16[32,40,128]{2,1,0:T(8,128)(2,1)S(1)} %get-tuple-element.24), channel_id=1, replica_groups=mesh['zl'=4,'x'=4,'y'=4,'core'=2,'rep'=4] {'x','y','core'}, dimensions={0} | all-to-all | bytes 655360 | tf_op jit(solution)/shard_map/all_to_all | solution.py:297
  43.1 0.7 shard_map.124
  43.8 14.0 %all-to-all-start.2 = ((bf16[16,16,128]{2,1,0:T(8,128)(2,1)}), bf16[16,16,128]{2,1,0:T(8,128)(2,1)S(1)}, u32[]{:S(2)}, u32[]{:S(2)}) async-start(bf16[16,16,128]{2,1,0:T(8,128)(2,1)} %get-tuple-element.28), calls=%async_computation.2 | async-start | bytes 131072 | tf_op jit(solution)/shard_map/all_to_all | solution.py:297
  57.8 5.1 %collective-permute-start.2 = (bf16[3,24,128]{2,1,0:T(8,128)(2,1)S(1)}, bf16[3,24,128]{2,1,0:T(8,128)(2,1)S(1)}, u32[]{:S(2)}, u32[]{:S(2)}) collective-permute-start(bf16[3,24,128]{2,1,0:T(8,128)(2,1)S(1)} %get-tuple-element.26), channel_id=1, source_target_pairs={{0,384},{128,0},{256,128},{384,256},{1,385},{129,1},{257,129},{385... | collective-permute-start | bytes 55304 | tf_op jit(solution)/shard_map/ppermute | solution.py:353
  62.9 1.9 %collective-permute-start.3 = (bf16[3,24,128]{2,1,0:T(8,128)(2,1)S(1)}, bf16[3,24,128]{2,1,0:T(8,128)(2,1)S(1)}, u32[]{:S(2)}, u32[]{:S(2)}) collective-permute-start(bf16[3,24,128]{2,1,0:T(8,128)(2,1)S(1)} %get-tuple-element.27), channel_id=1, source_target_pairs={{0,128},{128,256},{256,384},{384,0},{1,129},{129,257},{257,385},{3... | collective-permute-start | bytes 55304 | tf_op jit(solution)/shard_map/ppermute | solution.py:354
  64.8 0.0 collective-permute-done.2.down_ref
  64.8 4.7 %collective-permute-done.3.up_ref = bf16[3,24,128]{2,1,0:T(8,128)(2,1)S(1)} collective-permute-done((bf16[3,24,128]{2,1,0:T(8,128)(2,1)S(1)}, bf16[3,24,128]{2,1,0:T(8,128)(2,1)S(1)}, u32[]{:S(2)}, u32[]{:S(2)}) %collective-permute-start.3) | collective-permute-done | bytes 18464 | tf_op jit(solution)/shard_map/ppermute | solution.py:354
  69.5 0.0 all-to-all-done.2.parts_ref
  69.5 0.7 shard_map.126
  70.2 5.6 %all-to-all-start.3 = ((bf16[32,16,128]{2,1,0:T(8,128)(2,1)}), bf16[32,16,128]{2,1,0:T(8,128)(2,1)S(1)}, u32[]{:S(2)}, u32[]{:S(2)}) async-start(bf16[32,16,128]{2,1,0:T(8,128)(2,1)} %shard_map.126), calls=%async_computation.3 | async-start | bytes 262144 | tf_op jit(solution)/shard_map/all_to_all | solution.py:297
  75.7 0.0 copy-start.7
  75.8 0.7 copy-done.7
  76.4 0.8 shard_map.125
  77.2 6.3 %all-to-all-done.3.sums_ref = bf16[32,16,128]{2,1,0:T(8,128)(2,1)S(1)} async-done(((bf16[32,16,128]{2,1,0:T(8,128)(2,1)}), bf16[32,16,128]{2,1,0:T(8,128)(2,1)S(1)}, u32[]{:S(2)}, u32[]{:S(2)}) %all-to-all-start.3) | async-done | bytes 131104 | tf_op jit(solution)/shard_map/all_to_all | solution.py:297
  83.5 0.9 %shard_map.127 = (f32[384,128]{1,0:T(8,128)}, f32[8,128]{1,0:T(8,128)}) custom-call(bf16[32,16,128]{2,1,0:T(8,128)(2,1)S(1)} %all-to-all-done.3.sums_ref), custom_call_target="tpu_custom_call" | custom-call | tf_op jit(solution)/shard_map/pallas_call | solution.py:46
  (11 shorter events, 0.0 us)
Async XLA Ops:
  2.5 9.2 %copy-start.9 = (bf16[2,24,128]{2,1,0:T(8,128)(2,1)S(1)}, bf16[2,24,128]{2,1,0:T(8,128)(2,1)}, u32[]{:S(2)}) copy-start(bf16[2,24,128]{2,1,0:T(8,128)(2,1)} %get-tuple-element.18) | copy-start | bytes 36868
  2.5 21.2 %copy-start.1 = (f32[1,3,4096]{2,0,1:T(1,128)S(1)}, f32[1,3,4096]{2,0,1:T(1,128)}, u32[]{:S(2)}) copy-start(f32[1,3,4096]{2,0,1:T(1,128)} %param.16) | copy-start | bytes 147460
  2.5 22.0 %copy-start = (bf16[384,128]{1,0:T(8,128)(2,1)S(1)}, bf16[384,128]{1,0:T(8,128)(2,1)}, u32[]{:S(2)}) copy-start(bf16[384,128]{1,0:T(8,128)(2,1)} %wmix_ref.1) | copy-start | bytes 294916
  2.5 22.0 %all-to-all-start = ((bf16[16,24,128]{2,1,0:T(8,128)(2,1)}), bf16[16,24,128]{2,1,0:T(8,128)(2,1)S(1)}, u32[]{:S(2)}, u32[]{:S(2)}) async-start(bf16[16,24,128]{2,1,0:T(8,128)(2,1)} %get-tuple-element.19), calls=%async_computation | async-start | bytes 196608 | tf_op jit(solution)/shard_map/all_to_all | solution.py:297
  11.7 12.8 %copy-start.6 = (bf16[64,128]{1,0:T(8,128)(2,1)S(1)}, bf16[64,128]{1,0:T(8,128)(2,1)}, u32[]{:S(2)}) copy-start(bf16[64,128]{1,0:T(8,128)(2,1)} %get-tuple-element.17.own_ref) | copy-start | bytes 49156
  11.7 12.1 %collective-permute-start.1 = (bf16[24,128]{1,0:T(8,128)(2,1)S(1)}, bf16[24,128]{1,0:T(8,128)(2,1)S(1)}, u32[]{:S(2)}, u32[]{:S(2)}) collective-permute-start(bf16[24,128]{1,0:T(8,128)(2,1)S(1)} %get-tuple-element.31), channel_id=1, source_target_pairs={{4,8},{8,4},{12,16},{16,12},{20,24},{24,20},{28,32},{32,28},{36,40... | collective-permute-start | bytes 18440 | tf_op jit(solution)/shard_map/ppermute | solution.py:293
  15.7 8.7 %collective-permute-start = (bf16[24,128]{1,0:T(8,128)(2,1)S(1)}, bf16[24,128]{1,0:T(8,128)(2,1)S(1)}, u32[]{:S(2)}, u32[]{:S(2)}) collective-permute-start(bf16[24,128]{1,0:T(8,128)(2,1)S(1)} %get-tuple-element.32), channel_id=1, source_target_pairs={{0,4},{4,0},{8,12},{12,8},{16,20},{20,16},{24,28},{28,24},{32,36},... | collective-permute-start | bytes 18440 | tf_op jit(solution)/shard_map/ppermute | solution.py:293
  23.7 0.8 copy-start.3
  23.7 0.8 copy-start.4
  23.7 0.8 copy-start.5
  23.8 0.7 copy-start.8
  43.8 25.7 %all-to-all-start.2 = ((bf16[16,16,128]{2,1,0:T(8,128)(2,1)}), bf16[16,16,128]{2,1,0:T(8,128)(2,1)S(1)}, u32[]{:S(2)}, u32[]{:S(2)}) async-start(bf16[16,16,128]{2,1,0:T(8,128)(2,1)} %get-tuple-element.28), calls=%async_computation.2 | async-start | bytes 131072 | tf_op jit(solution)/shard_map/all_to_all | solution.py:297
  57.8 7.0 %collective-permute-start.2 = (bf16[3,24,128]{2,1,0:T(8,128)(2,1)S(1)}, bf16[3,24,128]{2,1,0:T(8,128)(2,1)S(1)}, u32[]{:S(2)}, u32[]{:S(2)}) collective-permute-start(bf16[3,24,128]{2,1,0:T(8,128)(2,1)S(1)} %get-tuple-element.26), channel_id=1, source_target_pairs={{0,384},{128,0},{256,128},{384,256},{1,385},{129,1},{257,129},{385... | collective-permute-start | bytes 55304 | tf_op jit(solution)/shard_map/ppermute | solution.py:353
  62.9 6.6 %collective-permute-start.3 = (bf16[3,24,128]{2,1,0:T(8,128)(2,1)S(1)}, bf16[3,24,128]{2,1,0:T(8,128)(2,1)S(1)}, u32[]{:S(2)}, u32[]{:S(2)}) collective-permute-start(bf16[3,24,128]{2,1,0:T(8,128)(2,1)S(1)} %get-tuple-element.27), channel_id=1, source_target_pairs={{0,128},{128,256},{256,384},{384,0},{1,129},{129,257},{257,385},{3... | collective-permute-start | bytes 55304 | tf_op jit(solution)/shard_map/ppermute | solution.py:354
  70.2 5.6 %copy-start.2 = (f32[64,128]{1,0:T(8,128)S(1)}, f32[64,128]{1,0:T(8,128)}, u32[]{:S(2)}) copy-start(f32[64,128]{1,0:T(8,128)} %get-tuple-element.23.gain_ref) | copy-start | bytes 98308
  70.2 13.3 %all-to-all-start.3 = ((bf16[32,16,128]{2,1,0:T(8,128)(2,1)}), bf16[32,16,128]{2,1,0:T(8,128)(2,1)S(1)}, u32[]{:S(2)}, u32[]{:S(2)}) async-start(bf16[32,16,128]{2,1,0:T(8,128)(2,1)} %shard_map.126), calls=%async_computation.3 | async-start | bytes 262144 | tf_op jit(solution)/shard_map/all_to_all | solution.py:297
  75.7 0.7 copy-start.7

commit v6 on v5

--- a/solution.py
+++ b/solution.py
@@ -159,7 +159,7 @@
     ext = jnp.concatenate(blocks, axis=0).T.astype(bf16)
     w_top, w_low = split(wrad_ref[...])
     wrad = jnp.concatenate([w_top, w_low, w_top], axis=0).T.astype(bf16)
-    mom_s[...] = jnp.zeros_like(mom_s)
+    turned = jnp.zeros((CHANS, 9 * ATOMS), f32)
     for start in range(0, EDGES, CHUNK):
         at = pl.ds(start, CHUNK)
         src = src_ref[:, at]
@@ -173,11 +173,13 @@
         radial_s[:, at] = radial
         message = (radial * source).astype(bf16)
         own_hot = rows_iota((ATOMS, CHUNK)) == dst_ref[:, at]
-        harm_s[0:ATOMS, at] = jnp.where(own_hot, 1.0, 0.0).astype(bf16)
+        own_hot = jnp.where(own_hot, 1.0, 0.0).astype(bf16)
+        harm_s[0:ATOMS, at] = own_hot
         for k in range(1, 9):
             harm = harm_ref[k : k + 1, at]
-            harm_s[k * ATOMS : (k + 1) * ATOMS, at] = jnp.where(own_hot, harm, 0.0).astype(bf16)
-        mom_s[...] += dot(harm_s[:, at], message, ((1,), (1,)))
+            harm_s[k * ATOMS : (k + 1) * ATOMS, at] = own_hot * harm.astype(bf16)
+        turned = turned + dot(message, harm_s[:, at], ((1,), (1,)))
+    mom_s[...] = turned.T
     moments = [msg_scale * mom_s[k * ATOMS : (k + 1) * ATOMS, :] for k in range(9)]
     squares = [m * m for m in moments]
     two = squares[4]
@@ -199,17 +201,18 @@
         part = dinv[:, groups[k] * CHANS : (groups[k] + 1) * CHANS]
         mom_s[k * ATOMS : (k + 1) * ATOMS, :] = (2.0 * msg_scale) * moments[k] * part
     dmom_s[...] = mom_s[...].T.astype(bf16)
-    dext = jnp.zeros((ROWS, CHANS), f32)
-    gradr = jnp.zeros((2 * NB, CHANS), f32)
+    both = jnp.zeros((ROWS + 2 * NB, 2 * CHANS), f32)
     for start in range(0, EDGES, CHUNK):
         at = pl.ds(start, CHUNK)
         dmsg = dot(dmom_s[...], harm_s[:, at], ((1,), (0,)))
         dradial = dmsg * source_s[:, at].astype(f32)
         dsource = (dmsg * radial_s[:, at]).astype(bf16)
-        dext = dext + dot(hot_s[:, at], dsource, ((1,), (1,)))
         b_top, b_low = split(basis_ref[:, at])
         basis = jnp.concatenate([b_top, b_low], axis=0).astype(bf16)
-        gradr = gradr + dot(basis, dradial.astype(bf16), ((1,), (1,)))
+        left = jnp.concatenate([hot_s[:, at], basis], axis=0)
+        right = jnp.concatenate([dsource, dradial.astype(bf16)], axis=0)
+        both = both + dot(left, right, ((1,), (1,)))
+    dext, gradr = both[:ROWS, :CHANS], both[ROWS:, CHANS:]
     gradr = jnp.concatenate([gradr[:NB] + gradr[NB:], nothing, nothing[:NB]], axis=0)
     send_ref[3 * CHANS // SHARD] = gradr.astype(bf16)
     for i in range(3 * CHANS // SHARD + 1, PEERS):
@@ -243,26 +246,30 @@
         out_ref[i] = total
 
 
-def slab_kernel(parts_ref, line_ref, out_ref, down_ref, up_ref):
+def slab_kernel(parts_ref, line_ref, out_ref, pass_ref):
     add_up(parts_ref, out_ref)
     blocks = passed(parts_ref)
-    down_ref[0], up_ref[0] = line_ref[0], line_ref[1]
-    down_ref[1], up_ref[1] = blocks[0].astype(bf16), blocks[1].astype(bf16)
-    down_ref[2], up_ref[2] = blocks[2].astype(bf16), blocks[3].astype(bf16)
-
-
-def line_kernel(parts_ref, down_ref, up_ref, out_ref):
+    odd = lax.rem(lax.axis_index("zl"), 2)
+    for i, (down, up) in enumerate([(line_ref[0], line_ref[1]), blocks[:2], blocks[2:]]):
+        pass_ref[1 - odd, i] = down.astype(bf16)
+        pass_ref[odd, i] = up.astype(bf16)
+
+
+def line_kernel(parts_ref, p0, p1, out_ref):
     add_up(parts_ref, out_ref)
 
 
-def feat_kernel(dext_ref, gain_ref, sends_ref, got_ref, down_ref, up_ref, dfeat_ref):
+def feat_kernel(dext_ref, gain_ref, sends_ref, got_ref, p0, p1, dfeat_ref):
     spot = place()
     local = passed(got_ref)
     blocks = []
-    for move, block, other in zip(MOVES, local, (down_ref[1], up_ref[1], down_ref[2], up_ref[2])):
+    a, b = p0[...].astype(f32), p1[...].astype(f32)
+    odd = lax.rem(lax.axis_index("zl"), 2)
+    down, up = jnp.where(odd == 0, a, b), jnp.where(odd == 0, b, a)
+    for move, block, other in zip(MOVES, local, (down[1], up[1], down[2], up[2])):
         crossed = spot - move >= PEERS if move < 0 else spot < move
-        blocks.append(jnp.where(crossed, other.astype(f32), block))
-    blocks += [down_ref[0].astype(f32), up_ref[0].astype(f32)]
+        blocks.append(jnp.where(crossed, other, block))
+    blocks += [down[0], up[0]]
     total = dext_ref[...]
     for face in range(FACES):
         hot = (rows_iota((ATOMS, GHOST)) == sends_ref[face]).astype(f32)
@@ -345,20 +352,20 @@
         ],
     )
     far = exchange(blocks, SLAB)
-    parts, down, up = call(
+    parts, passing = call(
         slab_kernel,
-        [shape((LINES, SHARD, CHANS), bf16)] + [shape((3, GHOST, CHANS), bf16)] * 2,
+        [shape((LINES, SHARD, CHANS), bf16), shape((2, 3, GHOST, CHANS), bf16)],
         far, line,
     )
-    down = lax.ppermute(down, "zl", [(i, (i + 3) % 4) for i in range(4)])
-    up = lax.ppermute(up, "zl", [(i, (i + 1) % 4) for i in range(4)])
+    pairs = [[(0, 1), (1, 0), (2, 3), (3, 2)], [(1, 2), (2, 1), (3, 0), (0, 3)]]
+    passing = [lax.ppermute(passing[q], "zl", pairs[q]) for q in range(2)]
     parts = exchange(parts, LINE)
-    (parts,) = call(line_kernel, [shape((PEERS, SHARD, CHANS), bf16)], parts, down, up)
+    (parts,) = call(line_kernel, [shape((PEERS, SHARD, CHANS), bf16)], parts, *passing)
     sums = exchange(parts, SLAB)
     (d_feat,) = call(
         feat_kernel,
         [shape((1, ATOMS, CHANS), f32)],
-        dext, gain, sends, far, down, up,
+        dext, gain, sends, far, *passing,
         cost=pl.CostEstimate(flops=10000000, bytes_accessed=500000, transcendentals=0),
     )
     gmix, grad_r = call(

time: 85.1 us -> 83.8 us (0.985)
  Pallas kernels: 10.8 us -> 9.5 us
    all_to_all x3, waiting for transfers between devices: 6.31 us -> 8.14 us  [exchange(): return lax.all_to_all(blocks, axes, 0, 0, tiled=True)]
    ppermute x2, waiting for transfers between devices: 4.68 us -> 2.87 us  [on_device(): passing = [lax.ppermute(passing[q], 'zl', pairs[q]) for q in range(2)]]
    pallas_call x7, Pallas kernels: 10.8 us -> 9.5 us  [call(): pl.pallas_call(kernel, out_shape=outs, in_specs=[pl.BlockSpec(memory_spac...]
  transfers between devices with their start and end apart: 7 -> 7, of which waited for: 3 -> 4; matrix products, arithmetic and copies ran while one was open for 0% -> 0% of each run, Pallas kernels for 1% -> 1%
where the time goes in v6:
time: 83.8 us; the launch traced here: 83.2 us
  starting transfers between devices  47.7 us (57%)
  blocking collectives  12.7 us (15%)
  waiting for transfers between devices  11.7 us (14%)
  Pallas kernels  9.5 us (11%)
  between operations  0.87 us (1%)
    all_to_all x3, starting transfers between devices, exchange(): return lax.all_to_all(blocks, axes, 0, 0, tiled=True)  28.7 us
    all_to_all x1, blocking collectives, exchange(): return lax.all_to_all(blocks, axes, 0, 0, tiled=True)  12.7 us
    ppermute x2, starting transfers between devices, swap(): return lax.ppermute(block, DOM, pairs)  11.9 us
    pallas_call x7, Pallas kernels, call(): pl.pallas_call(kernel, out_shape=outs, in_specs=[pl.BlockSpec(memory_spac...  9.5 us
    all_to_all x3, waiting for transfers between devices, exchange(): return lax.all_to_all(blocks, axes, 0, 0, tiled=True)  8.14 us
    ppermute x2, starting transfers between devices, on_device(): passing = [lax.ppermute(passing[q], 'zl', pairs[q]) for q in range(2)]  6.99 us
    ppermute x2, waiting for transfers between devices, on_device(): passing = [lax.ppermute(passing[q], 'zl', pairs[q]) for q in range(2)]  2.87 us
  transfers between devices with their start and end apart: 7, of which 4 were waited for; matrix products, arithmetic and copies ran while one was open for 0% of the time, Pallas kernels for 1%

profile of v6, /device:TPU:1, one launch (start us, length us, event | category | flops | bytes accessed | tf_op | source)
XLA Modules:
  0.0 83.2 jit_solution(11739840368909067441)
XLA Ops:
  0.6 1.8 %shard_map.121 = (bf16[64,128]{1,0:T(8,128)(2,1)}, f32[64,128]{1,0:T(8,128)}, bf16[2,24,128]{2,1,0:T(8,128)(2,1)}, bf16[16,24,128]{2,1,0:T(8,128)(2,1)}) custom-call(bf16[1,64,128]{2,1,0:T(8,128)(2,1)} %feat_hbm.1, s32[1,64]{1,0:T(1,128)} %species_hbm.1, f32[5,128]{1,0:T(8,128)} %gain_hbm.1, s32[6,1,24]{2,1,0:T(1,128)} %bitcast.11), custom_call_target="tpu_custom_call" | custom-call | tf_op jit(solution)/shard_map/pallas_call | solution.py:46
  2.5 0.0 copy-start.1
  2.5 0.0 copy-start
  2.5 9.2 %all-to-all-start = ((bf16[16,24,128]{2,1,0:T(8,128)(2,1)}), bf16[16,24,128]{2,1,0:T(8,128)(2,1)S(1)}, u32[]{:S(2)}, u32[]{:S(2)}) async-start(bf16[16,24,128]{2,1,0:T(8,128)(2,1)} %get-tuple-element.18), calls=%async_computation | async-start | bytes 196608 | tf_op jit(solution)/shard_map/all_to_all | solution.py:304
  11.7 0.0 copy-done.9
  11.7 0.0 copy-start.6
  11.7 4.0 %collective-permute-start.1 = (bf16[24,128]{1,0:T(8,128)(2,1)S(1)}, bf16[24,128]{1,0:T(8,128)(2,1)S(1)}, u32[]{:S(2)}, u32[]{:S(2)}) collective-permute-start(bf16[24,128]{1,0:T(8,128)(2,1)S(1)} %get-tuple-element.31), channel_id=1, source_target_pairs={{4,8},{8,4},{12,16},{16,12},{20,24},{24,20},{28,32},{32,28},{36,40... | collective-permute-start | bytes 18440 | tf_op jit(solution)/shard_map/ppermute | solution.py:300
  15.7 7.9 %collective-permute-start = (bf16[24,128]{1,0:T(8,128)(2,1)S(1)}, bf16[24,128]{1,0:T(8,128)(2,1)S(1)}, u32[]{:S(2)}, u32[]{:S(2)}) collective-permute-start(bf16[24,128]{1,0:T(8,128)(2,1)S(1)} %get-tuple-element.32), channel_id=1, source_target_pairs={{0,4},{4,0},{8,12},{12,8},{16,20},{20,16},{24,28},{28,24},{32,36},... | collective-permute-start | bytes 18440 | tf_op jit(solution)/shard_map/ppermute | solution.py:300
  23.7 0.0 copy-start.3
  23.7 0.0 copy-start.4
  23.7 0.0 copy-start.5
  23.7 0.1 shard_map.122
  23.8 0.0 copy-start.8
  23.8 0.0 collective-permute-done.1.p1
  23.8 0.7 collective-permute-done.p0
  24.4 0.0 all-to-all-done.got_ref
  24.5 4.6 %shard_map.123 = (f32[64,128]{1,0:T(8,128)S(1)}, bf16[2,24,128]{2,1,0:T(8,128)(2,1)S(1)}, bf16[32,40,128]{2,1,0:T(8,128)(2,1)S(1)}) custom-call(bf16[64,128]{1,0:T(8,128)(2,1)S(1)} %copy-done.6, bf16[24,128]{1,0:T(8,128)(2,1)S(1)} %collective-permute-done.p0, bf16[24,128]{1,0:T(8,128)(2,1)S(1)} %collective-permute-done.1.p1, ...), custom_call_target="tpu_custom_call" | custom-call | tf_op jit(solution)/shard_map/pallas_call | solution.py:46
  29.1 12.7 %all_to_all.20.parts_ref.got_ref = bf16[32,40,128]{2,1,0:T(8,128)(2,1)S(1)} all-to-all(bf16[32,40,128]{2,1,0:T(8,128)(2,1)S(1)} %get-tuple-element.23), channel_id=1, replica_groups=mesh['zl'=4,'x'=4,'y'=4,'core'=2,'rep'=4] {'x','y','core'}, dimensions={0} | all-to-all | bytes 655360 | tf_op jit(solution)/shard_map/all_to_all | solution.py:304
  41.8 0.7 shard_map.124
  42.5 14.0 %all-to-all-start.2 = ((bf16[16,16,128]{2,1,0:T(8,128)(2,1)}), bf16[16,16,128]{2,1,0:T(8,128)(2,1)S(1)}, u32[]{:S(2)}, u32[]{:S(2)}) async-start(bf16[16,16,128]{2,1,0:T(8,128)(2,1)} %get-tuple-element.26), calls=%async_computation.2 | async-start | bytes 131072 | tf_op jit(solution)/shard_map/all_to_all | solution.py:304
  56.5 5.1 %collective-permute-start.3 = (bf16[3,24,128]{2,1,0:T(8,128)(2,1)S(1)}, bf16[3,24,128]{2,1,0:T(8,128)(2,1)S(1)}, u32[]{:S(2)}, u32[]{:S(2)}) collective-permute-start(bf16[3,24,128]{2,1,0:T(8,128)(2,1)S(1)} %get-tuple-element.29), channel_id=1, source_target_pairs={{128,256},{256,128},{384,0},{0,384},{129,257},{257,129},{385,1},{1... | collective-permute-start | bytes 55304 | tf_op jit(solution)/shard_map/ppermute | solution.py:361
  61.6 1.9 %collective-permute-start.2 = (bf16[3,24,128]{2,1,0:T(8,128)(2,1)S(1)}, bf16[3,24,128]{2,1,0:T(8,128)(2,1)S(1)}, u32[]{:S(2)}, u32[]{:S(2)}) collective-permute-start(bf16[3,24,128]{2,1,0:T(8,128)(2,1)S(1)} %get-tuple-element.30), channel_id=1, source_target_pairs={{0,128},{128,0},{256,384},{384,256},{1,129},{129,1},{257,385},{385... | collective-permute-start | bytes 55304 | tf_op jit(solution)/shard_map/ppermute | solution.py:361
  63.5 0.0 collective-permute-done.3.p1
  63.5 2.9 %collective-permute-done.2.p0 = bf16[3,24,128]{2,1,0:T(8,128)(2,1)S(1)} collective-permute-done((bf16[3,24,128]{2,1,0:T(8,128)(2,1)S(1)}, bf16[3,24,128]{2,1,0:T(8,128)(2,1)S(1)}, u32[]{:S(2)}, u32[]{:S(2)}) %collective-permute-start.2) | collective-permute-done | bytes 18464 | tf_op jit(solution)/shard_map/ppermute | solution.py:361
  66.4 1.8 %all-to-all-done.2.parts_ref = bf16[16,16,128]{2,1,0:T(8,128)(2,1)S(1)} async-done(((bf16[16,16,128]{2,1,0:T(8,128)(2,1)}), bf16[16,16,128]{2,1,0:T(8,128)(2,1)S(1)}, u32[]{:S(2)}, u32[]{:S(2)}) %all-to-all-start.2) | async-done | bytes 65568 | tf_op jit(solution)/shard_map/all_to_all | solution.py:304
  68.2 0.7 shard_map.126
  68.9 5.6 %all-to-all-start.3 = ((bf16[32,16,128]{2,1,0:T(8,128)(2,1)}), bf16[32,16,128]{2,1,0:T(8,128)(2,1)S(1)}, u32[]{:S(2)}, u32[]{:S(2)}) async-start(bf16[32,16,128]{2,1,0:T(8,128)(2,1)} %shard_map.126), calls=%async_computation.3 | async-start | bytes 262144 | tf_op jit(solution)/shard_map/all_to_all | solution.py:304
  74.5 0.0 copy-start.7
  74.5 0.7 copy-done.7
  75.2 0.8 shard_map.125
  76.0 6.3 %all-to-all-done.3.sums_ref = bf16[32,16,128]{2,1,0:T(8,128)(2,1)S(1)} async-done(((bf16[32,16,128]{2,1,0:T(8,128)(2,1)}), bf16[32,16,128]{2,1,0:T(8,128)(2,1)S(1)}, u32[]{:S(2)}, u32[]{:S(2)}) %all-to-all-start.3) | async-done | bytes 131104 | tf_op jit(solution)/shard_map/all_to_all | solution.py:304
  82.3 0.9 %shard_map.127 = (f32[384,128]{1,0:T(8,128)}, f32[8,128]{1,0:T(8,128)}) custom-call(bf16[32,16,128]{2,1,0:T(8,128)(2,1)S(1)} %all-to-all-done.3.sums_ref), custom_call_target="tpu_custom_call" | custom-call | tf_op jit(solution)/shard_map/pallas_call | solution.py:46
  (12 shorter events, 0.0 us)
Async XLA Ops:
  2.5 9.2 %copy-start.9 = (bf16[2,24,128]{2,1,0:T(8,128)(2,1)S(1)}, bf16[2,24,128]{2,1,0:T(8,128)(2,1)}, u32[]{:S(2)}) copy-start(bf16[2,24,128]{2,1,0:T(8,128)(2,1)} %get-tuple-element.17) | copy-start | bytes 36868
  2.5 21.2 %copy-start.1 = (f32[1,3,4096]{2,0,1:T(1,128)S(1)}, f32[1,3,4096]{2,0,1:T(1,128)}, u32[]{:S(2)}) copy-start(f32[1,3,4096]{2,0,1:T(1,128)} %param.16) | copy-start | bytes 147460
  2.5 22.0 %copy-start = (bf16[384,128]{1,0:T(8,128)(2,1)S(1)}, bf16[384,128]{1,0:T(8,128)(2,1)}, u32[]{:S(2)}) copy-start(bf16[384,128]{1,0:T(8,128)(2,1)} %wmix_ref.1) | copy-start | bytes 294916
  2.5 22.0 %all-to-all-start = ((bf16[16,24,128]{2,1,0:T(8,128)(2,1)}), bf16[16,24,128]{2,1,0:T(8,128)(2,1)S(1)}, u32[]{:S(2)}, u32[]{:S(2)}) async-start(bf16[16,24,128]{2,1,0:T(8,128)(2,1)} %get-tuple-element.18), calls=%async_computation | async-start | bytes 196608 | tf_op jit(solution)/shard_map/all_to_all | solution.py:304
  11.7 12.8 %copy-start.6 = (bf16[64,128]{1,0:T(8,128)(2,1)S(1)}, bf16[64,128]{1,0:T(8,128)(2,1)}, u32[]{:S(2)}) copy-start(bf16[64,128]{1,0:T(8,128)(2,1)} %get-tuple-element.16.own_ref) | copy-start | bytes 49156
  11.7 12.1 %collective-permute-start.1 = (bf16[24,128]{1,0:T(8,128)(2,1)S(1)}, bf16[24,128]{1,0:T(8,128)(2,1)S(1)}, u32[]{:S(2)}, u32[]{:S(2)}) collective-permute-start(bf16[24,128]{1,0:T(8,128)(2,1)S(1)} %get-tuple-element.31), channel_id=1, source_target_pairs={{4,8},{8,4},{12,16},{16,12},{20,24},{24,20},{28,32},{32,28},{36,40... | collective-permute-start | bytes 18440 | tf_op jit(solution)/shard_map/ppermute | solution.py:300
  15.7 8.7 %collective-permute-start = (bf16[24,128]{1,0:T(8,128)(2,1)S(1)}, bf16[24,128]{1,0:T(8,128)(2,1)S(1)}, u32[]{:S(2)}, u32[]{:S(2)}) collective-permute-start(bf16[24,128]{1,0:T(8,128)(2,1)S(1)} %get-tuple-element.32), channel_id=1, source_target_pairs={{0,4},{4,0},{8,12},{12,8},{16,20},{20,16},{24,28},{28,24},{32,36},... | collective-permute-start | bytes 18440 | tf_op jit(solution)/shard_map/ppermute | solution.py:300
  23.7 0.8 copy-start.3
  23.7 0.8 copy-start.4
  23.7 0.8 copy-start.5
  23.8 0.7 copy-start.8
  42.5 25.7 %all-to-all-start.2 = ((bf16[16,16,128]{2,1,0:T(8,128)(2,1)}), bf16[16,16,128]{2,1,0:T(8,128)(2,1)S(1)}, u32[]{:S(2)}, u32[]{:S(2)}) async-start(bf16[16,16,128]{2,1,0:T(8,128)(2,1)} %get-tuple-element.26), calls=%async_computation.2 | async-start | bytes 131072 | tf_op jit(solution)/shard_map/all_to_all | solution.py:304
  56.5 7.0 %collective-permute-start.3 = (bf16[3,24,128]{2,1,0:T(8,128)(2,1)S(1)}, bf16[3,24,128]{2,1,0:T(8,128)(2,1)S(1)}, u32[]{:S(2)}, u32[]{:S(2)}) collective-permute-start(bf16[3,24,128]{2,1,0:T(8,128)(2,1)S(1)} %get-tuple-element.29), channel_id=1, source_target_pairs={{128,256},{256,128},{384,0},{0,384},{129,257},{257,129},{385,1},{1... | collective-permute-start | bytes 55304 | tf_op jit(solution)/shard_map/ppermute | solution.py:361
  61.6 4.8 %collective-permute-start.2 = (bf16[3,24,128]{2,1,0:T(8,128)(2,1)S(1)}, bf16[3,24,128]{2,1,0:T(8,128)(2,1)S(1)}, u32[]{:S(2)}, u32[]{:S(2)}) collective-permute-start(bf16[3,24,128]{2,1,0:T(8,128)(2,1)S(1)} %get-tuple-element.30), channel_id=1, source_target_pairs={{0,128},{128,0},{256,384},{384,256},{1,129},{129,1},{257,385},{385... | collective-permute-start | bytes 55304 | tf_op jit(solution)/shard_map/ppermute | solution.py:361
  68.9 5.6 %copy-start.2 = (f32[64,128]{1,0:T(8,128)S(1)}, f32[64,128]{1,0:T(8,128)}, u32[]{:S(2)}) copy-start(f32[64,128]{1,0:T(8,128)} %get-tuple-element.22.gain_ref) | copy-start | bytes 98308
  68.9 13.4 %all-to-all-start.3 = ((bf16[32,16,128]{2,1,0:T(8,128)(2,1)}), bf16[32,16,128]{2,1,0:T(8,128)(2,1)S(1)}, u32[]{:S(2)}, u32[]{:S(2)}) async-start(bf16[32,16,128]{2,1,0:T(8,128)(2,1)} %shard_map.126), calls=%async_computation.3 | async-start | bytes 262144 | tf_op jit(solution)/shard_map/all_to_all | solution.py:304
  74.5 0.7 copy-start.7

commit v7 on v6

--- a/solution.py
+++ b/solution.py
@@ -29,13 +29,10 @@
 MOVES = (-1, 1, -8, 8)
 DOM = ("zl", "x", "y", "core")
 STRIDES = (1, -1, 4, -4)
-HIGH = lax.Precision.HIGHEST
-
-
-def dot(a, b, dims, precision=None):
-    return lax.dot_general(
-        a, b, (dims, ((), ())), precision=precision, preferred_element_type=f32
-    )
+
+
+def dot(a, b, dims):
+    return lax.dot_general(a, b, (dims, ((), ())), preferred_element_type=f32)
 
 
 def rows_iota(shape):
@@ -85,7 +82,9 @@
         copy.wait()
     hot = (rows_iota((8, ATOMS)) == species_ref[...]).astype(f32)
     gains = jnp.concatenate([gain_ref[...], jnp.zeros((3, CHANS), f32)], axis=0)
-    gain = dot(hot, gains, ((0,), (0,)), HIGH)
+    top, low = split(gains)
+    gains = jnp.concatenate([top, *split(low)], axis=0).astype(bf16)
+    gain = dot(jnp.concatenate([hot] * 3, axis=0).astype(bf16), gains, ((0,), (0,)))
     own = (feat_ref[0].astype(f32) * gain).astype(bf16)
     own_ref[...] = own
     gain_out[...] = gain
@@ -259,7 +258,9 @@
     add_up(parts_ref, out_ref)
 
 
-def feat_kernel(dext_ref, gain_ref, sends_ref, got_ref, p0, p1, dfeat_ref):
+def post_kernel(
+    dext_ref, gain_ref, sends_ref, got_ref, p0, p1, sums_ref, dfeat_ref, gmix_ref, grad_ref
+):
     spot = place()
     local = passed(got_ref)
     blocks = []
@@ -275,9 +276,6 @@
         hot = (rows_iota((ATOMS, GHOST)) == sends_ref[face]).astype(f32)
         total = total + dot(hot.astype(bf16), blocks[face].astype(bf16), ((1,), (0,)))
     dfeat_ref[0] = total * gain_ref[...]
-
-
-def post_kernel(sums_ref, gmix_ref, grad_ref):
     whole = 3 * CHANS // SHARD
     parts = [sums_ref[i].astype(f32) for i in range(whole)]
     grad = sums_ref[whole].astype(f32)[:NB]
@@ -362,14 +360,10 @@
     parts = exchange(parts, LINE)
     (parts,) = call(line_kernel, [shape((PEERS, SHARD, CHANS), bf16)], parts, *passing)
     sums = exchange(parts, SLAB)
-    (d_feat,) = call(
-        feat_kernel,
-        [shape((1, ATOMS, CHANS), f32)],
-        dext, gain, sends, far, *passing,
-        cost=pl.CostEstimate(flops=10000000, bytes_accessed=500000, transcendentals=0),
-    )
-    gmix, grad_r = call(
-        post_kernel, [shape((3 * CHANS, CHANS), f32), shape((NB, CHANS), f32)], sums
+    d_feat, gmix, grad_r = call(
+        post_kernel,
+        [shape((1, ATOMS, CHANS), f32), shape((3 * CHANS, CHANS), f32), shape((NB, CHANS), f32)],
+        dext, gain, sends, far, *passing, sums,
     )
     return d_feat, gmix, grad_r
 

time: 83.8 us -> 83.3 us (level)
  blocking collectives: 12.7 us -> 25.6 us
  waiting for transfers between devices: 11.7 us -> 5.34 us
  starting transfers between devices: 47.7 us -> 42.1 us
  Pallas kernels: 9.5 us -> 8.01 us
    all_to_all x1 -> x2, blocking collectives: 12.7 us -> 25.6 us  [exchange(): return lax.all_to_all(blocks, axes, 0, 0, tiled=True)]
    all_to_all x3 -> x2, waiting for transfers between devices: 8.14 us -> 1.81 us  [exchange(): return lax.all_to_all(blocks, axes, 0, 0, tiled=True)]
    all_to_all x3 -> x2, starting transfers between devices: 28.7 us -> 23.2 us  [exchange(): return lax.all_to_all(blocks, axes, 0, 0, tiled=True)]
    pallas_call x7 -> x6, Pallas kernels: 9.5 us -> 8.01 us  [call(): pl.pallas_call(kernel, out_shape=outs, in_specs=[pl.BlockSpec(memory_spac...]
  transfers between devices with their start and end apart: 7 -> 6, of which waited for: 4 -> 3; matrix products, arithmetic and copies ran while one was open for 0% -> 0% of each run, Pallas kernels for 1% -> 0%
where the time goes in v7:
time: 83.3 us; the launch traced here: 82.7 us
  starting transfers between devices  42.1 us (51%)
  blocking collectives  25.6 us (31%)
  Pallas kernels  8.01 us (10%)
  waiting for transfers between devices  5.34 us (6%)
  between operations  0.85 us (1%)
    all_to_all x2, blocking collectives, exchange(): return lax.all_to_all(blocks, axes, 0, 0, tiled=True)  25.6 us
    all_to_all x2, starting transfers between devices, exchange(): return lax.all_to_all(blocks, axes, 0, 0, tiled=True)  23.2 us
    ppermute x2, starting transfers between devices, swap(): return lax.ppermute(block, DOM, pairs)  11.9 us
    pallas_call x6, Pallas kernels, call(): pl.pallas_call(kernel, out_shape=outs, in_specs=[pl.BlockSpec(memory_spac...  8.01 us
    ppermute x2, starting transfers between devices, on_device(): passing = [lax.ppermute(passing[q], 'zl', pairs[q]) for q in range(2)]  6.99 us
    ppermute x2, waiting for transfers between devices, on_device(): passing = [lax.ppermute(passing[q], 'zl', pairs[q]) for q in range(2)]  2.87 us
    all_to_all x2, waiting for transfers between devices, exchange(): return lax.all_to_all(blocks, axes, 0, 0, tiled=True)  1.81 us
  transfers between devices with their start and end apart: 6, of which 3 were waited for; matrix products, arithmetic and copies ran while one was open for 0% of the time, Pallas kernels for 0%

profile of v7, /device:TPU:1, one launch (start us, length us, event | category | flops | bytes accessed | tf_op | source)
XLA Modules:
  0.0 82.7 jit_solution(3068207435779184489)
XLA Ops:
  0.6 1.7 %shard_map.121 = (bf16[64,128]{1,0:T(8,128)(2,1)}, f32[64,128]{1,0:T(8,128)}, bf16[2,24,128]{2,1,0:T(8,128)(2,1)}, bf16[16,24,128]{2,1,0:T(8,128)(2,1)}) custom-call(bf16[1,64,128]{2,1,0:T(8,128)(2,1)} %feat_hbm.1, s32[1,64]{1,0:T(1,128)} %species_hbm.1, f32[5,128]{1,0:T(8,128)} %gain_hbm.1, s32[6,1,24]{2,1,0:T(1,128)} %bitcast.11), custom_call_target="tpu_custom_call" | custom-call | tf_op jit(solution)/shard_map/pallas_call | solution.py:43
  2.4 0.0 copy-start.9
  2.4 0.0 copy-start.1
  2.4 0.0 copy-start
  2.4 9.2 %all-to-all-start = ((bf16[16,24,128]{2,1,0:T(8,128)(2,1)}), bf16[16,24,128]{2,1,0:T(8,128)(2,1)S(1)}, u32[]{:S(2)}, u32[]{:S(2)}) async-start(bf16[16,24,128]{2,1,0:T(8,128)(2,1)} %get-tuple-element.16), calls=%async_computation | async-start | bytes 196608 | tf_op jit(solution)/shard_map/all_to_all | solution.py:302
  11.6 0.0 copy-done.9
  11.6 0.0 copy-start.6
  11.6 4.0 %collective-permute-start.1 = (bf16[24,128]{1,0:T(8,128)(2,1)S(1)}, bf16[24,128]{1,0:T(8,128)(2,1)S(1)}, u32[]{:S(2)}, u32[]{:S(2)}) collective-permute-start(bf16[24,128]{1,0:T(8,128)(2,1)S(1)} %get-tuple-element.27), channel_id=1, source_target_pairs={{4,8},{8,4},{12,16},{16,12},{20,24},{24,20},{28,32},{32,28},{36,40... | collective-permute-start | bytes 18440 | tf_op jit(solution)/shard_map/ppermute | solution.py:298
  15.7 7.9 %collective-permute-start = (bf16[24,128]{1,0:T(8,128)(2,1)S(1)}, bf16[24,128]{1,0:T(8,128)(2,1)S(1)}, u32[]{:S(2)}, u32[]{:S(2)}) collective-permute-start(bf16[24,128]{1,0:T(8,128)(2,1)S(1)} %get-tuple-element.28), channel_id=1, source_target_pairs={{0,4},{4,0},{8,12},{12,8},{16,20},{20,16},{24,28},{28,24},{32,36},... | collective-permute-start | bytes 18440 | tf_op jit(solution)/shard_map/ppermute | solution.py:298
  23.6 0.0 copy-done.1
  23.6 0.0 copy-start.3
  23.6 0.0 copy-start.4
  23.6 0.0 copy-start.5
  23.6 0.1 shard_map.122
  23.7 0.0 copy-start.8
  23.7 0.0 collective-permute-done.1.p1
  23.7 0.7 collective-permute-done.p0
  24.4 0.0 all-to-all-done.got_ref
  24.4 0.0 copy-done
  24.4 4.6 %shard_map.123 = (f32[64,128]{1,0:T(8,128)S(1)}, bf16[2,24,128]{2,1,0:T(8,128)(2,1)S(1)}, bf16[32,40,128]{2,1,0:T(8,128)(2,1)S(1)}) custom-call(bf16[64,128]{1,0:T(8,128)(2,1)S(1)} %copy-done.6, bf16[24,128]{1,0:T(8,128)(2,1)S(1)} %collective-permute-done.p0, bf16[24,128]{1,0:T(8,128)(2,1)S(1)} %collective-permute-done.1.p1, ...), custom_call_target="tpu_custom_call" | custom-call | tf_op jit(solution)/shard_map/pallas_call | solution.py:43
  29.0 12.7 %all_to_all.20.parts_ref.got_ref = bf16[32,40,128]{2,1,0:T(8,128)(2,1)S(1)} all-to-all(bf16[32,40,128]{2,1,0:T(8,128)(2,1)S(1)} %get-tuple-element.21), channel_id=1, replica_groups=mesh['zl'=4,'x'=4,'y'=4,'core'=2,'rep'=4] {'x','y','core'}, dimensions={0} | all-to-all | bytes 655360 | tf_op jit(solution)/shard_map/all_to_all | solution.py:302
  41.7 0.7 shard_map.124
  42.4 14.0 %all-to-all-start.2 = ((bf16[16,16,128]{2,1,0:T(8,128)(2,1)}), bf16[16,16,128]{2,1,0:T(8,128)(2,1)S(1)}, u32[]{:S(2)}, u32[]{:S(2)}) async-start(bf16[16,16,128]{2,1,0:T(8,128)(2,1)} %get-tuple-element.24), calls=%async_computation.2 | async-start | bytes 131072 | tf_op jit(solution)/shard_map/all_to_all | solution.py:302
  56.4 5.1 %collective-permute-start.3 = (bf16[3,24,128]{2,1,0:T(8,128)(2,1)S(1)}, bf16[3,24,128]{2,1,0:T(8,128)(2,1)S(1)}, u32[]{:S(2)}, u32[]{:S(2)}) collective-permute-start(bf16[3,24,128]{2,1,0:T(8,128)(2,1)S(1)} %get-tuple-element.25), channel_id=1, source_target_pairs={{128,256},{256,128},{384,0},{0,384},{129,257},{257,129},{385,1},{1... | collective-permute-start | bytes 55304 | tf_op jit(solution)/shard_map/ppermute | solution.py:359
  61.5 1.9 %collective-permute-start.2 = (bf16[3,24,128]{2,1,0:T(8,128)(2,1)S(1)}, bf16[3,24,128]{2,1,0:T(8,128)(2,1)S(1)}, u32[]{:S(2)}, u32[]{:S(2)}) collective-permute-start(bf16[3,24,128]{2,1,0:T(8,128)(2,1)S(1)} %get-tuple-element.26), channel_id=1, source_target_pairs={{0,128},{128,0},{256,384},{384,256},{1,129},{129,1},{257,385},{385... | collective-permute-start | bytes 55304 | tf_op jit(solution)/shard_map/ppermute | solution.py:359
  63.4 0.0 collective-permute-done.3.p1
  63.5 2.9 %collective-permute-done.2.p0 = bf16[3,24,128]{2,1,0:T(8,128)(2,1)S(1)} collective-permute-done((bf16[3,24,128]{2,1,0:T(8,128)(2,1)S(1)}, bf16[3,24,128]{2,1,0:T(8,128)(2,1)S(1)}, u32[]{:S(2)}, u32[]{:S(2)}) %collective-permute-start.2) | collective-permute-done | bytes 18464 | tf_op jit(solution)/shard_map/ppermute | solution.py:359
  66.3 1.8 %all-to-all-done.2.parts_ref = bf16[16,16,128]{2,1,0:T(8,128)(2,1)S(1)} async-done(((bf16[16,16,128]{2,1,0:T(8,128)(2,1)}), bf16[16,16,128]{2,1,0:T(8,128)(2,1)S(1)}, u32[]{:S(2)}, u32[]{:S(2)}) %all-to-all-start.2) | async-done | bytes 65568 | tf_op jit(solution)/shard_map/all_to_all | solution.py:302
  68.2 0.0 copy-start.2
  68.2 12.9 %all_to_all.21.sums_ref = bf16[32,16,128]{2,1,0:T(8,128)(2,1)S(1)} all-to-all(bf16[32,16,128]{2,1,0:T(8,128)(2,1)S(1)} %shard_map.125), channel_id=1, replica_groups=mesh['zl'=4,'x'=4,'y'=4,'core'=2,'rep'=4] {'x','y','core'}, dimensions={0} | all-to-all | bytes 262144 | tf_op jit(solution)/shard_map/all_to_all | solution.py:302
  81.1 0.7 copy-done.7
  81.8 0.9 %shard_map.126 = (f32[1,64,128]{2,1,0:T(8,128)}, f32[384,128]{1,0:T(8,128)}, f32[8,128]{1,0:T(8,128)}) custom-call(f32[64,128]{1,0:T(8,128)S(1)} %get-tuple-element.19.dext_ref, f32[64,128]{1,0:T(8,128)S(1)} %copy-done.2, s32[6,1,24]{2,1,0:T(1,128)S(1)} %bitcast.12, bf16[32,40,128]{2,1,0:T(8,128)(2,1)S(1)} %all_to_all.20.parts_ref.got_ref, ...), custom_call_target="tpu_custom_call" | custom-call | tf_op jit(solution)/shard_map/pallas_call | solution.py:43
  (10 shorter events, 0.1 us)
Async XLA Ops:
  2.4 9.2 %copy-start.9 = (bf16[2,24,128]{2,1,0:T(8,128)(2,1)S(1)}, bf16[2,24,128]{2,1,0:T(8,128)(2,1)}, u32[]{:S(2)}) copy-start(bf16[2,24,128]{2,1,0:T(8,128)(2,1)} %get-tuple-element.15) | copy-start | bytes 36868
  2.4 21.2 %copy-start.1 = (f32[1,3,4096]{2,0,1:T(1,128)S(1)}, f32[1,3,4096]{2,0,1:T(1,128)}, u32[]{:S(2)}) copy-start(f32[1,3,4096]{2,0,1:T(1,128)} %param.16) | copy-start | bytes 147460
  2.4 22.0 %copy-start = (bf16[384,128]{1,0:T(8,128)(2,1)S(1)}, bf16[384,128]{1,0:T(8,128)(2,1)}, u32[]{:S(2)}) copy-start(bf16[384,128]{1,0:T(8,128)(2,1)} %wmix_ref.1) | copy-start | bytes 294916
  2.4 22.0 %all-to-all-start = ((bf16[16,24,128]{2,1,0:T(8,128)(2,1)}), bf16[16,24,128]{2,1,0:T(8,128)(2,1)S(1)}, u32[]{:S(2)}, u32[]{:S(2)}) async-start(bf16[16,24,128]{2,1,0:T(8,128)(2,1)} %get-tuple-element.16), calls=%async_computation | async-start | bytes 196608 | tf_op jit(solution)/shard_map/all_to_all | solution.py:302
  11.6 12.8 %copy-start.6 = (bf16[64,128]{1,0:T(8,128)(2,1)S(1)}, bf16[64,128]{1,0:T(8,128)(2,1)}, u32[]{:S(2)}) copy-start(bf16[64,128]{1,0:T(8,128)(2,1)} %get-tuple-element.14.own_ref) | copy-start | bytes 49156
  11.6 12.1 %collective-permute-start.1 = (bf16[24,128]{1,0:T(8,128)(2,1)S(1)}, bf16[24,128]{1,0:T(8,128)(2,1)S(1)}, u32[]{:S(2)}, u32[]{:S(2)}) collective-permute-start(bf16[24,128]{1,0:T(8,128)(2,1)S(1)} %get-tuple-element.27), channel_id=1, source_target_pairs={{4,8},{8,4},{12,16},{16,12},{20,24},{24,20},{28,32},{32,28},{36,40... | collective-permute-start | bytes 18440 | tf_op jit(solution)/shard_map/ppermute | solution.py:298
  15.7 8.7 %collective-permute-start = (bf16[24,128]{1,0:T(8,128)(2,1)S(1)}, bf16[24,128]{1,0:T(8,128)(2,1)S(1)}, u32[]{:S(2)}, u32[]{:S(2)}) collective-permute-start(bf16[24,128]{1,0:T(8,128)(2,1)S(1)} %get-tuple-element.28), channel_id=1, source_target_pairs={{0,4},{4,0},{8,12},{12,8},{16,20},{20,16},{24,28},{28,24},{32,36},... | collective-permute-start | bytes 18440 | tf_op jit(solution)/shard_map/ppermute | solution.py:298
  23.6 0.8 copy-start.3
  23.6 0.8 copy-start.4
  23.6 0.8 copy-start.5
  23.7 0.7 copy-start.8
  42.4 25.7 %all-to-all-start.2 = ((bf16[16,16,128]{2,1,0:T(8,128)(2,1)}), bf16[16,16,128]{2,1,0:T(8,128)(2,1)S(1)}, u32[]{:S(2)}, u32[]{:S(2)}) async-start(bf16[16,16,128]{2,1,0:T(8,128)(2,1)} %get-tuple-element.24), calls=%async_computation.2 | async-start | bytes 131072 | tf_op jit(solution)/shard_map/all_to_all | solution.py:302
  56.4 7.0 %collective-permute-start.3 = (bf16[3,24,128]{2,1,0:T(8,128)(2,1)S(1)}, bf16[3,24,128]{2,1,0:T(8,128)(2,1)S(1)}, u32[]{:S(2)}, u32[]{:S(2)}) collective-permute-start(bf16[3,24,128]{2,1,0:T(8,128)(2,1)S(1)} %get-tuple-element.25), channel_id=1, source_target_pairs={{128,256},{256,128},{384,0},{0,384},{129,257},{257,129},{385,1},{1... | collective-permute-start | bytes 55304 | tf_op jit(solution)/shard_map/ppermute | solution.py:359
  61.5 4.8 %collective-permute-start.2 = (bf16[3,24,128]{2,1,0:T(8,128)(2,1)S(1)}, bf16[3,24,128]{2,1,0:T(8,128)(2,1)S(1)}, u32[]{:S(2)}, u32[]{:S(2)}) collective-permute-start(bf16[3,24,128]{2,1,0:T(8,128)(2,1)S(1)} %get-tuple-element.26), channel_id=1, source_target_pairs={{0,128},{128,0},{256,384},{384,256},{1,129},{129,1},{257,385},{385... | collective-permute-start | bytes 55304 | tf_op jit(solution)/shard_map/ppermute | solution.py:359
  68.2 12.9 %copy-start.2 = (f32[64,128]{1,0:T(8,128)S(1)}, f32[64,128]{1,0:T(8,128)}, u32[]{:S(2)}) copy-start(f32[64,128]{1,0:T(8,128)} %get-tuple-element.20.gain_ref) | copy-start | bytes 98308
  81.1 0.7 copy-start.7

commit v8 on v7

--- a/solution.py
+++ b/solution.py
@@ -147,7 +147,7 @@
 
 def main_kernel(
     own_ref, p0, p1, got_ref, src_ref, dst_ref, harm_ref, basis_ref, wrad_ref, wmix_ref, cot_ref,
-    dext_ref, line_ref, send_ref,
+    lists_ref, dext_ref, line_ref, send_ref, lists_out,
     hot_s, harm_s, radial_s, source_s, mom_s, dmom_s,
 ):
     ring, core = position()
@@ -225,6 +225,7 @@
         send_ref[to] = jnp.concatenate([shard, block], axis=0).astype(bf16)
     line_ref[0] = ghosts[4].astype(bf16)
     line_ref[1] = ghosts[5].astype(bf16)
+    lists_out[...] = lists_ref[...]
 
 
 def place():
@@ -248,25 +249,26 @@
 def slab_kernel(parts_ref, line_ref, out_ref, pass_ref):
     add_up(parts_ref, out_ref)
     blocks = passed(parts_ref)
-    odd = lax.rem(lax.axis_index("zl"), 2)
+    level = lax.axis_index("zl")
+    pass_ref[...] = jnp.zeros_like(pass_ref)
     for i, (down, up) in enumerate([(line_ref[0], line_ref[1]), blocks[:2], blocks[2:]]):
-        pass_ref[1 - odd, i] = down.astype(bf16)
-        pass_ref[odd, i] = up.astype(bf16)
-
-
-def line_kernel(parts_ref, p0, p1, out_ref):
+        pass_ref[lax.rem(level + 3, 4), i] = down.astype(bf16)
+        pass_ref[lax.rem(level + 1, 4), i] = up.astype(bf16)
+
+
+def line_kernel(parts_ref, passed_ref, out_ref):
     add_up(parts_ref, out_ref)
 
 
 def post_kernel(
-    dext_ref, gain_ref, sends_ref, got_ref, p0, p1, sums_ref, dfeat_ref, gmix_ref, grad_ref
+    dext_ref, gain_ref, sends_ref, got_ref, passed_ref, sums_ref, dfeat_ref, gmix_ref, grad_ref
 ):
     spot = place()
     local = passed(got_ref)
     blocks = []
-    a, b = p0[...].astype(f32), p1[...].astype(f32)
-    odd = lax.rem(lax.axis_index("zl"), 2)
-    down, up = jnp.where(odd == 0, a, b), jnp.where(odd == 0, b, a)
+    level = lax.axis_index("zl")
+    down = passed_ref[lax.rem(level + 1, 4)].astype(f32)
+    up = passed_ref[lax.rem(level + 3, 4)].astype(f32)
     for move, block, other in zip(MOVES, local, (down[1], up[1], down[2], up[2])):
         crossed = spot - move >= PEERS if move < 0 else spot < move
         blocks.append(jnp.where(crossed, other, block))
@@ -332,14 +334,15 @@
         edge_vec.reshape(3, 1, EDGES),
         cost=pl.CostEstimate(flops=1000000, bytes_accessed=400000, transcendentals=0),
     )
-    dext, line, blocks = call(
+    dext, line, blocks, lists = call(
         main_kernel,
         [
             shape((ATOMS, CHANS), f32),
             shape((2, GHOST, CHANS), bf16),
             shape((PEERS, SHARD + GHOST, CHANS), bf16),
+            shape((FACES, 1, GHOST), jnp.int32),
         ],
-        own, *near, far, edge_src, edge_dst, harm, basis, w_rad, w_mix, out_cot,
+        own, *near, far, edge_src, edge_dst, harm, basis, w_rad, w_mix, out_cot, sends,
         scratch=[
             pltpu.VMEM((ROWS, EDGES), bf16),
             pltpu.VMEM((9 * ATOMS, EDGES), bf16),
@@ -352,18 +355,17 @@
     far = exchange(blocks, SLAB)
     parts, passing = call(
         slab_kernel,
-        [shape((LINES, SHARD, CHANS), bf16), shape((2, 3, GHOST, CHANS), bf16)],
+        [shape((LINES, SHARD, CHANS), bf16), shape((4, 3, GHOST, CHANS), bf16)],
         far, line,
     )
-    pairs = [[(0, 1), (1, 0), (2, 3), (3, 2)], [(1, 2), (2, 1), (3, 0), (0, 3)]]
-    passing = [lax.ppermute(passing[q], "zl", pairs[q]) for q in range(2)]
+    passing = exchange(passing, "zl")
     parts = exchange(parts, LINE)
-    (parts,) = call(line_kernel, [shape((PEERS, SHARD, CHANS), bf16)], parts, *passing)
+    (parts,) = call(line_kernel, [shape((PEERS, SHARD, CHANS), bf16)], parts, passing)
     sums = exchange(parts, SLAB)
     d_feat, gmix, grad_r = call(
         post_kernel,
         [shape((1, ATOMS, CHANS), f32), shape((3 * CHANS, CHANS), f32), shape((NB, CHANS), f32)],
-        dext, gain, sends, far, *passing, sums,
+        dext, gain, lists, far, passing, sums,
     )
     return d_feat, gmix, grad_r
 

time: 83.3 us -> 91.6 us (1.100)
  blocking collectives: 25.6 us -> 61.1 us
  starting transfers between devices: 42.1 us -> 21.1 us
  waiting for transfers between devices: 5.34 us -> 0.64 us
    all_to_all x2 -> x4, blocking collectives: 25.6 us -> 61.1 us  [exchange(): return lax.all_to_all(blocks, axes, 0, 0, tiled=True)]
    all_to_all x2 -> x1, starting transfers between devices: 23.2 us -> 9.16 us  [exchange(): return lax.all_to_all(blocks, axes, 0, 0, tiled=True)]
    ppermute x2 -> x0, starting transfers between devices: 6.99 us -> none  [on_device(): passing = [lax.ppermute(passing[q], 'zl', pairs[q]) for q in range(2)]]
    ppermute x2 -> x0, waiting for transfers between devices: 2.87 us -> none  [on_device(): passing = [lax.ppermute(passing[q], 'zl', pairs[q]) for q in range(2)]]
    all_to_all x2 -> x1, waiting for transfers between devices: 1.81 us -> 0.01 us  [exchange(): return lax.all_to_all(blocks, axes, 0, 0, tiled=True)]
  transfers between devices with their start and end apart: 6 -> 3, of which waited for: 3 -> 1; matrix products, arithmetic and copies ran while one was open for 0% -> 0% of each run, Pallas kernels for 0% -> 0%
where the time goes in v8:
time: 91.6 us; the launch traced here: 91.1 us
  blocking collectives  61.1 us (67%)
  starting transfers between devices  21.1 us (23%)
  Pallas kernels  7.37 us (8%)
    all_to_all x4, blocking collectives, exchange(): return lax.all_to_all(blocks, axes, 0, 0, tiled=True)  61.1 us
    ppermute x2, starting transfers between devices, swap(): return lax.ppermute(block, DOM, pairs)  11.9 us
    all_to_all x1, starting transfers between devices, exchange(): return lax.all_to_all(blocks, axes, 0, 0, tiled=True)  9.16 us
    pallas_call x6, Pallas kernels, call(): pl.pallas_call(kernel, out_shape=outs, in_specs=[pl.BlockSpec(memory_spac...  7.37 us
  transfers between devices with their start and end apart: 3, of which 1 were waited for; matrix products, arithmetic and copies ran while one was open for 0% of the time, Pallas kernels for 0%

profile of v8, /device:TPU:1, one launch (start us, length us, event | category | flops | bytes accessed | tf_op | source)
XLA Modules:
  0.0 91.1 jit_solution(9040366072608342133)
XLA Ops:
  0.6 1.7 %shard_map.121 = (bf16[64,128]{1,0:T(8,128)(2,1)}, f32[64,128]{1,0:T(8,128)}, bf16[2,24,128]{2,1,0:T(8,128)(2,1)}, bf16[16,24,128]{2,1,0:T(8,128)(2,1)}) custom-call(bf16[1,64,128]{2,1,0:T(8,128)(2,1)} %feat_hbm.1, s32[1,64]{1,0:T(1,128)} %species_hbm.1, f32[5,128]{1,0:T(8,128)} %gain_hbm.1, s32[6,1,24]{2,1,0:T(1,128)} %bitcast.7), custom_call_target="tpu_custom_call" | custom-call | tf_op jit(solution)/shard_map/pallas_call | solution.py:43
  2.4 0.0 copy-start.9
  2.4 0.0 copy-start.1
  2.4 0.0 copy-start
  2.4 9.2 %all-to-all-start = ((bf16[16,24,128]{2,1,0:T(8,128)(2,1)}), bf16[16,24,128]{2,1,0:T(8,128)(2,1)S(1)}, u32[]{:S(2)}, u32[]{:S(2)}) async-start(bf16[16,24,128]{2,1,0:T(8,128)(2,1)} %get-tuple-element.17), calls=%async_computation | async-start | bytes 196608 | tf_op jit(solution)/shard_map/all_to_all | solution.py:304
  11.6 0.0 copy-done.9
  11.6 0.0 copy-start.6
  11.6 4.0 %collective-permute-start.1 = (bf16[24,128]{1,0:T(8,128)(2,1)S(1)}, bf16[24,128]{1,0:T(8,128)(2,1)S(1)}, u32[]{:S(2)}, u32[]{:S(2)}) collective-permute-start(bf16[24,128]{1,0:T(8,128)(2,1)S(1)} %get-tuple-element.27), channel_id=1, source_target_pairs={{4,8},{8,4},{12,16},{16,12},{20,24},{24,20},{28,32},{32,28},{36,40... | collective-permute-start | bytes 18440 | tf_op jit(solution)/shard_map/ppermute | solution.py:300
  15.7 7.9 %collective-permute-start = (bf16[24,128]{1,0:T(8,128)(2,1)S(1)}, bf16[24,128]{1,0:T(8,128)(2,1)S(1)}, u32[]{:S(2)}, u32[]{:S(2)}) collective-permute-start(bf16[24,128]{1,0:T(8,128)(2,1)S(1)} %get-tuple-element.28), channel_id=1, source_target_pairs={{0,4},{4,0},{8,12},{12,8},{16,20},{20,16},{24,28},{28,24},{32,36},... | collective-permute-start | bytes 18440 | tf_op jit(solution)/shard_map/ppermute | solution.py:300
  23.6 0.0 copy-start.8
  23.6 0.0 copy-done.1
  23.6 0.0 copy-start.3
  23.6 0.0 copy-start.4
  23.6 0.0 copy-start.5
  23.6 0.1 shard_map.122
  23.7 0.0 copy-start.7
  23.7 0.0 collective-permute-done.1.p1
  23.7 0.6 collective-permute-done.p0
  24.4 0.0 all-to-all-done.got_ref
  24.4 0.0 copy-done
  24.4 0.0 copy-done.6
  24.4 0.0 copy-done.8
  24.4 0.0 copy-done.3
  24.4 0.0 copy-done.4
  24.4 0.0 copy-done.5
  24.4 4.6 %shard_map.123 = (f32[64,128]{1,0:T(8,128)S(1)}, bf16[2,24,128]{2,1,0:T(8,128)(2,1)S(1)}, bf16[32,40,128]{2,1,0:T(8,128)(2,1)S(1)}, s32[6,1,24]{2,1,0:T(1,128)S(1)}) custom-call(bf16[64,128]{1,0:T(8,128)(2,1)S(1)} %copy-done.6, bf16[24,128]{1,0:T(8,128)(2,1)S(1)} %collective-permute-done.p0, bf16[24,128]{1,0:T(8,128)(2,1)S(1)} %collective-permute-done.1.p1, ...), custom_call_target="tpu_custom_call" | custom-call | tf_op jit(solution)/shard_map/pallas_call | solution.py:43
  29.0 12.7 %all_to_all.25.parts_ref.got_ref = bf16[32,40,128]{2,1,0:T(8,128)(2,1)S(1)} all-to-all(bf16[32,40,128]{2,1,0:T(8,128)(2,1)S(1)} %get-tuple-element.23), channel_id=1, replica_groups=mesh['zl'=4,'x'=4,'y'=4,'core'=2,'rep'=4] {'x','y','core'}, dimensions={0} | all-to-all | bytes 655360 | tf_op jit(solution)/shard_map/all_to_all | solution.py:304
  41.8 10.5 %all_to_all.26.passed_ref = bf16[4,3,24,128]{3,2,1,0:T(8,128)(2,1)S(1)} all-to-all(bf16[4,3,24,128]{3,2,1,0:T(8,128)(2,1)S(1)} %get-tuple-element.25), channel_id=1, replica_groups=mesh['zl'=4,'x'=4,'y'=4,'core'=2,'rep'=4] {'zl'}, dimensions={0} | all-to-all | bytes 147456 | tf_op jit(solution)/shard_map/all_to_all | solution.py:304
  52.3 23.7 %all_to_all.27.parts_ref = bf16[16,16,128]{2,1,0:T(8,128)(2,1)S(1)} all-to-all(bf16[16,16,128]{2,1,0:T(8,128)(2,1)S(1)} %get-tuple-element.26), channel_id=1, replica_groups=mesh['zl'=4,'x'=4,'y'=4,'core'=2,'rep'=4] {'zl','rep'}, dimensions={0} | all-to-all | bytes 131072 | tf_op jit(solution)/shard_map/all_to_all | solution.py:304
  76.1 0.0 copy-start.2
  76.1 14.1 %all_to_all.28.sums_ref = bf16[32,16,128]{2,1,0:T(8,128)(2,1)S(1)} all-to-all(bf16[32,16,128]{2,1,0:T(8,128)(2,1)S(1)} %shard_map.125), channel_id=1, replica_groups=mesh['zl'=4,'x'=4,'y'=4,'core'=2,'rep'=4] {'x','y','core'}, dimensions={0} | all-to-all | bytes 262144 | tf_op jit(solution)/shard_map/all_to_all | solution.py:304
  90.2 0.9 shard_map.126
  (5 shorter events, 0.1 us)
Async XLA Ops:
  2.4 9.2 %copy-start.9 = (bf16[2,24,128]{2,1,0:T(8,128)(2,1)S(1)}, bf16[2,24,128]{2,1,0:T(8,128)(2,1)}, u32[]{:S(2)}) copy-start(bf16[2,24,128]{2,1,0:T(8,128)(2,1)} %get-tuple-element.16) | copy-start | bytes 36868
  2.4 21.2 %copy-start.1 = (f32[1,3,4096]{2,0,1:T(1,128)S(1)}, f32[1,3,4096]{2,0,1:T(1,128)}, u32[]{:S(2)}) copy-start(f32[1,3,4096]{2,0,1:T(1,128)} %param.16) | copy-start | bytes 147460
  2.4 22.0 %copy-start = (bf16[384,128]{1,0:T(8,128)(2,1)S(1)}, bf16[384,128]{1,0:T(8,128)(2,1)}, u32[]{:S(2)}) copy-start(bf16[384,128]{1,0:T(8,128)(2,1)} %wmix_ref.1) | copy-start | bytes 294916
  2.4 22.0 %all-to-all-start = ((bf16[16,24,128]{2,1,0:T(8,128)(2,1)}), bf16[16,24,128]{2,1,0:T(8,128)(2,1)S(1)}, u32[]{:S(2)}, u32[]{:S(2)}) async-start(bf16[16,24,128]{2,1,0:T(8,128)(2,1)} %get-tuple-element.17), calls=%async_computation | async-start | bytes 196608 | tf_op jit(solution)/shard_map/all_to_all | solution.py:304
  11.6 12.8 %copy-start.6 = (bf16[64,128]{1,0:T(8,128)(2,1)S(1)}, bf16[64,128]{1,0:T(8,128)(2,1)}, u32[]{:S(2)}) copy-start(bf16[64,128]{1,0:T(8,128)(2,1)} %get-tuple-element.15.own_ref) | copy-start | bytes 49156
  11.6 12.1 %collective-permute-start.1 = (bf16[24,128]{1,0:T(8,128)(2,1)S(1)}, bf16[24,128]{1,0:T(8,128)(2,1)S(1)}, u32[]{:S(2)}, u32[]{:S(2)}) collective-permute-start(bf16[24,128]{1,0:T(8,128)(2,1)S(1)} %get-tuple-element.27), channel_id=1, source_target_pairs={{4,8},{8,4},{12,16},{16,12},{20,24},{24,20},{28,32},{32,28},{36,40... | collective-permute-start | bytes 18440 | tf_op jit(solution)/shard_map/ppermute | solution.py:300
  15.7 8.7 %collective-permute-start = (bf16[24,128]{1,0:T(8,128)(2,1)S(1)}, bf16[24,128]{1,0:T(8,128)(2,1)S(1)}, u32[]{:S(2)}, u32[]{:S(2)}) collective-permute-start(bf16[24,128]{1,0:T(8,128)(2,1)S(1)} %get-tuple-element.28), channel_id=1, source_target_pairs={{0,4},{4,0},{8,12},{12,8},{16,20},{20,16},{24,28},{28,24},{32,36},... | collective-permute-start | bytes 18440 | tf_op jit(solution)/shard_map/ppermute | solution.py:300
  23.6 0.8 copy-start.8
  23.6 0.8 copy-start.3
  23.6 0.8 copy-start.4
  23.6 0.8 copy-start.5
  23.7 0.7 copy-start.7
  76.1 14.1 %copy-start.2 = (f32[64,128]{1,0:T(8,128)S(1)}, f32[64,128]{1,0:T(8,128)}, u32[]{:S(2)}) copy-start(f32[64,128]{1,0:T(8,128)} %get-tuple-element.21.gain_ref) | copy-start | bytes 98308

commit v9 on v7

--- a/solution.py
+++ b/solution.py
@@ -147,7 +147,7 @@
 
 def main_kernel(
     own_ref, p0, p1, got_ref, src_ref, dst_ref, harm_ref, basis_ref, wrad_ref, wmix_ref, cot_ref,
-    dext_ref, line_ref, send_ref,
+    lists_ref, dext_ref, line_ref, send_ref, lists_out,
     hot_s, harm_s, radial_s, source_s, mom_s, dmom_s,
 ):
     ring, core = position()
@@ -225,6 +225,7 @@
         send_ref[to] = jnp.concatenate([shard, block], axis=0).astype(bf16)
     line_ref[0] = ghosts[4].astype(bf16)
     line_ref[1] = ghosts[5].astype(bf16)
+    lists_out[...] = lists_ref[...]
 
 
 def place():
@@ -254,7 +255,7 @@
         pass_ref[odd, i] = up.astype(bf16)
 
 
-def line_kernel(parts_ref, p0, p1, out_ref):
+def line_kernel(parts_ref, out_ref):
     add_up(parts_ref, out_ref)
 
 
@@ -332,14 +333,15 @@
         edge_vec.reshape(3, 1, EDGES),
         cost=pl.CostEstimate(flops=1000000, bytes_accessed=400000, transcendentals=0),
     )
-    dext, line, blocks = call(
+    dext, line, blocks, lists = call(
         main_kernel,
         [
             shape((ATOMS, CHANS), f32),
             shape((2, GHOST, CHANS), bf16),
             shape((PEERS, SHARD + GHOST, CHANS), bf16),
+            shape((FACES, 1, GHOST), jnp.int32),
         ],
-        own, *near, far, edge_src, edge_dst, harm, basis, w_rad, w_mix, out_cot,
+        own, *near, far, edge_src, edge_dst, harm, basis, w_rad, w_mix, out_cot, sends,
         scratch=[
             pltpu.VMEM((ROWS, EDGES), bf16),
             pltpu.VMEM((9 * ATOMS, EDGES), bf16),
@@ -358,12 +360,12 @@
     pairs = [[(0, 1), (1, 0), (2, 3), (3, 2)], [(1, 2), (2, 1), (3, 0), (0, 3)]]
     passing = [lax.ppermute(passing[q], "zl", pairs[q]) for q in range(2)]
     parts = exchange(parts, LINE)
-    (parts,) = call(line_kernel, [shape((PEERS, SHARD, CHANS), bf16)], parts, *passing)
+    (parts,) = call(line_kernel, [shape((PEERS, SHARD, CHANS), bf16)], parts)
     sums = exchange(parts, SLAB)
     d_feat, gmix, grad_r = call(
         post_kernel,
         [shape((1, ATOMS, CHANS), f32), shape((3 * CHANS, CHANS), f32), shape((NB, CHANS), f32)],
-        dext, gain, sends, far, *passing, sums,
+        dext, gain, lists, far, *passing, sums,
     )
     return d_feat, gmix, grad_r
 

time: 83.3 us -> 83.3 us (level)
  blocking collectives: 25.6 us -> 38.2 us
  starting transfers between devices: 42.1 us -> 32.1 us
  waiting for transfers between devices: 5.34 us -> 2.91 us
    all_to_all x2, blocking collectives: 25.6 us -> 38.2 us  [exchange(): return lax.all_to_all(blocks, axes, 0, 0, tiled=True)]
    all_to_all x2, starting transfers between devices: 23.2 us -> 14.6 us  [exchange(): return lax.all_to_all(blocks, axes, 0, 0, tiled=True)]
    all_to_all x2, waiting for transfers between devices: 1.81 us -> 0.01 us  [exchange(): return lax.all_to_all(blocks, axes, 0, 0, tiled=True)]
    ppermute x2, starting transfers between devices: 6.99 us -> 5.55 us  [on_device(): passing = [lax.ppermute(passing[q], 'zl', pairs[q]) for q in range(2)]]
where the time goes in v9:
time: 83.3 us; the launch traced here: 82.1 us
  blocking collectives  38.2 us (46%)
  starting transfers between devices  32.1 us (39%)
  Pallas kernels  8.04 us (10%)
  waiting for transfers between devices  2.91 us (3%)
  between operations  0.86 us (1%)
    all_to_all x2, blocking collectives, exchange(): return lax.all_to_all(blocks, axes, 0, 0, tiled=True)  38.2 us
    all_to_all x2, starting transfers between devices, exchange(): return lax.all_to_all(blocks, axes, 0, 0, tiled=True)  14.6 us
    ppermute x2, starting transfers between devices, swap(): return lax.ppermute(block, DOM, pairs)  11.9 us
    pallas_call x6, Pallas kernels, call(): pl.pallas_call(kernel, out_shape=outs, in_specs=[pl.BlockSpec(memory_spac...  8.04 us
    ppermute x2, starting transfers between devices, on_device(): passing = [lax.ppermute(passing[q], 'zl', pairs[q]) for q in range(2)]  5.55 us
    ppermute x2, waiting for transfers between devices, on_device(): passing = [lax.ppermute(passing[q], 'zl', pairs[q]) for q in range(2)]  2.26 us
  transfers between devices with their start and end apart: 6, of which 3 were waited for; matrix products, arithmetic and copies ran while one was open for 0% of the time, Pallas kernels for 0%

profile of v9, /device:TPU:1, one launch (start us, length us, event | category | flops | bytes accessed | tf_op | source)
XLA Modules:
  0.0 82.1 jit_solution(3596986497398619141)
XLA Ops:
  0.6 1.7 %shard_map.121 = (bf16[64,128]{1,0:T(8,128)(2,1)}, f32[64,128]{1,0:T(8,128)}, bf16[2,24,128]{2,1,0:T(8,128)(2,1)}, bf16[16,24,128]{2,1,0:T(8,128)(2,1)}) custom-call(bf16[1,64,128]{2,1,0:T(8,128)(2,1)} %feat_hbm.1, s32[1,64]{1,0:T(1,128)} %species_hbm.1, f32[5,128]{1,0:T(8,128)} %gain_hbm.1, s32[6,1,24]{2,1,0:T(1,128)} %bitcast.11), custom_call_target="tpu_custom_call" | custom-call | tf_op jit(solution)/shard_map/pallas_call | solution.py:43
  2.4 0.0 copy-start.9
  2.4 0.0 copy-start.1
  2.4 0.0 copy-start
  2.4 9.2 %all-to-all-start = ((bf16[16,24,128]{2,1,0:T(8,128)(2,1)}), bf16[16,24,128]{2,1,0:T(8,128)(2,1)S(1)}, u32[]{:S(2)}, u32[]{:S(2)}) async-start(bf16[16,24,128]{2,1,0:T(8,128)(2,1)} %get-tuple-element.17), calls=%async_computation | async-start | bytes 196608 | tf_op jit(solution)/shard_map/all_to_all | solution.py:303
  11.6 0.0 copy-done.9
  11.6 0.0 copy-start.6
  11.6 4.0 %collective-permute-start.1 = (bf16[24,128]{1,0:T(8,128)(2,1)S(1)}, bf16[24,128]{1,0:T(8,128)(2,1)S(1)}, u32[]{:S(2)}, u32[]{:S(2)}) collective-permute-start(bf16[24,128]{1,0:T(8,128)(2,1)S(1)} %get-tuple-element.29), channel_id=1, source_target_pairs={{4,8},{8,4},{12,16},{16,12},{20,24},{24,20},{28,32},{32,28},{36,40... | collective-permute-start | bytes 18440 | tf_op jit(solution)/shard_map/ppermute | solution.py:299
  15.7 7.9 %collective-permute-start = (bf16[24,128]{1,0:T(8,128)(2,1)S(1)}, bf16[24,128]{1,0:T(8,128)(2,1)S(1)}, u32[]{:S(2)}, u32[]{:S(2)}) collective-permute-start(bf16[24,128]{1,0:T(8,128)(2,1)S(1)} %get-tuple-element.30), channel_id=1, source_target_pairs={{0,4},{4,0},{8,12},{12,8},{16,20},{20,16},{24,28},{28,24},{32,36},... | collective-permute-start | bytes 18440 | tf_op jit(solution)/shard_map/ppermute | solution.py:299
  23.6 0.0 copy-start.8
  23.6 0.0 copy-done.1
  23.6 0.0 copy-start.3
  23.6 0.0 copy-start.4
  23.6 0.0 copy-start.5
  23.6 0.1 shard_map.122
  23.7 0.0 copy-start.7
  23.7 0.0 collective-permute-done.1.p1
  23.7 0.6 collective-permute-done.p0
  24.4 0.0 all-to-all-done.got_ref
  24.4 0.0 copy-done
  24.4 4.6 %shard_map.123 = (f32[64,128]{1,0:T(8,128)S(1)}, bf16[2,24,128]{2,1,0:T(8,128)(2,1)S(1)}, bf16[32,40,128]{2,1,0:T(8,128)(2,1)S(1)}, s32[6,1,24]{2,1,0:T(1,128)S(1)}) custom-call(bf16[64,128]{1,0:T(8,128)(2,1)S(1)} %copy-done.6, bf16[24,128]{1,0:T(8,128)(2,1)S(1)} %collective-permute-done.p0, bf16[24,128]{1,0:T(8,128)(2,1)S(1)} %collective-permute-done.1.p1, ...), custom_call_target="tpu_custom_call" | custom-call | tf_op jit(solution)/shard_map/pallas_call | solution.py:43
  29.0 12.7 %all_to_all.20.parts_ref.got_ref = bf16[32,40,128]{2,1,0:T(8,128)(2,1)S(1)} all-to-all(bf16[32,40,128]{2,1,0:T(8,128)(2,1)S(1)} %get-tuple-element.23), channel_id=1, replica_groups=mesh['zl'=4,'x'=4,'y'=4,'core'=2,'rep'=4] {'x','y','core'}, dimensions={0} | all-to-all | bytes 655360 | tf_op jit(solution)/shard_map/all_to_all | solution.py:303
  41.8 25.4 %all_to_all.21.parts_ref = bf16[16,16,128]{2,1,0:T(8,128)(2,1)S(1)} all-to-all(bf16[16,16,128]{2,1,0:T(8,128)(2,1)S(1)} %get-tuple-element.26), channel_id=1, replica_groups=mesh['zl'=4,'x'=4,'y'=4,'core'=2,'rep'=4] {'zl','rep'}, dimensions={0} | all-to-all | bytes 131072 | tf_op jit(solution)/shard_map/all_to_all | solution.py:303
  67.2 0.7 shard_map.125
  67.9 5.4 %all-to-all-start.3 = ((bf16[32,16,128]{2,1,0:T(8,128)(2,1)}), bf16[32,16,128]{2,1,0:T(8,128)(2,1)S(1)}, u32[]{:S(2)}, u32[]{:S(2)}) async-start(bf16[32,16,128]{2,1,0:T(8,128)(2,1)} %shard_map.125), calls=%async_computation.3 | async-start | bytes 262144 | tf_op jit(solution)/shard_map/all_to_all | solution.py:303
  73.4 0.0 copy-start.2
  73.4 3.3 %collective-permute-start.3 = (bf16[3,24,128]{2,1,0:T(8,128)(2,1)S(1)}, bf16[3,24,128]{2,1,0:T(8,128)(2,1)S(1)}, u32[]{:S(2)}, u32[]{:S(2)}) collective-permute-start(bf16[3,24,128]{2,1,0:T(8,128)(2,1)S(1)} %get-tuple-element.27), channel_id=1, source_target_pairs={{128,256},{256,128},{384,0},{0,384},{129,257},{257,129},{385,1},{1... | collective-permute-start | bytes 55304 | tf_op jit(solution)/shard_map/ppermute | solution.py:361
  76.7 2.2 %collective-permute-start.2 = (bf16[3,24,128]{2,1,0:T(8,128)(2,1)S(1)}, bf16[3,24,128]{2,1,0:T(8,128)(2,1)S(1)}, u32[]{:S(2)}, u32[]{:S(2)}) collective-permute-start(bf16[3,24,128]{2,1,0:T(8,128)(2,1)S(1)} %get-tuple-element.28), channel_id=1, source_target_pairs={{0,128},{128,0},{256,384},{384,256},{1,129},{129,1},{257,385},{385... | collective-permute-start | bytes 55304 | tf_op jit(solution)/shard_map/ppermute | solution.py:361
  79.0 1.0 %collective-permute-done.3.p1 = bf16[3,24,128]{2,1,0:T(8,128)(2,1)S(1)} collective-permute-done((bf16[3,24,128]{2,1,0:T(8,128)(2,1)S(1)}, bf16[3,24,128]{2,1,0:T(8,128)(2,1)S(1)}, u32[]{:S(2)}, u32[]{:S(2)}) %collective-permute-start.3) | collective-permute-done | bytes 18464 | tf_op jit(solution)/shard_map/ppermute | solution.py:361
  80.0 1.2 %collective-permute-done.2.p0 = bf16[3,24,128]{2,1,0:T(8,128)(2,1)S(1)} collective-permute-done((bf16[3,24,128]{2,1,0:T(8,128)(2,1)S(1)}, bf16[3,24,128]{2,1,0:T(8,128)(2,1)S(1)}, u32[]{:S(2)}, u32[]{:S(2)}) %collective-permute-start.2) | collective-permute-done | bytes 18464 | tf_op jit(solution)/shard_map/ppermute | solution.py:361
  81.2 0.0 all-to-all-done.3.sums_ref
  81.2 0.9 %shard_map.126 = (f32[1,64,128]{2,1,0:T(8,128)}, f32[384,128]{1,0:T(8,128)}, f32[8,128]{1,0:T(8,128)}) custom-call(f32[64,128]{1,0:T(8,128)S(1)} %get-tuple-element.20.dext_ref, f32[64,128]{1,0:T(8,128)S(1)} %copy-done.2, s32[6,1,24]{2,1,0:T(1,128)S(1)} %get-tuple-element.22.sends_ref, bf16[32,40,128]{2,1,0:T(8,128)(2,1)S(1)} %all_to_all.20.parts_ref.got_ref, ...), custom_call_target="tpu_custom_call" | custom-call | tf_op jit(solution)/shard_map/pallas_call | solution.py:43
  (10 shorter events, 0.1 us)
Async XLA Ops:
  2.4 9.2 %copy-start.9 = (bf16[2,24,128]{2,1,0:T(8,128)(2,1)S(1)}, bf16[2,24,128]{2,1,0:T(8,128)(2,1)}, u32[]{:S(2)}) copy-start(bf16[2,24,128]{2,1,0:T(8,128)(2,1)} %get-tuple-element.16) | copy-start | bytes 36868
  2.4 21.2 %copy-start.1 = (f32[1,3,4096]{2,0,1:T(1,128)S(1)}, f32[1,3,4096]{2,0,1:T(1,128)}, u32[]{:S(2)}) copy-start(f32[1,3,4096]{2,0,1:T(1,128)} %param.16) | copy-start | bytes 147460
  2.4 22.0 %copy-start = (bf16[384,128]{1,0:T(8,128)(2,1)S(1)}, bf16[384,128]{1,0:T(8,128)(2,1)}, u32[]{:S(2)}) copy-start(bf16[384,128]{1,0:T(8,128)(2,1)} %wmix_ref.1) | copy-start | bytes 294916
  2.4 22.0 %all-to-all-start = ((bf16[16,24,128]{2,1,0:T(8,128)(2,1)}), bf16[16,24,128]{2,1,0:T(8,128)(2,1)S(1)}, u32[]{:S(2)}, u32[]{:S(2)}) async-start(bf16[16,24,128]{2,1,0:T(8,128)(2,1)} %get-tuple-element.17), calls=%async_computation | async-start | bytes 196608 | tf_op jit(solution)/shard_map/all_to_all | solution.py:303
  11.6 12.8 %copy-start.6 = (bf16[64,128]{1,0:T(8,128)(2,1)S(1)}, bf16[64,128]{1,0:T(8,128)(2,1)}, u32[]{:S(2)}) copy-start(bf16[64,128]{1,0:T(8,128)(2,1)} %get-tuple-element.15.own_ref) | copy-start | bytes 49156
  11.6 12.1 %collective-permute-start.1 = (bf16[24,128]{1,0:T(8,128)(2,1)S(1)}, bf16[24,128]{1,0:T(8,128)(2,1)S(1)}, u32[]{:S(2)}, u32[]{:S(2)}) collective-permute-start(bf16[24,128]{1,0:T(8,128)(2,1)S(1)} %get-tuple-element.29), channel_id=1, source_target_pairs={{4,8},{8,4},{12,16},{16,12},{20,24},{24,20},{28,32},{32,28},{36,40... | collective-permute-start | bytes 18440 | tf_op jit(solution)/shard_map/ppermute | solution.py:299
  15.7 8.7 %collective-permute-start = (bf16[24,128]{1,0:T(8,128)(2,1)S(1)}, bf16[24,128]{1,0:T(8,128)(2,1)S(1)}, u32[]{:S(2)}, u32[]{:S(2)}) collective-permute-start(bf16[24,128]{1,0:T(8,128)(2,1)S(1)} %get-tuple-element.30), channel_id=1, source_target_pairs={{0,4},{4,0},{8,12},{12,8},{16,20},{20,16},{24,28},{28,24},{32,36},... | collective-permute-start | bytes 18440 | tf_op jit(solution)/shard_map/ppermute | solution.py:299
  23.6 0.8 copy-start.8
  23.6 0.8 copy-start.3
  23.6 0.8 copy-start.4
  23.6 0.8 copy-start.5
  23.7 0.7 copy-start.7
  67.9 13.3 %all-to-all-start.3 = ((bf16[32,16,128]{2,1,0:T(8,128)(2,1)}), bf16[32,16,128]{2,1,0:T(8,128)(2,1)S(1)}, u32[]{:S(2)}, u32[]{:S(2)}) async-start(bf16[32,16,128]{2,1,0:T(8,128)(2,1)} %shard_map.125), calls=%async_computation.3 | async-start | bytes 262144 | tf_op jit(solution)/shard_map/all_to_all | solution.py:303
  73.4 7.9 %copy-start.2 = (f32[64,128]{1,0:T(8,128)S(1)}, f32[64,128]{1,0:T(8,128)}, u32[]{:S(2)}) copy-start(f32[64,128]{1,0:T(8,128)} %get-tuple-element.21.gain_ref) | copy-start | bytes 98308
  73.4 6.6 %collective-permute-start.3 = (bf16[3,24,128]{2,1,0:T(8,128)(2,1)S(1)}, bf16[3,24,128]{2,1,0:T(8,128)(2,1)S(1)}, u32[]{:S(2)}, u32[]{:S(2)}) collective-permute-start(bf16[3,24,128]{2,1,0:T(8,128)(2,1)S(1)} %get-tuple-element.27), channel_id=1, source_target_pairs={{128,256},{256,128},{384,0},{0,384},{129,257},{257,129},{385,1},{1... | collective-permute-start | bytes 55304 | tf_op jit(solution)/shard_map/ppermute | solution.py:361
  76.7 4.5 %collective-permute-start.2 = (bf16[3,24,128]{2,1,0:T(8,128)(2,1)S(1)}, bf16[3,24,128]{2,1,0:T(8,128)(2,1)S(1)}, u32[]{:S(2)}, u32[]{:S(2)}) collective-permute-start(bf16[3,24,128]{2,1,0:T(8,128)(2,1)S(1)} %get-tuple-element.28), channel_id=1, source_target_pairs={{0,128},{128,0},{256,384},{384,256},{1,129},{129,1},{257,385},{385... | collective-permute-start | bytes 55304 | tf_op jit(solution)/shard_map/ppermute | solution.py:361

commit v10 on v9

--- a/solution.py
+++ b/solution.py
@@ -147,7 +147,7 @@
 
 def main_kernel(
     own_ref, p0, p1, got_ref, src_ref, dst_ref, harm_ref, basis_ref, wrad_ref, wmix_ref, cot_ref,
-    lists_ref, dext_ref, line_ref, send_ref, lists_out,
+    lists_ref, dext_ref, local_ref, pass_ref, send_ref, lists_out,
     hot_s, harm_s, radial_s, source_s, mom_s, dmom_s,
 ):
     ring, core = position()
@@ -193,7 +193,7 @@
     nothing = jnp.zeros((GHOST, CHANS), f32)
     for i in range(3 * CHANS // SHARD):
         shard = gmix[i * SHARD : (i + 1) * SHARD]
-        send_ref[i] = jnp.concatenate([shard, nothing], axis=0).astype(bf16)
+        send_ref[i] = shard.astype(bf16)
     dinv = dot(dpre, wmix_ref[...], ((1,), (1,)))
     groups = [0, 1, 1, 1, 2, 2, 2, 2, 2]
     for k in range(9):
@@ -212,19 +212,19 @@
         right = jnp.concatenate([dsource, dradial.astype(bf16)], axis=0)
         both = both + dot(left, right, ((1,), (1,)))
     dext, gradr = both[:ROWS, :CHANS], both[ROWS:, CHANS:]
-    gradr = jnp.concatenate([gradr[:NB] + gradr[NB:], nothing, nothing[:NB]], axis=0)
+    gradr = jnp.concatenate([gradr[:NB] + gradr[NB:], nothing[: SHARD - NB]], axis=0)
     send_ref[3 * CHANS // SHARD] = gradr.astype(bf16)
     for i in range(3 * CHANS // SHARD + 1, PEERS):
-        send_ref[i] = jnp.zeros((SHARD + GHOST, CHANS), bf16)
+        send_ref[i] = jnp.zeros((SHARD, CHANS), bf16)
     dext_ref[...] = dext[:ATOMS]
     ghosts = [dext[ATOMS + face * GHOST : ATOMS + (face + 1) * GHOST] for face in range(FACES)]
-    spot = place()
-    for move, block in zip(MOVES, ghosts[:4]):
-        to = lax.rem(spot + move + PEERS, PEERS)
-        shard = send_ref[to].astype(f32)[:SHARD]
-        send_ref[to] = jnp.concatenate([shard, block], axis=0).astype(bf16)
-    line_ref[0] = ghosts[4].astype(bf16)
-    line_ref[1] = ghosts[5].astype(bf16)
+    ghosts = [block.astype(bf16) for block in ghosts]
+    odd = lax.rem(lax.axis_index("zl"), 2)
+    for i in range(4):
+        local_ref[i] = ghosts[i]
+    for i, pair in enumerate((4, 0, 2)):
+        pass_ref[1 - odd, i] = ghosts[pair]
+        pass_ref[odd, i] = ghosts[pair + 1]
     lists_out[...] = lists_ref[...]
 
 
@@ -232,45 +232,47 @@
     return (lax.axis_index("x") * 4 + lax.axis_index("y")) * 2 + lax.axis_index("core")
 
 
-def passed(got_ref):
+def total_of(parts_ref):
+    total = parts_ref[0].astype(f32)
+    for i in range(1, parts_ref.shape[0]):
+        total = total + parts_ref[i].astype(f32)
+    return total
+
+
+def crossed(p0, p1):
+    odd = lax.rem(lax.axis_index("zl"), 2)
+    a, b = p0[...].astype(f32), p1[...].astype(f32)
+    return jnp.where(odd == 0, a, b), jnp.where(odd == 0, b, a)
+
+
+def slab_kernel(parts_ref, p0, p1, out_ref):
+    total = total_of(parts_ref).astype(bf16)
+    for i in range(LINES):
+        out_ref[i] = total
+
+
+def line_kernel(parts_ref, local_ref, p0, p1, out_ref):
+    total = total_of(parts_ref)
+    plain = jnp.concatenate([total, jnp.zeros((GHOST, CHANS), f32)], axis=0).astype(bf16)
+    for i in range(PEERS):
+        out_ref[i] = plain
+    down, up = crossed(p0, p1)
     spot = place()
-    return [got_ref[lax.rem(spot - move + PEERS, PEERS)].astype(f32)[SHARD:] for move in MOVES]
-
-
-def add_up(parts_ref, out_ref):
-    total = parts_ref[0].astype(f32)[:SHARD]
-    for i in range(1, parts_ref.shape[0]):
-        total = total + parts_ref[i].astype(f32)[:SHARD]
-    total = total.astype(bf16)
-    for i in range(out_ref.shape[0]):
-        out_ref[i] = total
-
-
-def slab_kernel(parts_ref, line_ref, out_ref, pass_ref):
-    add_up(parts_ref, out_ref)
-    blocks = passed(parts_ref)
-    odd = lax.rem(lax.axis_index("zl"), 2)
-    for i, (down, up) in enumerate([(line_ref[0], line_ref[1]), blocks[:2], blocks[2:]]):
-        pass_ref[1 - odd, i] = down.astype(bf16)
-        pass_ref[odd, i] = up.astype(bf16)
-
-
-def line_kernel(parts_ref, out_ref):
-    add_up(parts_ref, out_ref)
+    for i, (move, other) in enumerate(zip(MOVES, (down[1], up[1], down[2], up[2]))):
+        leaves = spot < -move if move < 0 else spot + move >= PEERS
+        block = jnp.where(leaves, other, local_ref[i].astype(f32))
+        block = jnp.concatenate([total, block], axis=0).astype(bf16)
+        out_ref[lax.rem(spot + move + PEERS, PEERS)] = block
 
 
 def post_kernel(
-    dext_ref, gain_ref, sends_ref, got_ref, p0, p1, sums_ref, dfeat_ref, gmix_ref, grad_ref
+    dext_ref, gain_ref, sends_ref, p0, p1, sums_ref, dfeat_ref, gmix_ref, grad_ref
 ):
     spot = place()
-    local = passed(got_ref)
-    blocks = []
-    a, b = p0[...].astype(f32), p1[...].astype(f32)
-    odd = lax.rem(lax.axis_index("zl"), 2)
-    down, up = jnp.where(odd == 0, a, b), jnp.where(odd == 0, b, a)
-    for move, block, other in zip(MOVES, local, (down[1], up[1], down[2], up[2])):
-        crossed = spot - move >= PEERS if move < 0 else spot < move
-        blocks.append(jnp.where(crossed, other, block))
+    down, up = crossed(p0, p1)
+    blocks = [
+        sums_ref[lax.rem(spot - move + PEERS, PEERS)].astype(f32)[SHARD:] for move in MOVES
+    ]
     blocks += [down[0], up[0]]
     total = dext_ref[...]
     for face in range(FACES):
@@ -278,7 +280,7 @@
         total = total + dot(hot.astype(bf16), blocks[face].astype(bf16), ((1,), (0,)))
     dfeat_ref[0] = total * gain_ref[...]
     whole = 3 * CHANS // SHARD
-    parts = [sums_ref[i].astype(f32) for i in range(whole)]
+    parts = [sums_ref[i].astype(f32)[:SHARD] for i in range(whole)]
     grad = sums_ref[whole].astype(f32)[:NB]
     square = grad * grad
     for part in parts:
@@ -333,12 +335,13 @@
         edge_vec.reshape(3, 1, EDGES),
         cost=pl.CostEstimate(flops=1000000, bytes_accessed=400000, transcendentals=0),
     )
-    dext, line, blocks, lists = call(
+    dext, local, passing, parts, lists = call(
         main_kernel,
         [
             shape((ATOMS, CHANS), f32),
-            shape((2, GHOST, CHANS), bf16),
-            shape((PEERS, SHARD + GHOST, CHANS), bf16),
+            shape((4, GHOST, CHANS), bf16),
+            shape((2, 3, GHOST, CHANS), bf16),
+            shape((PEERS, SHARD, CHANS), bf16),
             shape((FACES, 1, GHOST), jnp.int32),
         ],
         own, *near, far, edge_src, edge_dst, harm, basis, w_rad, w_mix, out_cot, sends,
@@ -351,21 +354,19 @@
             pltpu.VMEM((CHANS, 9 * ATOMS), bf16),
         ],
     )
-    far = exchange(blocks, SLAB)
-    parts, passing = call(
-        slab_kernel,
-        [shape((LINES, SHARD, CHANS), bf16), shape((2, 3, GHOST, CHANS), bf16)],
-        far, line,
-    )
     pairs = [[(0, 1), (1, 0), (2, 3), (3, 2)], [(1, 2), (2, 1), (3, 0), (0, 3)]]
     passing = [lax.ppermute(passing[q], "zl", pairs[q]) for q in range(2)]
+    parts = exchange(parts, SLAB)
+    (parts,) = call(slab_kernel, [shape((LINES, SHARD, CHANS), bf16)], parts, *passing)
     parts = exchange(parts, LINE)
-    (parts,) = call(line_kernel, [shape((PEERS, SHARD, CHANS), bf16)], parts)
+    (parts,) = call(
+        line_kernel, [shape((PEERS, SHARD + GHOST, CHANS), bf16)], parts, local, *passing
+    )
     sums = exchange(parts, SLAB)
     d_feat, gmix, grad_r = call(
         post_kernel,
         [shape((1, ATOMS, CHANS), f32), shape((3 * CHANS, CHANS), f32), shape((NB, CHANS), f32)],
-        dext, gain, lists, far, *passing, sums,
+        dext, gain, lists, *passing, sums,
     )
     return d_feat, gmix, grad_r
 

time: 83.3 us -> 89.1 us (1.070)
  blocking collectives: 38.2 us -> 43.3 us
  starting transfers between devices: 32.1 us -> 33 us
    all_to_all x2, blocking collectives: 38.2 us -> 43.3 us  [exchange(): return lax.all_to_all(blocks, axes, 0, 0, tiled=True)]
    ppermute x2, starting transfers between devices: 5.55 us -> 8.04 us  [on_device(): passing = [lax.ppermute(passing[q], 'zl', pairs[q]) for q in range(2)]]
    all_to_all x2, starting transfers between devices: 14.6 us -> 13 us  [exchange(): return lax.all_to_all(blocks, axes, 0, 0, tiled=True)]
  transfers between devices with their start and end apart: 6 -> 6, of which waited for: 3 -> 2; matrix products, arithmetic and copies ran while one was open for 0% -> 0% of each run, Pallas kernels for 0% -> 0%
where the time goes in v10:
time: 89.1 us; the launch traced here: 88.5 us
  blocking collectives  43.3 us (49%)
  starting transfers between devices  33 us (37%)
  Pallas kernels  8.05 us (9%)
  waiting for transfers between devices  3.22 us (4%)
    all_to_all x2, blocking collectives, exchange(): return lax.all_to_all(blocks, axes, 0, 0, tiled=True)  43.3 us
    all_to_all x2, starting transfers between devices, exchange(): return lax.all_to_all(blocks, axes, 0, 0, tiled=True)  13 us
    ppermute x2, starting transfers between devices, swap(): return lax.ppermute(block, DOM, pairs)  11.9 us
    pallas_call x6, Pallas kernels, call(): pl.pallas_call(kernel, out_shape=outs, in_specs=[pl.BlockSpec(memory_spac...  8.05 us
    ppermute x2, starting transfers between devices, on_device(): passing = [lax.ppermute(passing[q], 'zl', pairs[q]) for q in range(2)]  8.04 us
    ppermute x2, waiting for transfers between devices, on_device(): passing = [lax.ppermute(passing[q], 'zl', pairs[q]) for q in range(2)]  2.57 us
  transfers between devices with their start and end apart: 6, of which 2 were waited for; matrix products, arithmetic and copies ran while one was open for 0% of the time, Pallas kernels for 0%

profile of v10, /device:TPU:1, one launch (start us, length us, event | category | flops | bytes accessed | tf_op | source)
XLA Modules:
  0.0 88.5 jit_solution(1214731964300497431)
XLA Ops:
  0.6 1.7 %shard_map.121 = (bf16[64,128]{1,0:T(8,128)(2,1)}, f32[64,128]{1,0:T(8,128)}, bf16[2,24,128]{2,1,0:T(8,128)(2,1)}, bf16[16,24,128]{2,1,0:T(8,128)(2,1)}) custom-call(bf16[1,64,128]{2,1,0:T(8,128)(2,1)} %feat_hbm.1, s32[1,64]{1,0:T(1,128)} %species_hbm.1, f32[5,128]{1,0:T(8,128)} %gain_hbm.1, s32[6,1,24]{2,1,0:T(1,128)} %bitcast.11), custom_call_target="tpu_custom_call" | custom-call | tf_op jit(solution)/shard_map/pallas_call | solution.py:43
  2.4 0.0 copy-start.9
  2.4 0.0 copy-start.1
  2.4 0.0 copy-start
  2.4 9.2 %all-to-all-start = ((bf16[16,24,128]{2,1,0:T(8,128)(2,1)}), bf16[16,24,128]{2,1,0:T(8,128)(2,1)S(1)}, u32[]{:S(2)}, u32[]{:S(2)}) async-start(bf16[16,24,128]{2,1,0:T(8,128)(2,1)} %get-tuple-element.16), calls=%async_computation | async-start | bytes 196608 | tf_op jit(solution)/shard_map/all_to_all | solution.py:305
  11.6 0.0 copy-done.9
  11.6 0.0 copy-start.6
  11.6 4.0 %collective-permute-start.1 = (bf16[24,128]{1,0:T(8,128)(2,1)S(1)}, bf16[24,128]{1,0:T(8,128)(2,1)S(1)}, u32[]{:S(2)}, u32[]{:S(2)}) collective-permute-start(bf16[24,128]{1,0:T(8,128)(2,1)S(1)} %get-tuple-element.27), channel_id=1, source_target_pairs={{4,8},{8,4},{12,16},{16,12},{20,24},{24,20},{28,32},{32,28},{36,40... | collective-permute-start | bytes 18440 | tf_op jit(solution)/shard_map/ppermute | solution.py:301
  15.7 7.9 %collective-permute-start = (bf16[24,128]{1,0:T(8,128)(2,1)S(1)}, bf16[24,128]{1,0:T(8,128)(2,1)S(1)}, u32[]{:S(2)}, u32[]{:S(2)}) collective-permute-start(bf16[24,128]{1,0:T(8,128)(2,1)S(1)} %get-tuple-element.28), channel_id=1, source_target_pairs={{0,4},{4,0},{8,12},{12,8},{16,20},{20,16},{24,28},{28,24},{32,36},... | collective-permute-start | bytes 18440 | tf_op jit(solution)/shard_map/ppermute | solution.py:301
  23.6 0.0 copy-start.8
  23.6 0.0 copy-done.1
  23.6 0.0 copy-start.3
  23.6 0.0 copy-start.4
  23.6 0.0 copy-start.5
  23.6 0.1 shard_map.122
  23.7 0.0 copy-start.7
  23.7 0.0 collective-permute-done.1.p1
  23.7 0.6 collective-permute-done.p0
  24.4 0.0 all-to-all-done.got_ref
  24.4 0.0 copy-done
  24.4 0.0 copy-done.6
  24.4 5.2 %shard_map.123 = (f32[64,128]{1,0:T(8,128)S(1)}, bf16[4,24,128]{2,1,0:T(8,128)(2,1)S(1)}, bf16[2,3,24,128]{3,2,1,0:T(8,128)(2,1)S(1)}, bf16[32,16,128]{2,1,0:T(8,128)(2,1)}, s32[6,1,24]{2,1,0:T(1,128)S(1)}) custom-call(bf16[64,128]{1,0:T(8,128)(2,1)S(1)} %copy-done.6, bf16[24,128]{1,0:T(8,128)(2,1)S(1)} %collective-permute-done.p0, ...), custom_call_target="tpu_custom_call" | custom-call | tf_op jit(solution)/shard_map/pallas_call | solution.py:43
  29.7 3.9 %all-to-all-start.1 = ((bf16[32,16,128]{2,1,0:T(8,128)(2,1)}), bf16[32,16,128]{2,1,0:T(8,128)(2,1)S(1)}, u32[]{:S(2)}, u32[]{:S(2)}) async-start(bf16[32,16,128]{2,1,0:T(8,128)(2,1)} %get-tuple-element.23), calls=%async_computation.1 | async-start | bytes 262144 | tf_op jit(solution)/shard_map/all_to_all | solution.py:305
  33.5 6.1 %collective-permute-start.3 = (bf16[3,24,128]{2,1,0:T(8,128)(2,1)S(1)}, bf16[3,24,128]{2,1,0:T(8,128)(2,1)S(1)}, u32[]{:S(2)}, u32[]{:S(2)}) collective-permute-start(bf16[3,24,128]{2,1,0:T(8,128)(2,1)S(1)} %get-tuple-element.25), channel_id=1, source_target_pairs={{128,256},{256,128},{384,0},{0,384},{129,257},{257,129},{385,1},{1... | collective-permute-start | bytes 55304 | tf_op jit(solution)/shard_map/ppermute | solution.py:358
  39.7 1.9 %collective-permute-start.2 = (bf16[3,24,128]{2,1,0:T(8,128)(2,1)S(1)}, bf16[3,24,128]{2,1,0:T(8,128)(2,1)S(1)}, u32[]{:S(2)}, u32[]{:S(2)}) collective-permute-start(bf16[3,24,128]{2,1,0:T(8,128)(2,1)S(1)} %get-tuple-element.26), channel_id=1, source_target_pairs={{0,128},{128,0},{256,384},{384,256},{1,129},{129,1},{257,385},{385... | collective-permute-start | bytes 55304 | tf_op jit(solution)/shard_map/ppermute | solution.py:358
  41.6 0.0 collective-permute-done.3.p1
  41.6 2.6 %collective-permute-done.2.p0 = bf16[3,24,128]{2,1,0:T(8,128)(2,1)S(1)} collective-permute-done((bf16[3,24,128]{2,1,0:T(8,128)(2,1)S(1)}, bf16[3,24,128]{2,1,0:T(8,128)(2,1)S(1)}, u32[]{:S(2)}, u32[]{:S(2)}) %collective-permute-start.2) | collective-permute-done | bytes 18464 | tf_op jit(solution)/shard_map/ppermute | solution.py:358
  44.2 0.0 all-to-all-done.1.parts_ref
  44.2 23.7 %all_to_all.20.parts_ref = bf16[16,16,128]{2,1,0:T(8,128)(2,1)S(1)} all-to-all(bf16[16,16,128]{2,1,0:T(8,128)(2,1)S(1)} %shard_map.124), channel_id=1, replica_groups=mesh['zl'=4,'x'=4,'y'=4,'core'=2,'rep'=4] {'zl','rep'}, dimensions={0} | all-to-all | bytes 131072 | tf_op jit(solution)/shard_map/all_to_all | solution.py:305
  67.9 0.0 copy-start.2
  68.0 19.7 %all_to_all.21.sums_ref = bf16[32,40,128]{2,1,0:T(8,128)(2,1)S(1)} all-to-all(bf16[32,40,128]{2,1,0:T(8,128)(2,1)S(1)} %shard_map.125), channel_id=1, replica_groups=mesh['zl'=4,'x'=4,'y'=4,'core'=2,'rep'=4] {'x','y','core'}, dimensions={0} | all-to-all | bytes 655360 | tf_op jit(solution)/shard_map/all_to_all | solution.py:305
  87.6 0.9 %shard_map.126 = (f32[1,64,128]{2,1,0:T(8,128)}, f32[384,128]{1,0:T(8,128)}, f32[8,128]{1,0:T(8,128)}) custom-call(f32[64,128]{1,0:T(8,128)S(1)} %get-tuple-element.19.dext_ref, f32[64,128]{1,0:T(8,128)S(1)} %copy-done.2, s32[6,1,24]{2,1,0:T(1,128)S(1)} %get-tuple-element.21.sends_ref, bf16[3,24,128]{2,1,0:T(8,128)(2,1)S(1)} %collective-permute-done.2.p0, ...), custom_call_target="tpu_custom_call" | custom-call | tf_op jit(solution)/shard_map/pallas_call | solution.py:43
  (10 shorter events, 0.1 us)
Async XLA Ops:
  2.4 9.2 %copy-start.9 = (bf16[2,24,128]{2,1,0:T(8,128)(2,1)S(1)}, bf16[2,24,128]{2,1,0:T(8,128)(2,1)}, u32[]{:S(2)}) copy-start(bf16[2,24,128]{2,1,0:T(8,128)(2,1)} %get-tuple-element.15) | copy-start | bytes 36868
  2.4 21.2 %copy-start.1 = (f32[1,3,4096]{2,0,1:T(1,128)S(1)}, f32[1,3,4096]{2,0,1:T(1,128)}, u32[]{:S(2)}) copy-start(f32[1,3,4096]{2,0,1:T(1,128)} %param.16) | copy-start | bytes 147460
  2.4 22.0 %copy-start = (bf16[384,128]{1,0:T(8,128)(2,1)S(1)}, bf16[384,128]{1,0:T(8,128)(2,1)}, u32[]{:S(2)}) copy-start(bf16[384,128]{1,0:T(8,128)(2,1)} %wmix_ref.1) | copy-start | bytes 294916
  2.4 22.0 %all-to-all-start = ((bf16[16,24,128]{2,1,0:T(8,128)(2,1)}), bf16[16,24,128]{2,1,0:T(8,128)(2,1)S(1)}, u32[]{:S(2)}, u32[]{:S(2)}) async-start(bf16[16,24,128]{2,1,0:T(8,128)(2,1)} %get-tuple-element.16), calls=%async_computation | async-start | bytes 196608 | tf_op jit(solution)/shard_map/all_to_all | solution.py:305
  11.6 12.8 %copy-start.6 = (bf16[64,128]{1,0:T(8,128)(2,1)S(1)}, bf16[64,128]{1,0:T(8,128)(2,1)}, u32[]{:S(2)}) copy-start(bf16[64,128]{1,0:T(8,128)(2,1)} %get-tuple-element.14.own_ref) | copy-start | bytes 49156
  11.6 12.1 %collective-permute-start.1 = (bf16[24,128]{1,0:T(8,128)(2,1)S(1)}, bf16[24,128]{1,0:T(8,128)(2,1)S(1)}, u32[]{:S(2)}, u32[]{:S(2)}) collective-permute-start(bf16[24,128]{1,0:T(8,128)(2,1)S(1)} %get-tuple-element.27), channel_id=1, source_target_pairs={{4,8},{8,4},{12,16},{16,12},{20,24},{24,20},{28,32},{32,28},{36,40... | collective-permute-start | bytes 18440 | tf_op jit(solution)/shard_map/ppermute | solution.py:301
  15.7 8.7 %collective-permute-start = (bf16[24,128]{1,0:T(8,128)(2,1)S(1)}, bf16[24,128]{1,0:T(8,128)(2,1)S(1)}, u32[]{:S(2)}, u32[]{:S(2)}) collective-permute-start(bf16[24,128]{1,0:T(8,128)(2,1)S(1)} %get-tuple-element.28), channel_id=1, source_target_pairs={{0,4},{4,0},{8,12},{12,8},{16,20},{20,16},{24,28},{28,24},{32,36},... | collective-permute-start | bytes 18440 | tf_op jit(solution)/shard_map/ppermute | solution.py:301
  23.6 0.8 copy-start.8
  23.6 0.8 copy-start.3
  23.6 0.8 copy-start.4
  23.6 0.8 copy-start.5
  23.7 0.7 copy-start.7
  29.7 14.5 %all-to-all-start.1 = ((bf16[32,16,128]{2,1,0:T(8,128)(2,1)}), bf16[32,16,128]{2,1,0:T(8,128)(2,1)S(1)}, u32[]{:S(2)}, u32[]{:S(2)}) async-start(bf16[32,16,128]{2,1,0:T(8,128)(2,1)} %get-tuple-element.23), calls=%async_computation.1 | async-start | bytes 262144 | tf_op jit(solution)/shard_map/all_to_all | solution.py:305
  33.5 8.1 %collective-permute-start.3 = (bf16[3,24,128]{2,1,0:T(8,128)(2,1)S(1)}, bf16[3,24,128]{2,1,0:T(8,128)(2,1)S(1)}, u32[]{:S(2)}, u32[]{:S(2)}) collective-permute-start(bf16[3,24,128]{2,1,0:T(8,128)(2,1)S(1)} %get-tuple-element.25), channel_id=1, source_target_pairs={{128,256},{256,128},{384,0},{0,384},{129,257},{257,129},{385,1},{1... | collective-permute-start | bytes 55304 | tf_op jit(solution)/shard_map/ppermute | solution.py:358
  39.7 4.5 %collective-permute-start.2 = (bf16[3,24,128]{2,1,0:T(8,128)(2,1)S(1)}, bf16[3,24,128]{2,1,0:T(8,128)(2,1)S(1)}, u32[]{:S(2)}, u32[]{:S(2)}) collective-permute-start(bf16[3,24,128]{2,1,0:T(8,128)(2,1)S(1)} %get-tuple-element.26), channel_id=1, source_target_pairs={{0,128},{128,0},{256,384},{384,256},{1,129},{129,1},{257,385},{385... | collective-permute-start | bytes 55304 | tf_op jit(solution)/shard_map/ppermute | solution.py:358
  67.9 19.7 %copy-start.2 = (f32[64,128]{1,0:T(8,128)S(1)}, f32[64,128]{1,0:T(8,128)}, u32[]{:S(2)}) copy-start(f32[64,128]{1,0:T(8,128)} %get-tuple-element.20.gain_ref) | copy-start | bytes 98308

commit v11 on v9

--- a/solution.py
+++ b/solution.py
@@ -61,7 +61,7 @@
 
 
 def pre_kernel(
-    feat_hbm, species_hbm, gain_hbm, sends_hbm, own_ref, gain_out, pair_ref, pick_ref,
+    feat_hbm, species_hbm, gain_hbm, sends_hbm, own_ref, gain_out, first_ref, second_ref, pick_ref,
     feat_ref, species_ref, gain_ref, sends_ref, sems,
 ):
     copies = [
@@ -89,13 +89,16 @@
     own_ref[...] = own
     gain_out[...] = gain
     ring, core = position()
+    near = []
     for face in range(FACES):
         hot = (rows_iota((ATOMS, GHOST)) == sends_ref[face]).astype(f32)
-        picked = dot(hot.astype(bf16), own, ((0,), (0,))).astype(bf16)
+        picked = dot(hot.astype(bf16), own, ((0,), (0,)))
         if face < 2:
-            pair_ref[lax.rem(core + face, 2)] = picked
+            near.append(picked)
         else:
-            pick_ref[peer(ring, STRIDES[face - 2])] = picked
+            pick_ref[peer(ring, STRIDES[face - 2])] = picked.astype(bf16)
+    first_ref[...] = jnp.where(core == 0, near[0], near[1]).astype(bf16)
+    second_ref[...] = jnp.where(core == 0, near[1], near[0]).astype(bf16)
 
 
 def geo_kernel(vec_ref, harm_ref, basis_ref):
@@ -255,7 +258,7 @@
         pass_ref[odd, i] = up.astype(bf16)
 
 
-def line_kernel(parts_ref, out_ref):
+def line_kernel(parts_ref, p0, p1, out_ref):
     add_up(parts_ref, out_ref)
 
 
@@ -306,12 +309,13 @@
 def on_device(feat, species, species_gain, send_lists, edge_src, edge_dst, edge_vec, w_rad, w_mix, out_cot):
     shape = jax.ShapeDtypeStruct
     sends = send_lists.reshape(FACES, 1, GHOST)
-    own, gain, pair, picks = call(
+    own, gain, first, second, picks = call(
         pre_kernel,
         [
             shape((ATOMS, CHANS), bf16),
             shape((ATOMS, CHANS), f32),
-            shape((2, GHOST, CHANS), bf16),
+            shape((GHOST, CHANS), bf16),
+            shape((GHOST, CHANS), bf16),
             shape((RING, GHOST, CHANS), bf16),
         ],
         feat, species, species_gain, sends,
@@ -325,7 +329,7 @@
         space=pl.ANY,
         limit=60,
     )
-    near = [swap(pair[q], q) for q in range(2)]
+    near = [swap(first, 0), swap(second, 1)]
     far = exchange(picks, PLANE)
     harm, basis = call(
         geo_kernel,
@@ -360,7 +364,7 @@
     pairs = [[(0, 1), (1, 0), (2, 3), (3, 2)], [(1, 2), (2, 1), (3, 0), (0, 3)]]
     passing = [lax.ppermute(passing[q], "zl", pairs[q]) for q in range(2)]
     parts = exchange(parts, LINE)
-    (parts,) = call(line_kernel, [shape((PEERS, SHARD, CHANS), bf16)], parts)
+    (parts,) = call(line_kernel, [shape((PEERS, SHARD, CHANS), bf16)], parts, *passing)
     sums = exchange(parts, SLAB)
     d_feat, gmix, grad_r = call(
         post_kernel,

time: 83.3 us -> 85.7 us (1.029)
  blocking collectives: 38.2 us -> 33 us
  waiting for transfers between devices: 2.91 us -> 7.07 us
  starting transfers between devices: 32.1 us -> 36.1 us
    all_to_all x2, starting transfers between devices: 14.6 us -> 23.2 us  [exchange(): return lax.all_to_all(blocks, axes, 0, 0, tiled=True)]
    ppermute x2, starting transfers between devices: 11.9 us -> 5.97 us  [swap(): return lax.ppermute(block, DOM, pairs)]
    all_to_all x2, blocking collectives: 38.2 us -> 33 us  [exchange(): return lax.all_to_all(blocks, axes, 0, 0, tiled=True)]
    all_to_all x2, waiting for transfers between devices: 0.01 us -> 1.81 us  [exchange(): return lax.all_to_all(blocks, axes, 0, 0, tiled=True)]
    ppermute x2, waiting for transfers between devices: 0.64 us -> 2.39 us  [swap(): return lax.ppermute(block, DOM, pairs)]
    ppermute x2, starting transfers between devices: 5.55 us -> 6.99 us  [on_device(): passing = [lax.ppermute(passing[q], 'zl', pairs[q]) for q in range(2)]]
where the time goes in v11:
time: 85.7 us; the launch traced here: 85.2 us
  starting transfers between devices  36.1 us (42%)
  blocking collectives  33 us (39%)
  Pallas kernels  8.02 us (9%)
  waiting for transfers between devices  7.07 us (8%)
  between operations  0.88 us (1%)
    all_to_all x2, blocking collectives, exchange(): return lax.all_to_all(blocks, axes, 0, 0, tiled=True)  33 us
    all_to_all x2, starting transfers between devices, exchange(): return lax.all_to_all(blocks, axes, 0, 0, tiled=True)  23.2 us
    pallas_call x6, Pallas kernels, call(): pl.pallas_call(kernel, out_shape=outs, in_specs=[pl.BlockSpec(memory_spac...  8.02 us
    ppermute x2, starting transfers between devices, on_device(): passing = [lax.ppermute(passing[q], 'zl', pairs[q]) for q in range(2)]  6.99 us
    ppermute x2, starting transfers between devices, swap(): return lax.ppermute(block, DOM, pairs)  5.97 us
    ppermute x2, waiting for transfers between devices, on_device(): passing = [lax.ppermute(passing[q], 'zl', pairs[q]) for q in range(2)]  2.87 us
    ppermute x2, waiting for transfers between devices, swap(): return lax.ppermute(block, DOM, pairs)  2.39 us
    all_to_all x2, waiting for transfers between devices, exchange(): return lax.all_to_all(blocks, axes, 0, 0, tiled=True)  1.81 us
  transfers between devices with their start and end apart: 6, of which 3 were waited for; matrix products, arithmetic and copies ran while one was open for 0% of the time, Pallas kernels for 0%

profile of v11, /device:TPU:1, one launch (start us, length us, event | category | flops | bytes accessed | tf_op | source)
XLA Modules:
  0.0 85.2 jit_solution(12549368487213651139)
XLA Ops:
  0.6 1.7 %shard_map.121 = (bf16[64,128]{1,0:T(8,128)(2,1)}, f32[64,128]{1,0:T(8,128)}, bf16[24,128]{1,0:T(8,128)(2,1)}, bf16[24,128]{1,0:T(8,128)(2,1)}, bf16[16,24,128]{2,1,0:T(8,128)(2,1)}) custom-call(bf16[1,64,128]{2,1,0:T(8,128)(2,1)} %feat_hbm.1, s32[1,64]{1,0:T(1,128)} %species_hbm.1, f32[5,128]{1,0:T(8,128)} %gain_hbm.1, s32[6,1,24]{2,1,0:T(1,128)} %bitcast.7), custom_call_target="tpu_custom_call" | custom-call | tf_op jit(solution)/shard_map/pallas_call | solution.py:43
  2.4 0.0 copy-start.10
  2.4 0.0 copy-start.9
  2.4 0.0 copy-start.1
  2.4 0.0 copy-start
  2.4 9.2 %all-to-all-start = ((bf16[16,24,128]{2,1,0:T(8,128)(2,1)}), bf16[16,24,128]{2,1,0:T(8,128)(2,1)S(1)}, u32[]{:S(2)}, u32[]{:S(2)}) async-start(bf16[16,24,128]{2,1,0:T(8,128)(2,1)} %get-tuple-element.19), calls=%async_computation | async-start | bytes 196608 | tf_op jit(solution)/shard_map/all_to_all | solution.py:306
  11.6 0.0 copy-done.10
  11.6 3.3 %collective-permute-start = (bf16[24,128]{1,0:T(8,128)(2,1)S(1)}, bf16[24,128]{1,0:T(8,128)(2,1)S(1)}, u32[]{:S(2)}, u32[]{:S(2)}) collective-permute-start(bf16[24,128]{1,0:T(8,128)(2,1)S(1)} %copy-done.10), channel_id=1, source_target_pairs={{0,4},{4,0},{8,12},{12,8},{16,20},{20,16},{24,28},{28,24},{32,36},... | collective-permute-start | bytes 18440 | tf_op jit(solution)/shard_map/ppermute | solution.py:302
  14.9 2.7 %collective-permute-start.1 = (bf16[24,128]{1,0:T(8,128)(2,1)S(1)}, bf16[24,128]{1,0:T(8,128)(2,1)S(1)}, u32[]{:S(2)}, u32[]{:S(2)}) collective-permute-start(bf16[24,128]{1,0:T(8,128)(2,1)S(1)} %copy-done.9), channel_id=1, source_target_pairs={{4,8},{8,4},{12,16},{16,12},{20,24},{24,20},{28,32},{32,28},{36,40... | collective-permute-start | bytes 18440 | tf_op jit(solution)/shard_map/ppermute | solution.py:302
  17.6 0.0 copy-start.8
  17.6 0.0 copy-done.1
  17.6 0.0 copy-start.3
  17.6 0.0 copy-start.4
  17.6 0.0 copy-start.5
  17.7 0.1 shard_map.122
  17.7 0.0 copy-start.7
  17.8 0.0 collective-permute-done.p0
  17.8 2.4 %collective-permute-done.1.p1 = bf16[24,128]{1,0:T(8,128)(2,1)S(1)} collective-permute-done((bf16[24,128]{1,0:T(8,128)(2,1)S(1)}, bf16[24,128]{1,0:T(8,128)(2,1)S(1)}, u32[]{:S(2)}, u32[]{:S(2)}) %collective-permute-start.1) | collective-permute-done | bytes 6176 | tf_op jit(solution)/shard_map/ppermute | solution.py:302
  20.1 0.0 all-to-all-done.got_ref
  20.2 4.6 %shard_map.123 = (f32[64,128]{1,0:T(8,128)S(1)}, bf16[2,24,128]{2,1,0:T(8,128)(2,1)S(1)}, bf16[32,40,128]{2,1,0:T(8,128)(2,1)S(1)}, s32[6,1,24]{2,1,0:T(1,128)S(1)}) custom-call(bf16[64,128]{1,0:T(8,128)(2,1)S(1)} %copy-done.6, bf16[24,128]{1,0:T(8,128)(2,1)S(1)} %collective-permute-done.p0, bf16[24,128]{1,0:T(8,128)(2,1)S(1)} %collective-permute-done.1.p1, ...), custom_call_target="tpu_custom_call" | custom-call | tf_op jit(solution)/shard_map/pallas_call | solution.py:43
  24.8 20.1 %all_to_all.20.parts_ref.got_ref = bf16[32,40,128]{2,1,0:T(8,128)(2,1)S(1)} all-to-all(bf16[32,40,128]{2,1,0:T(8,128)(2,1)S(1)} %get-tuple-element.25), channel_id=1, replica_groups=mesh['zl'=4,'x'=4,'y'=4,'core'=2,'rep'=4] {'x','y','core'}, dimensions={0} | all-to-all | bytes 655360 | tf_op jit(solution)/shard_map/all_to_all | solution.py:306
  44.9 0.7 shard_map.124
  45.6 14.0 %all-to-all-start.2 = ((bf16[16,16,128]{2,1,0:T(8,128)(2,1)}), bf16[16,16,128]{2,1,0:T(8,128)(2,1)S(1)}, u32[]{:S(2)}, u32[]{:S(2)}) async-start(bf16[16,16,128]{2,1,0:T(8,128)(2,1)} %get-tuple-element.28), calls=%async_computation.2 | async-start | bytes 131072 | tf_op jit(solution)/shard_map/all_to_all | solution.py:306
  59.6 5.1 %collective-permute-start.3 = (bf16[3,24,128]{2,1,0:T(8,128)(2,1)S(1)}, bf16[3,24,128]{2,1,0:T(8,128)(2,1)S(1)}, u32[]{:S(2)}, u32[]{:S(2)}) collective-permute-start(bf16[3,24,128]{2,1,0:T(8,128)(2,1)S(1)} %get-tuple-element.29), channel_id=1, source_target_pairs={{128,256},{256,128},{384,0},{0,384},{129,257},{257,129},{385,1},{1... | collective-permute-start | bytes 55304 | tf_op jit(solution)/shard_map/ppermute | solution.py:365
  64.7 1.9 %collective-permute-start.2 = (bf16[3,24,128]{2,1,0:T(8,128)(2,1)S(1)}, bf16[3,24,128]{2,1,0:T(8,128)(2,1)S(1)}, u32[]{:S(2)}, u32[]{:S(2)}) collective-permute-start(bf16[3,24,128]{2,1,0:T(8,128)(2,1)S(1)} %get-tuple-element.30), channel_id=1, source_target_pairs={{0,128},{128,0},{256,384},{384,256},{1,129},{129,1},{257,385},{385... | collective-permute-start | bytes 55304 | tf_op jit(solution)/shard_map/ppermute | solution.py:365
  66.6 0.0 collective-permute-done.3.p1
  66.6 2.9 %collective-permute-done.2.p0 = bf16[3,24,128]{2,1,0:T(8,128)(2,1)S(1)} collective-permute-done((bf16[3,24,128]{2,1,0:T(8,128)(2,1)S(1)}, bf16[3,24,128]{2,1,0:T(8,128)(2,1)S(1)}, u32[]{:S(2)}, u32[]{:S(2)}) %collective-permute-start.2) | collective-permute-done | bytes 18464 | tf_op jit(solution)/shard_map/ppermute | solution.py:365
  69.5 1.8 %all-to-all-done.2.parts_ref = bf16[16,16,128]{2,1,0:T(8,128)(2,1)S(1)} async-done(((bf16[16,16,128]{2,1,0:T(8,128)(2,1)}), bf16[16,16,128]{2,1,0:T(8,128)(2,1)S(1)}, u32[]{:S(2)}, u32[]{:S(2)}) %all-to-all-start.2) | async-done | bytes 65568 | tf_op jit(solution)/shard_map/all_to_all | solution.py:306
  71.3 0.0 copy-start.2
  71.3 12.9 %all_to_all.21.sums_ref = bf16[32,16,128]{2,1,0:T(8,128)(2,1)S(1)} all-to-all(bf16[32,16,128]{2,1,0:T(8,128)(2,1)S(1)} %shard_map.125), channel_id=1, replica_groups=mesh['zl'=4,'x'=4,'y'=4,'core'=2,'rep'=4] {'x','y','core'}, dimensions={0} | all-to-all | bytes 262144 | tf_op jit(solution)/shard_map/all_to_all | solution.py:306
  84.2 0.0 copy-done.2
  84.2 0.9 %shard_map.126 = (f32[1,64,128]{2,1,0:T(8,128)}, f32[384,128]{1,0:T(8,128)}, f32[8,128]{1,0:T(8,128)}) custom-call(f32[64,128]{1,0:T(8,128)S(1)} %get-tuple-element.22.dext_ref, f32[64,128]{1,0:T(8,128)S(1)} %copy-done.2, s32[6,1,24]{2,1,0:T(1,128)S(1)} %get-tuple-element.24.sends_ref, bf16[32,40,128]{2,1,0:T(8,128)(2,1)S(1)} %all_to_all.20.parts_ref.got_ref, ...), custom_call_target="tpu_custom_call" | custom-call | tf_op jit(solution)/shard_map/pallas_call | solution.py:43
  (11 shorter events, 0.1 us)
Async XLA Ops:
  2.4 9.2 %copy-start.10 = (bf16[24,128]{1,0:T(8,128)(2,1)S(1)}, bf16[24,128]{1,0:T(8,128)(2,1)}, u32[]{:S(2)}) copy-start(bf16[24,128]{1,0:T(8,128)(2,1)} %get-tuple-element.17) | copy-start | bytes 18436
  2.4 12.5 %copy-start.9 = (bf16[24,128]{1,0:T(8,128)(2,1)S(1)}, bf16[24,128]{1,0:T(8,128)(2,1)}, u32[]{:S(2)}) copy-start(bf16[24,128]{1,0:T(8,128)(2,1)} %get-tuple-element.18) | copy-start | bytes 18436
  2.4 15.2 %copy-start.1 = (f32[1,3,4096]{2,0,1:T(1,128)S(1)}, f32[1,3,4096]{2,0,1:T(1,128)}, u32[]{:S(2)}) copy-start(f32[1,3,4096]{2,0,1:T(1,128)} %param.16) | copy-start | bytes 147460
  2.4 17.7 %copy-start = (bf16[384,128]{1,0:T(8,128)(2,1)S(1)}, bf16[384,128]{1,0:T(8,128)(2,1)}, u32[]{:S(2)}) copy-start(bf16[384,128]{1,0:T(8,128)(2,1)} %wmix_ref.1) | copy-start | bytes 294916
  2.4 17.7 %copy-start.6 = (bf16[64,128]{1,0:T(8,128)(2,1)S(1)}, bf16[64,128]{1,0:T(8,128)(2,1)}, u32[]{:S(2)}) copy-start(bf16[64,128]{1,0:T(8,128)(2,1)} %get-tuple-element.16.own_ref) | copy-start | bytes 49156
  2.4 17.7 %all-to-all-start = ((bf16[16,24,128]{2,1,0:T(8,128)(2,1)}), bf16[16,24,128]{2,1,0:T(8,128)(2,1)S(1)}, u32[]{:S(2)}, u32[]{:S(2)}) async-start(bf16[16,24,128]{2,1,0:T(8,128)(2,1)} %get-tuple-element.19), calls=%async_computation | async-start | bytes 196608 | tf_op jit(solution)/shard_map/all_to_all | solution.py:306
  11.6 6.1 %collective-permute-start = (bf16[24,128]{1,0:T(8,128)(2,1)S(1)}, bf16[24,128]{1,0:T(8,128)(2,1)S(1)}, u32[]{:S(2)}, u32[]{:S(2)}) collective-permute-start(bf16[24,128]{1,0:T(8,128)(2,1)S(1)} %copy-done.10), channel_id=1, source_target_pairs={{0,4},{4,0},{8,12},{12,8},{16,20},{20,16},{24,28},{28,24},{32,36},... | collective-permute-start | bytes 18440 | tf_op jit(solution)/shard_map/ppermute | solution.py:302
  14.9 5.2 %collective-permute-start.1 = (bf16[24,128]{1,0:T(8,128)(2,1)S(1)}, bf16[24,128]{1,0:T(8,128)(2,1)S(1)}, u32[]{:S(2)}, u32[]{:S(2)}) collective-permute-start(bf16[24,128]{1,0:T(8,128)(2,1)S(1)} %copy-done.9), channel_id=1, source_target_pairs={{4,8},{8,4},{12,16},{16,12},{20,24},{24,20},{28,32},{32,28},{36,40... | collective-permute-start | bytes 18440 | tf_op jit(solution)/shard_map/ppermute | solution.py:302
  17.6 2.6 %copy-start.8 = (f32[8,128]{1,0:T(8,128)S(1)}, f32[8,128]{1,0:T(8,128)}, u32[]{:S(2)}) copy-start(f32[8,128]{1,0:T(8,128)} %wrad_ref.1) | copy-start | bytes 12292
  17.6 2.5 %copy-start.3 = (s32[1,4096]{1,0:T(1,128)S(1)}, s32[1,4096]{1,0:T(1,128)}, u32[]{:S(2)}) copy-start(s32[1,4096]{1,0:T(1,128)} %src_ref.1) | copy-start | bytes 49156
  17.6 2.5 %copy-start.4 = (s32[1,4096]{1,0:T(1,128)S(1)}, s32[1,4096]{1,0:T(1,128)}, u32[]{:S(2)}) copy-start(s32[1,4096]{1,0:T(1,128)} %dst_ref.1) | copy-start | bytes 49156
  17.6 2.5 %copy-start.5 = (bf16[1,64,128]{2,1,0:T(8,128)(2,1)S(1)}, bf16[1,64,128]{2,1,0:T(8,128)(2,1)}, u32[]{:S(2)}) copy-start(bf16[1,64,128]{2,1,0:T(8,128)(2,1)} %cot_ref.1) | copy-start | bytes 49156
  17.7 2.5 %copy-start.7 = (s32[1,6,24]{2,0,1:T(1,128)S(1)}, s32[1,6,24]{2,0,1:T(1,128)}, u32[]{:S(2)}) copy-start(s32[1,6,24]{2,0,1:T(1,128)} %param.13) | copy-start | bytes 1732
  45.6 25.7 %all-to-all-start.2 = ((bf16[16,16,128]{2,1,0:T(8,128)(2,1)}), bf16[16,16,128]{2,1,0:T(8,128)(2,1)S(1)}, u32[]{:S(2)}, u32[]{:S(2)}) async-start(bf16[16,16,128]{2,1,0:T(8,128)(2,1)} %get-tuple-element.28), calls=%async_computation.2 | async-start | bytes 131072 | tf_op jit(solution)/shard_map/all_to_all | solution.py:306
  59.6 7.0 %collective-permute-start.3 = (bf16[3,24,128]{2,1,0:T(8,128)(2,1)S(1)}, bf16[3,24,128]{2,1,0:T(8,128)(2,1)S(1)}, u32[]{:S(2)}, u32[]{:S(2)}) collective-permute-start(bf16[3,24,128]{2,1,0:T(8,128)(2,1)S(1)} %get-tuple-element.29), channel_id=1, source_target_pairs={{128,256},{256,128},{384,0},{0,384},{129,257},{257,129},{385,1},{1... | collective-permute-start | bytes 55304 | tf_op jit(solution)/shard_map/ppermute | solution.py:365
  64.7 4.8 %collective-permute-start.2 = (bf16[3,24,128]{2,1,0:T(8,128)(2,1)S(1)}, bf16[3,24,128]{2,1,0:T(8,128)(2,1)S(1)}, u32[]{:S(2)}, u32[]{:S(2)}) collective-permute-start(bf16[3,24,128]{2,1,0:T(8,128)(2,1)S(1)} %get-tuple-element.30), channel_id=1, source_target_pairs={{0,128},{128,0},{256,384},{384,256},{1,129},{129,1},{257,385},{385... | collective-permute-start | bytes 55304 | tf_op jit(solution)/shard_map/ppermute | solution.py:365
  71.3 12.9 %copy-start.2 = (f32[64,128]{1,0:T(8,128)S(1)}, f32[64,128]{1,0:T(8,128)}, u32[]{:S(2)}) copy-start(f32[64,128]{1,0:T(8,128)} %get-tuple-element.23.gain_ref) | copy-start | bytes 98308
